TPU v7x, 32 devices: a whole 2x2x4 slice. The times are simulated.
32 devices in a mesh: row: 8 (over z, y), col: 4 (over x, core).
Axes of the slice: x: 2, y: 2, z: 4, core: 2. Of those that a mesh axis runs over, the one named last changes fastest.
Arguments:
- layer_input: bfloat16 [16384, 2048], P(('col', 'row')), may hold values from -6 to 6
- segments: int32 [16384], P('col'), may hold values from 0 to 3, as said below
- w_query: bfloat16 [2048, 2048], P('col', 'row')
- w_key: bfloat16 [2048, 2048], P('col', 'row')
- w_value: bfloat16 [2048, 2048], P('col', 'row'), may hold values from -0.125 to 0.125
- w_out: bfloat16 [2048, 2048], P('row', 'col'), may hold values from -0.125 to 0.125
- query_gain: bfloat16 [2048], P(('row', 'col'))
- key_gain: bfloat16 [2048], P(('row', 'col'))
- attn_gain: bfloat16 [2048], P('col'), may hold values from 0.25 to 1.75
- w_gate: bfloat16 [2048, 8192], P('col', 'row'), may hold values from -0.125 to 0.125
- w_up: bfloat16 [2048, 8192], P('col', 'row'), may hold values from -0.125 to 0.125
- w_down: bfloat16 [8192, 2048], P('row', 'col'), may hold values from -0.0625 to 0.0625
- mlp_gain: bfloat16 [2048], P('col'), may hold values from 0.25 to 1.75
- cotangent: bfloat16 [16384, 2048], P(('col', 'row')), may hold values from -6 to 6
Outputs:
- layer_output: bfloat16 [16384, 2048], P(('col', 'row'))
- input_grad: bfloat16 [16384, 2048], P(('col', 'row'))
- w_query_grad: float32 [2048, 2048], P('col', 'row')
- w_key_grad: float32 [2048, 2048], P('col', 'row')
- w_value_grad: float32 [2048, 2048], P('col', 'row')
- w_out_grad: float32 [2048, 2048], P('row', 'col')
- query_gain_grad: float32 [2048], P(('row', 'col'))
- key_gain_grad: float32 [2048], P(('row', 'col'))
- attn_gain_grad: float32 [2048], P('col')
- w_gate_grad: float32 [2048, 8192], P('col', 'row')
- w_up_grad: float32 [2048, 8192], P('col', 'row')
- w_down_grad: float32 [8192, 2048], P('row', 'col')
- mlp_gain_grad: float32 [2048], P('col')
Inputs may be any that keep to these rules, and one draw needn't show every extreme that they name: `segments`: each packed sequence of 4096 consecutive tokens holds exactly four documents; segment numbers start at 0 and rise by one at each document boundary, and every document holds at least 204 tokens.
All inputs are finite; a program needn't handle non-finite values.
Results may differ from a plain program's by a relative error of at most 0.025.
Values may be sent and summed in bfloat16 or wider, within the bound.
A program may use at most 448 MiB of HBM per device.

v0:
```python
import jax
import jax.numpy as jnp
from jax import lax
from jax.sharding import PartitionSpec as P

HEADS = 16


EPS = 1e-06
THETA = 500000.0
MASKED = -1e30


def doc_positions(segments):
    token_index = jnp.arange(segments.shape[0], dtype=jnp.int32)
    change = jnp.concatenate([jnp.ones((1,), dtype=bool), segments[1:] != segments[:-1]])
    first_index = lax.cummax(jnp.where(change, token_index, 0), axis=0)
    return token_index - first_index


def rotate(values, places, sign):
    half = values.shape[-1] // 2
    freqs = THETA ** (-(jnp.arange(half, dtype=jnp.float32) * 2.0) / values.shape[-1])
    angle = places.astype(jnp.float32)[:, None] * freqs[None, :]
    cosine = jnp.cos(angle)[:, None, :]
    sine = sign * jnp.sin(angle)[:, None, :]
    first_half = values[..., :half]
    second_half = values[..., half:]
    return jnp.concatenate(
        [first_half * cosine - second_half * sine, second_half * cosine + first_half * sine],
        axis=-1,
    )


def contract_rows(left, right):
    return lax.dot_general(
        left, right, (((0,), (0,)), ((), ())), preferred_element_type=jnp.float32
    )


def contract_cols(left, right):
    return lax.dot_general(
        left, right, (((1,), (1,)), ((), ())), preferred_element_type=jnp.float32
    )


def body(
    layer_input,
    segments,
    w_query,
    w_key,
    w_value,
    w_out,
    query_gain,
    key_gain,
    attn_gain,
    w_gate,
    w_up,
    w_down,
    mlp_gain,
    cotangent,
):
    gathered = (
        lax.all_gather(w_query, "col", axis=0, tiled=True),
        lax.all_gather(w_key, "col", axis=0, tiled=True),
        lax.all_gather(w_value, "col", axis=0, tiled=True),
        lax.all_gather(w_out, "col", axis=1, tiled=True),
        lax.all_gather(query_gain, "col", axis=0, tiled=True),
        lax.all_gather(key_gain, "col", axis=0, tiled=True),
        lax.all_gather(attn_gain, "col", axis=0, tiled=True),
        lax.all_gather(w_gate, "col", axis=0, tiled=True),
        lax.all_gather(w_up, "col", axis=0, tiled=True),
        lax.all_gather(w_down, "col", axis=1, tiled=True),
        lax.all_gather(mlp_gain, "col", axis=0, tiled=True),
    )
    (
        query_cols,
        key_cols,
        value_cols,
        out_rows,
        query_scale,
        key_scale,
        attn_scale,
        gate_cols,
        up_cols,
        down_rows,
        mlp_scale,
    ) = gathered
    query_scale = query_scale.astype(jnp.float32)
    key_scale = key_scale.astype(jnp.float32)
    attn_scale = attn_scale.astype(jnp.float32)
    mlp_scale = mlp_scale.astype(jnp.float32)
    model_width = layer_input.shape[1]
    head_size = model_width // HEADS
    local_width = query_cols.shape[1]
    local_heads = local_width // head_size
    seq_len = segments.shape[0]
    score_scale = head_size ** (-0.5)
    proj_weight = jnp.concatenate([query_cols, key_cols, value_cols], axis=1)
    gathered_x, out_full = (
        lax.all_gather(layer_input, "row", axis=0, tiled=True),
        lax.all_gather(out_rows, "row", axis=0, tiled=True),
    )
    projected = jnp.dot(gathered_x, proj_weight, preferred_element_type=jnp.float32)
    query_proj = projected[:, :local_width]
    key_proj = projected[:, local_width : 2 * local_width]
    value_proj = projected[:, 2 * local_width :]
    query_sq, key_sq = lax.psum(
        (jnp.sum(query_proj * query_proj, axis=-1), jnp.sum(key_proj * key_proj, axis=-1)), "row"
    )
    query_inv = lax.rsqrt(query_sq / model_width + EPS)[:, None]
    key_inv = lax.rsqrt(key_sq / model_width + EPS)[:, None]
    query_hat = query_proj * query_inv
    key_hat = key_proj * key_inv
    places = doc_positions(segments)
    query_vectors = rotate(
        (query_hat * query_scale).reshape(seq_len, local_heads, head_size), places, 1.0
    ).astype(jnp.bfloat16)
    key_vectors = rotate(
        (key_hat * key_scale).reshape(seq_len, local_heads, head_size), places, 1.0
    ).astype(jnp.bfloat16)
    value_vectors = value_proj.astype(jnp.bfloat16).reshape(seq_len, local_heads, head_size)
    block_rows = min(512, seq_len)
    block_count = seq_len // block_rows
    token_index = jnp.arange(seq_len, dtype=jnp.int32)

    def block_scores(row_start):
        row_end = row_start + block_rows
        raw = (
            jnp.einsum(
                "qhd,khd->hqk",
                query_vectors[row_start:row_end],
                key_vectors[:row_end],
                preferred_element_type=jnp.float32,
            )
            * score_scale
        )
        same_doc = segments[row_start:row_end][:, None] == segments[:row_end][None, :]
        causal = token_index[row_start:row_end][:, None] >= token_index[:row_end][None, :]
        return jnp.where((same_doc & causal)[None], raw, MASKED)

    block_outputs = []
    block_sums = []
    for block_index in range(block_count):
        row_start = block_index * block_rows
        row_end = row_start + block_rows
        scores = block_scores(row_start)
        row_max = jnp.max(scores, axis=-1, keepdims=True)
        exp_scores = jnp.exp(scores - row_max)
        row_total = jnp.sum(exp_scores, axis=-1, keepdims=True)
        attn_probs = (exp_scores / row_total).astype(jnp.bfloat16)
        block_outputs.append(
            jnp.einsum(
                "hqk,khd->qhd",
                attn_probs,
                value_vectors[:row_end],
                preferred_element_type=jnp.float32,
            )
        )
        block_sums.append(row_max[..., 0] + jnp.log(row_total[..., 0]))
    attn_out = (
        jnp.concatenate(block_outputs, axis=0).reshape(seq_len, local_width).astype(jnp.bfloat16)
    )
    log_sums = jnp.concatenate(block_sums, axis=1)
    attn_tokens = lax.all_to_all(attn_out, "row", split_axis=0, concat_axis=1, tiled=True)
    out_proj = jnp.dot(attn_tokens, out_full, preferred_element_type=jnp.float32)
    attn_inv = lax.rsqrt(jnp.mean(out_proj * out_proj, axis=-1, keepdims=True) + EPS)
    attn_hat = out_proj * attn_inv
    hidden = layer_input.astype(jnp.float32) + attn_hat * attn_scale
    hidden_low = hidden.astype(jnp.bfloat16)
    gathered_h = lax.all_gather(hidden_low, "row", axis=0, tiled=True)
    ff_weight = jnp.concatenate([gate_cols, up_cols], axis=1)
    ff_width = gate_cols.shape[1]
    gate_up = jnp.dot(gathered_h, ff_weight, preferred_element_type=jnp.float32)
    gate_val = gate_up[:, :ff_width]
    up_val = gate_up[:, ff_width:]
    activated = (jax.nn.silu(gate_val) * up_val).astype(jnp.bfloat16)
    mlp_out = lax.psum_scatter(
        jnp.dot(activated, down_rows, preferred_element_type=jnp.float32).astype(jnp.bfloat16),
        "row",
        scatter_dimension=0,
        tiled=True,
    ).astype(jnp.float32)
    mlp_inv = lax.rsqrt(jnp.mean(mlp_out * mlp_out, axis=-1, keepdims=True) + EPS)
    mlp_hat = mlp_out * mlp_inv
    layer_output = (hidden + mlp_hat * mlp_scale).astype(jnp.bfloat16)
    upstream = cotangent.astype(jnp.float32)
    mlp_gain_part = jnp.sum(upstream * mlp_hat, axis=0)
    scaled = upstream * mlp_scale
    mlp_grad = (
        mlp_inv * (scaled - mlp_hat * jnp.mean(scaled * mlp_hat, axis=-1, keepdims=True))
    ).astype(jnp.bfloat16)
    shard_rows = lax.all_gather(mlp_grad, "row", axis=0, tiled=True)
    weight_acc = contract_rows(activated, shard_rows)
    act_part = contract_cols(shard_rows, down_rows)
    gate_sigmoid = jax.nn.sigmoid(gate_val)
    gate_grad = act_part * up_val * gate_sigmoid * (1.0 + gate_val * (1.0 - gate_sigmoid))
    up_grad = act_part * gate_val * gate_sigmoid
    ff_grad = jnp.concatenate([gate_grad, up_grad], axis=1).astype(jnp.bfloat16)
    hidden_grad_mlp = lax.psum_scatter(
        contract_cols(ff_grad, ff_weight).astype(jnp.bfloat16),
        "row",
        scatter_dimension=0,
        tiled=True,
    ).astype(jnp.float32)
    ff_weight_grad = contract_rows(gathered_h, ff_grad)
    gate_weight_grad = ff_weight_grad[:, :ff_width]
    up_weight_grad = ff_weight_grad[:, ff_width:]
    hidden_grad = upstream + hidden_grad_mlp
    attn_gain_part = jnp.sum(hidden_grad * attn_hat, axis=0)
    scaled_attn = hidden_grad * attn_scale
    proj_grad = (
        attn_inv
        * (scaled_attn - attn_hat * jnp.mean(scaled_attn * attn_hat, axis=-1, keepdims=True))
    ).astype(jnp.bfloat16)
    out_full_grad = contract_rows(attn_tokens, proj_grad)
    out_token_grad = contract_cols(proj_grad, out_full).astype(jnp.bfloat16)
    attn_grad_low = lax.all_to_all(
        out_token_grad, "row", split_axis=1, concat_axis=0, tiled=True
    ).reshape(seq_len, local_heads, head_size)
    out_weight_grad = lax.psum_scatter(
        out_full_grad.astype(jnp.bfloat16), "row", scatter_dimension=0, tiled=True
    )
    key_acc = jnp.zeros((seq_len, local_heads, head_size), jnp.float32)
    value_acc = jnp.zeros((seq_len, local_heads, head_size), jnp.float32)
    query_parts = []
    for block_index in range(block_count):
        row_start = block_index * block_rows
        row_end = row_start + block_rows
        scores = block_scores(row_start)
        soft = jnp.exp(scores - log_sums[:, row_start:row_end][..., None])
        grad_rows = attn_grad_low[row_start:row_end]
        prob_grad = jnp.einsum(
            "qhd,khd->hqk", grad_rows, value_vectors[:row_end], preferred_element_type=jnp.float32
        )
        value_acc = value_acc.at[:row_end].add(
            jnp.einsum(
                "hqk,qhd->khd",
                soft.astype(jnp.bfloat16),
                grad_rows,
                preferred_element_type=jnp.float32,
            )
        )
        score_grad = (
            soft * (prob_grad - jnp.sum(soft * prob_grad, axis=-1, keepdims=True))
        ).astype(jnp.bfloat16)
        query_parts.append(
            jnp.einsum(
                "hqk,khd->qhd",
                score_grad,
                key_vectors[:row_end],
                preferred_element_type=jnp.float32,
            )
            * score_scale
        )
        key_acc = key_acc.at[:row_end].add(
            jnp.einsum(
                "hqk,qhd->khd",
                score_grad,
                query_vectors[row_start:row_end],
                preferred_element_type=jnp.float32,
            )
            * score_scale
        )
    query_grad = rotate(jnp.concatenate(query_parts, axis=0), places, -1.0).reshape(
        seq_len, local_width
    )
    key_grad = rotate(key_acc, places, -1.0).reshape(seq_len, local_width)
    query_gain_part = jnp.sum(query_grad * query_hat, axis=0)
    key_gain_part = jnp.sum(key_grad * key_hat, axis=0)
    query_scaled = query_grad * query_scale
    key_scaled = key_grad * key_scale
    query_dot, key_dot, attn_gain_sum, mlp_gain_sum = (
        lax.psum(jnp.sum(query_scaled * query_hat, axis=-1).astype(jnp.bfloat16), "row").astype(
            jnp.float32
        ),
        lax.psum(jnp.sum(key_scaled * key_hat, axis=-1).astype(jnp.bfloat16), "row").astype(
            jnp.float32
        ),
        lax.psum(attn_gain_part.astype(jnp.bfloat16), "row").astype(jnp.float32),
        lax.psum(mlp_gain_part.astype(jnp.bfloat16), "row").astype(jnp.float32),
    )
    query_proj_grad = query_inv * (query_scaled - query_hat * (query_dot / model_width)[:, None])
    key_proj_grad = key_inv * (key_scaled - key_hat * (key_dot / model_width)[:, None])
    value_grad = value_acc.reshape(seq_len, local_width)
    proj_grad_all = jnp.concatenate([query_proj_grad, key_proj_grad, value_grad], axis=1).astype(
        jnp.bfloat16
    )
    input_grad_attn = lax.psum_scatter(
        contract_cols(proj_grad_all, proj_weight).astype(jnp.bfloat16),
        "row",
        scatter_dimension=0,
        tiled=True,
    ).astype(jnp.float32)
    proj_weight_grad = contract_rows(gathered_x, proj_grad_all)
    query_weight_grad = proj_weight_grad[:, :local_width]
    key_weight_grad = proj_weight_grad[:, local_width : 2 * local_width]
    value_weight_grad = proj_weight_grad[:, 2 * local_width :]
    input_grad = (hidden_grad + input_grad_attn).astype(jnp.bfloat16)
    (
        query_sum,
        key_sum,
        value_sum,
        out_sum,
        qgain_sum,
        kgain_sum,
        again_sum,
        gate_sum,
        up_sum,
        down_sum,
        mgain_sum,
    ) = (
        lax.psum_scatter(
            query_weight_grad.astype(jnp.bfloat16), "col", scatter_dimension=0, tiled=True
        ).astype(jnp.float32),
        lax.psum_scatter(
            key_weight_grad.astype(jnp.bfloat16), "col", scatter_dimension=0, tiled=True
        ).astype(jnp.float32),
        lax.psum_scatter(
            value_weight_grad.astype(jnp.bfloat16), "col", scatter_dimension=0, tiled=True
        ).astype(jnp.float32),
        lax.psum_scatter(out_weight_grad, "col", scatter_dimension=1, tiled=True).astype(
            jnp.float32
        ),
        lax.psum_scatter(
            query_gain_part.astype(jnp.bfloat16), "col", scatter_dimension=0, tiled=True
        ).astype(jnp.float32),
        lax.psum_scatter(
            key_gain_part.astype(jnp.bfloat16), "col", scatter_dimension=0, tiled=True
        ).astype(jnp.float32),
        lax.psum_scatter(
            attn_gain_sum.astype(jnp.bfloat16), "col", scatter_dimension=0, tiled=True
        ).astype(jnp.float32),
        lax.psum_scatter(
            gate_weight_grad.astype(jnp.bfloat16), "col", scatter_dimension=0, tiled=True
        ).astype(jnp.float32),
        lax.psum_scatter(
            up_weight_grad.astype(jnp.bfloat16), "col", scatter_dimension=0, tiled=True
        ).astype(jnp.float32),
        lax.psum_scatter(
            weight_acc.astype(jnp.bfloat16), "col", scatter_dimension=1, tiled=True
        ).astype(jnp.float32),
        lax.psum_scatter(
            mlp_gain_sum.astype(jnp.bfloat16), "col", scatter_dimension=0, tiled=True
        ).astype(jnp.float32),
    )
    return (
        layer_output,
        input_grad,
        query_sum,
        key_sum,
        value_sum,
        out_sum,
        qgain_sum,
        kgain_sum,
        again_sum,
        gate_sum,
        up_sum,
        down_sum,
        mgain_sum,
    )


def solution(mesh):
    placed = (
        P(("col", "row"), None),
        P("col"),
        P("col", "row"),
        P("col", "row"),
        P("col", "row"),
        P("row", "col"),
        P(("row", "col")),
        P(("row", "col")),
        P("col"),
        P("col", "row"),
        P("col", "row"),
        P("row", "col"),
        P("col"),
        P(("col", "row"), None),
    )
    return jax.shard_map(
        body,
        mesh=mesh,
        in_specs=placed,
        out_specs=(
            P(("col", "row"), None),
            P(("col", "row"), None),
            P("col", "row"),
            P("col", "row"),
            P("col", "row"),
            P("row", "col"),
            P(("row", "col")),
            P(("row", "col")),
            P("col"),
            P("col", "row"),
            P("col", "row"),
            P("row", "col"),
            P("col"),
        ),
        check_vma=False,
    )
```

profile of v0, /device:TPU:1, one launch (start us, length us, event | category | flops | bytes accessed | tf_op | source)
XLA Modules:
  0.0 2667.1 jit_solution(5666561886426839380)
XLA Ops:
  10.7 18.2 all-gather.22.cloned.1.call-done
  43.0 9.4 broadcast_multiply_fusion
  68.5 15.2 all-gather.18.cloned.1.call-done
  86.0 226.5 %all-gather.20.cloned.1.call-done = bf16[4096,2048]{1,0:T(8,128)(2,1)} async-done(((bf16[512,2048]{1,0:T(8,128)(2,1)}), bf16[4096,2048]{1,0:T(8,128)(2,1)}) %all-gather.20.cloned.1.call-update) | async-done | bytes 16777232 | tf_op jit(solution)/shard_map/all_gather | solution.py:101
  312.5 21.5 fusion.228
  350.4 28.8 %all-reduce.8 = (f32[4096]{0:T(1024)S(1)}, f32[4096]{0:T(1024)S(1)}) all-reduce(f32[4096]{0:T(1024)S(1)} %get-tuple-element.267, f32[4096]{0:T(1024)S(1)} %get-tuple-element.266), channel_id=1, replica_groups=mesh['row'=8,'col'=4] {'row'}, use_global_device_ids=true, to_apply=%region_5.6 | all-reduce | flops 8192 | bytes 65536 | tf_op jit(solution)/shard_map/psum | solution.py:108
  404.1 7.6 add_convert_fusion.2
  434.5 7.5 fusion.235
  460.7 7.4 fusion.1
  468.2 8.5 fusion.236
  476.7 8.8 fusion
  509.0 8.0 fusion.176
  523.7 12.9 all-gather
  536.6 30.1 %all-to-all-done = bf16[8,512,256]{1,2,0:T(8,128)(2,1)S(1)} async-done(((bf16[8,512,256]{1,2,0:T(8,128)(2,1)}), bf16[8,512,256]{1,2,0:T(8,128)(2,1)S(1)}, u32[]{:S(2)}, u32[]{:S(2)}) %all-to-all-start) | async-done | bytes 2097184 | tf_op jit(solution)/shard_map/all_to_all | solution.py:165
  566.8 7.9 multiply_reduce_fusion.11
  588.8 221.5 %all-gather.26.cloned.1.call-done = bf16[4096,2048]{1,0:T(8,128)(2,1)} async-done(((bf16[512,2048]{1,0:T(8,128)(2,1)}), bf16[4096,2048]{1,0:T(8,128)(2,1)}) %all-gather.26.cloned.1.call-update) | async-done | bytes 16777232 | tf_op jit(solution)/shard_map/all_gather | solution.py:171
  810.3 43.6 %fusion.237 = f32[4096,2048]{0,1:T(8,128)} fusion(bf16[4096,2048]{1,0:T(8,128)(2,1)} %all-gather.26.cloned.1.call-done, bf16[2048,2048]{1,0:T(8,128)(2,1)} %constant_dynamic-update-slice_fusion.3), kind=kOutput, calls=%fused_computation.364 | convolution fusion | flops 34359738368 | bytes 58720256 | tf_op jit(solution)/shard_map/dot_general | solution.py:174
  853.9 14.8 multiply_convert_fusion.3
  868.8 25.1 convolution_convert_fusion.1
  900.6 274.7 %reduce-scatter.12.cloned.1.call-done = bf16[512,2048]{1,0:T(8,128)(2,1)} async-done(((bf16[4096,2048]{1,0:T(8,128)(2,1)}), bf16[512,2048]{1,0:T(8,128)(2,1)}) %reduce-scatter.12.cloned.1.call-update) | async-done | bytes 2097168 | tf_op jit(solution)/shard_map/reduce_scatter | solution.py:178
  1183.7 226.1 %all-gather.34.cloned.1.call-done = bf16[4096,2048]{1,0:T(8,128)(2,1)} async-done(((bf16[512,2048]{1,0:T(8,128)(2,1)}), bf16[4096,2048]{1,0:T(8,128)(2,1)}) %all-gather.34.cloned.1.call-update) | async-done | bytes 16777232 | tf_op jit(solution)/shard_map/all_gather | solution.py:193
  1409.8 33.4 %multiply_convert_fusion.2 = (bf16[4096,1024]{0,1:T(8,128)(2,1)}, bf16[4096,1024]{0,1:T(8,128)(2,1)}) fusion(f32[4096,2048]{0,1:T(8,128)} %fusion.237, bf16[4096,2048]{1,0:T(8,128)(2,1)} %all-gather.34.cloned.1.call-done, bf16[1024,2048]{1,0:T(8,128)(2,1)} %all-gather.32.cloned.1.call-done), kind=kOutput, calls=%fused_computation.5 | convolution fusion | flops 17234395136 | bytes 71303168 | tf_op jit(solution)/shard_map/dot_general | solution.py:42
  1443.1 42.2 %convolution_convert_fusion.2 = bf16[4096,2048]{1,0:T(8,128)(2,1)} fusion(bf16[2048,2048]{1,0:T(8,128)(2,1)} %constant_dynamic-update-slice_fusion.3, bf16[4096,1024]{0,1:T(8,128)(2,1)} %get-tuple-element.285, bf16[4096,1024]{0,1:T(8,128)(2,1)} %get-tuple-element.284), kind=kOutput, calls=%fused_computation.13 | convolution fusion | flops 34401681408 | bytes 41943040 | tf_op jit(solution)/shard_map/dot_general | solution.py:42
  1485.4 281.5 %reduce-scatter.14.cloned.1.call-done = bf16[512,2048]{1,0:T(8,128)(2,1)} async-done(((bf16[4096,2048]{1,0:T(8,128)(2,1)}), bf16[512,2048]{1,0:T(8,128)(2,1)}) %reduce-scatter.14.cloned.1.call-update) | async-done | bytes 2097168 | tf_op jit(solution)/shard_map/reduce_scatter | solution.py:200
  1785.6 23.7 convolution_convert_fusion.4
  1809.4 45.7 %fusion.14 = bf16[2048,2048]{1,0:T(8,128)(2,1)} fusion(bf16[4096,2048]{1,0:T(8,128)(2,1)} %all-gather.26.cloned.1.call-done, bf16[4096,1024]{0,1:T(8,128)(2,1)} %get-tuple-element.285, bf16[4096,1024]{0,1:T(8,128)(2,1)} %get-tuple-element.284), kind=kOutput, calls=%fused_computation.52 | convolution fusion | flops 34397487104 | bytes 41943040 | tf_op jit(solution)/shard_map/dot_general | solution.py:36
  1861.3 8.7 convolution_convert_fusion.6
  1878.1 68.3 %all-to-all-done.1 = bf16[512,8,256]{0,2,1:T(8,128)(2,1)} async-done(((bf16[512,8,256]{0,2,1:T(8,128)(2,1)}), bf16[512,8,256]{0,2,1:T(8,128)(2,1)}, u32[]{:S(2)}, u32[]{:S(2)}) %all-to-all-start.1) | async-done | bytes 2097184 | tf_op jit(solution)/shard_map/all_to_all | solution.py:218
  1999.4 8.9 multiply_convert_fusion.7
  2028.5 11.7 multiply_reduce_fusion.2
  2041.2 10.3 multiply_convert_fusion.5
  2051.5 8.3 fusion.79
  2066.1 8.5 multiply_reduce_fusion.1
  2074.6 10.9 multiply_convert_fusion.4
  2085.5 9.2 fusion.31
  2097.7 11.0 multiply_reduce_fusion
  2108.7 12.5 multiply_convert_fusion
  2128.1 7.9 multiply_subtract_fusion.1
  2164.3 10.0 all-reduce.10
  2174.5 27.5 %all-reduce.9 = (bf16[4096]{0:T(1024)(128)(2,1)S(1)}, bf16[4096]{0:T(1024)(128)(2,1)S(1)}, bf16[512]{0:T(512)(128)(2,1)S(1)}, bf16[512]{0:T(512)(128)(2,1)S(1)}) all-reduce(bf16[4096]{0:T(1024)(128)(2,1)S(1)} %get-tuple-element.261, bf16[4096]{0:T(1024)(128)(2,1)S(1)} %get-tuple-element.264, ...), channel_id=1, replica_groups=mesh['row'=8,'col'=4] {'row'}, use_global_device_ids=true, to_apply=%region_39.40 | all-reduce | flops 9216 | bytes 36864 | tf_op jit(solution)/shard_map/psum | solution.py:277
  2202.1 9.6 fusion.92
  2211.7 10.9 fusion.40
  2235.6 18.2 fusion.101
  2257.8 19.8 convolution_convert_fusion
  2291.1 22.0 reduce-scatter.20.cloned.1.call-done
  2315.0 26.0 reduce-scatter.22.cloned.1.call-done
  2342.9 25.8 reduce-scatter.26.cloned.1.call-done
  2370.4 284.8 %reduce-scatter.16.cloned.1.call-done = bf16[512,2048]{1,0:T(8,128)(2,1)} async-done(((bf16[4096,2048]{1,0:T(8,128)(2,1)}), bf16[512,2048]{1,0:T(8,128)(2,1)}) %reduce-scatter.16.cloned.1.call-update) | async-done | bytes 2097168 | tf_op jit(solution)/shard_map/reduce_scatter | solution.py:289
  (542 shorter events, 366.9 us)
Async XLA Ops:
  7.2 21.6 all-gather.22.cloned.1.call-start
  8.0 55.8 %all-gather.14.cloned.1.call-start = ((), (), s32[]{:S(2)}) async-start(), calls=%async_computation.13 | async-start | bytes 1310720 | tf_op jit(solution)/shard_map/all_gather | solution.py:64
  8.7 57.4 %all-gather.16.cloned.1.call-start = ((), (), s32[]{:S(2)}) async-start(), calls=%async_computation.14 | async-start | bytes 1310720 | tf_op jit(solution)/shard_map/all_gather | solution.py:65
  9.4 74.2 %all-gather.18.cloned.1.call-start = ((), (), s32[]{:S(2)}) async-start(), calls=%async_computation.15 | async-start | bytes 1310720 | tf_op jit(solution)/shard_map/all_gather | solution.py:66
  10.0 302.5 %all-gather.20.cloned.1.call-start = ((), (), s32[]{:S(2)}) async-start(), calls=%async_computation.16 | async-start | bytes 18874368 | tf_op jit(solution)/shard_map/all_gather | solution.py:101
  10.6 526.0 %all-gather.24.cloned.1.call-start = ((), (), s32[]{:S(2)}) async-start(), calls=%async_computation.18 | async-start | bytes 9437184 | tf_op jit(solution)/shard_map/all_gather | solution.py:102
  28.9 550.5 %all-gather.28.cloned.1.call-start = ((), (), s32[]{:S(2)}) async-start(), calls=%async_computation.20 | async-start | bytes 5242880 | tf_op jit(solution)/shard_map/all_gather | solution.py:71
  29.6 554.4 %all-gather.30.cloned.1.call-start = ((), (), s32[]{:S(2)}) async-start(), calls=%async_computation.21 | async-start | bytes 5242880 | tf_op jit(solution)/shard_map/all_gather | solution.py:72
  37.7 341.6 %copy-start.109 = (f32[256]{0:T(256)}, f32[256]{0:T(256)S(1)}, u32[]{:S(2)}) copy-start(f32[256]{0:T(256)S(1)} %convert_element_type.224) | copy-start | bytes 3076
  37.7 341.6 %copy-start.111 = (f32[256]{0:T(256)}, f32[256]{0:T(256)S(1)}, u32[]{:S(2)}) copy-start(f32[256]{0:T(256)S(1)} %convert_element_type.222) | copy-start | bytes 3076
  52.3 351.7 %copy-start.28 = (f32[4096,64]{1,0:T(8,128)}, f32[4096,64]{1,0:T(8,128)S(1)}, u32[]{:S(2)}) copy-start(f32[4096,64]{1,0:T(8,128)S(1)} %get-tuple-element.323) | copy-start | bytes 3145732
  411.7 56.4 %copy-start.4 = (bf16[4096,2,64]{2,0,1:T(8,128)(2,1)}, bf16[4096,2,64]{2,0,1:T(8,128)(2,1)S(1)}, u32[]{:S(2)}) copy-start(bf16[4096,2,64]{2,0,1:T(8,128)(2,1)S(1)} %get-tuple-element.304) | copy-start | bytes 3145732
  411.7 56.4 %copy-start.6 = (bf16[4096,2,64]{2,0,1:T(8,128)(2,1)}, bf16[4096,2,64]{2,0,1:T(8,128)(2,1)S(1)}, u32[]{:S(2)}) copy-start(bf16[4096,2,64]{2,0,1:T(8,128)(2,1)S(1)} %get-tuple-element.305) | copy-start | bytes 3145732
  414.6 70.9 %copy-start.83 = (f32[2,512]{1,0:T(2,128)}, f32[2,512]{1,0:T(2,128)S(1)}, u32[]{:S(2)}) copy-start(f32[2,512]{1,0:T(2,128)S(1)} %get-tuple-element.338) | copy-start | bytes 12292
  416.7 72.2 %copy-start.75 = (f32[2,512]{1,0:T(2,128)}, f32[2,512]{1,0:T(2,128)S(1)}, u32[]{:S(2)}) copy-start(f32[2,512]{1,0:T(2,128)S(1)} %get-tuple-element.340) | copy-start | bytes 12292
  421.9 69.0 %copy-start.73 = (f32[2,512]{1,0:T(2,128)}, f32[2,512]{1,0:T(2,128)S(1)}, u32[]{:S(2)}) copy-start(f32[2,512]{1,0:T(2,128)S(1)} %get-tuple-element.342) | copy-start | bytes 12292
  427.7 66.7 %copy-start.77 = (f32[2,512]{1,0:T(2,128)}, f32[2,512]{1,0:T(2,128)S(1)}, u32[]{:S(2)}) copy-start(f32[2,512]{1,0:T(2,128)S(1)} %get-tuple-element.344) | copy-start | bytes 12292
  434.5 63.6 %copy-start.79 = (f32[2,512]{1,0:T(2,128)}, f32[2,512]{1,0:T(2,128)S(1)}, u32[]{:S(2)}) copy-start(f32[2,512]{1,0:T(2,128)S(1)} %get-tuple-element.346) | copy-start | bytes 12292
  442.0 62.7 %copy-start.85 = (f32[2,512]{1,0:T(2,128)}, f32[2,512]{1,0:T(2,128)S(1)}, u32[]{:S(2)}) copy-start(f32[2,512]{1,0:T(2,128)S(1)} %get-tuple-element.348) | copy-start | bytes 12292
  445.4 40.1 %copy-start.102 = (f32[2,512]{1,0:T(2,128)}, f32[2,512]{1,0:T(2,128)S(1)}, u32[]{:S(2)}) copy-start(f32[2,512]{1,0:T(2,128)S(1)} %fusion.95) | copy-start | bytes 12292
  446.5 42.5 %copy-start.97 = (f32[2,512]{1,0:T(2,128)}, f32[2,512]{1,0:T(2,128)S(1)}, u32[]{:S(2)}) copy-start(f32[2,512]{1,0:T(2,128)S(1)} %fusion.25) | copy-start | bytes 12292
  452.6 38.3 %copy-start.89 = (f32[2,512]{1,0:T(2,128)}, f32[2,512]{1,0:T(2,128)S(1)}, u32[]{:S(2)}) copy-start(f32[2,512]{1,0:T(2,128)S(1)} %fusion.15) | copy-start | bytes 12292
  454.3 40.1 %copy-start.95 = (f32[2,512]{1,0:T(2,128)}, f32[2,512]{1,0:T(2,128)S(1)}, u32[]{:S(2)}) copy-start(f32[2,512]{1,0:T(2,128)S(1)} %fusion.7) | copy-start | bytes 12292
  460.7 37.4 %copy-start.93 = (f32[2,512]{1,0:T(2,128)}, f32[2,512]{1,0:T(2,128)S(1)}, u32[]{:S(2)}) copy-start(f32[2,512]{1,0:T(2,128)S(1)} %fusion.4) | copy-start | bytes 12292
  468.2 36.6 %copy-start.91 = (f32[2,512]{1,0:T(2,128)}, f32[2,512]{1,0:T(2,128)S(1)}, u32[]{:S(2)}) copy-start(f32[2,512]{1,0:T(2,128)S(1)} %fusion.1) | copy-start | bytes 12292
  520.0 46.8 %all-to-all-start = ((bf16[8,512,256]{1,2,0:T(8,128)(2,1)}), bf16[8,512,256]{1,2,0:T(8,128)(2,1)S(1)}, u32[]{:S(2)}, u32[]{:S(2)}) async-start(bf16[8,512,256]{1,2,0:T(8,128)(2,1)} %copy.156), calls=%async_computation | async-start | bytes 4194304 | tf_op jit(solution)/shard_map/all_to_all | solution.py:165
  523.6 286.7 %all-gather.26.cloned.1.call-start = ((), (), s32[]{:S(2)}) async-start(), calls=%async_computation.19 | async-start | bytes 18874368 | tf_op jit(solution)/shard_map/all_gather | solution.py:171
  536.6 38.1 %copy-start.71 = (f32[4,1,512]{2,1,0:T(1,128)}, f32[4,1,512]{2,1,0:T(1,128)S(1)}, u32[]{:S(2)}) copy-start(f32[4,1,512]{2,1,0:T(1,128)S(1)} %convert_element_type.287) | copy-start | bytes 24580
  578.7 290.1 %all-gather.32.cloned.1.call-start = ((), (), s32[]{:S(2)}) async-start(), calls=%async_computation.22 | async-start | bytes 5242880 | tf_op jit(solution)/shard_map/all_gather | solution.py:73
  579.3 596.0 %reduce-scatter.12.cloned.1.call-start = ((), (), s32[]{:S(2)}) async-start(), calls=%async_computation.23 | async-start | bytes 18874368 | tf_op jit(solution)/shard_map/reduce_scatter | solution.py:178
  893.8 283.7 %copy-start.20 = (bf16[512,2048]{1,0:T(8,128)(2,1)S(1)}, bf16[512,2048]{1,0:T(8,128)(2,1)}, u32[]{:S(2)}) copy-start(bf16[512,2048]{1,0:T(8,128)(2,1)} %param.63) | copy-start | bytes 6291460
  893.9 515.9 %all-gather.34.cloned.1.call-start = ((), (), s32[]{:S(2)}) async-start(), calls=%async_computation.24 | async-start | bytes 18874368 | tf_op jit(solution)/shard_map/all_gather | solution.py:193
  1183.4 583.4 %reduce-scatter.14.cloned.1.call-start = ((), (), s32[]{:S(2)}) async-start(), calls=%async_computation.25 | async-start | bytes 18874368 | tf_op jit(solution)/shard_map/reduce_scatter | solution.py:200
  1485.3 281.6 %copy-start.72 = (f32[4,1,512]{2,1,0:T(1,128)S(1)}, f32[4,1,512]{2,1,0:T(1,128)}, u32[]{:S(2)}) copy-start(f32[4,1,512]{2,1,0:T(1,128)} %copy-done.71) | copy-start | bytes 24580
  1485.3 281.6 %copy-start.88 = (f32[512]{0:T(512)S(1)}, f32[512]{0:T(512)}, u32[]{:S(2)}) copy-start(f32[512]{0:T(512)} %copy-done.87) | copy-start | bytes 6148
  1485.3 771.8 %reduce-scatter.24.cloned.1.call-start = ((), (), s32[]{:S(2)}) async-start(), calls=%async_computation.30 | async-start | bytes 9437184 | tf_op jit(solution)/shard_map/reduce_scatter | solution.py:221
  1785.5 492.7 %reduce-scatter.32.cloned.1.call-start = ((), (), s32[]{:S(2)}) async-start(), calls=%async_computation.34 | async-start | bytes 5242880 | tf_op jit(solution)/shard_map/reduce_scatter | solution.py:340
  1809.3 471.8 %reduce-scatter.28.cloned.1.call-start = ((), (), s32[]{:S(2)}) async-start(), calls=%async_computation.32 | async-start | bytes 5242880 | tf_op jit(solution)/shard_map/reduce_scatter | solution.py:334
  1872.6 73.7 %all-to-all-start.1 = ((bf16[512,8,256]{0,2,1:T(8,128)(2,1)}), bf16[512,8,256]{0,2,1:T(8,128)(2,1)}, u32[]{:S(2)}, u32[]{:S(2)}) async-start(bf16[512,8,256]{0,2,1:T(8,128)(2,1)} %bitcast.26), calls=%async_computation.3 | async-start | bytes 4194304 | tf_op jit(solution)/shard_map/all_to_all | solution.py:218
  1877.0 407.1 %reduce-scatter.30.cloned.1.call-start = ((), (), s32[]{:S(2)}) async-start(), calls=%async_computation.33 | async-start | bytes 5242880 | tf_op jit(solution)/shard_map/reduce_scatter | solution.py:337
  1878.0 70.1 %copy-start.19 = (f32[2,512,512]{1,2,0:T(8,128)S(1)}, f32[2,512,512]{1,2,0:T(8,128)}, u32[]{:S(2)}) copy-start(f32[2,512,512]{1,2,0:T(8,128)} %copy-done.18) | copy-start | bytes 6291460
  1878.0 70.6 %copy-start.63 = (bf16[512,256]{0,1:T(8,128)(2,1)S(1)}, bf16[512,256]{0,1:T(8,128)(2,1)}, u32[]{:S(2)}) copy-start(bf16[512,256]{0,1:T(8,128)(2,1)} %slice.843) | copy-start | bytes 786436
  1878.0 411.2 %reduce-scatter.18.cloned.1.call-start = ((), (), s32[]{:S(2)}) async-start(), calls=%async_computation.27 | async-start | bytes 1310720 | tf_op jit(solution)/shard_map/reduce_scatter | solution.py:313
  2255.7 57.4 %reduce-scatter.20.cloned.1.call-start = ((), (), s32[]{:S(2)}) async-start(), calls=%async_computation.28 | async-start | bytes 1310720 | tf_op jit(solution)/shard_map/reduce_scatter | solution.py:316
  2256.4 84.6 %reduce-scatter.22.cloned.1.call-start = ((), (), s32[]{:S(2)}) async-start(), calls=%async_computation.29 | async-start | bytes 1310720 | tf_op jit(solution)/shard_map/reduce_scatter | solution.py:319
  2257.0 111.6 %reduce-scatter.26.cloned.1.call-start = ((), (), s32[]{:S(2)}) async-start(), calls=%async_computation.31 | async-start | bytes 1310720 | tf_op jit(solution)/shard_map/reduce_scatter | solution.py:322
  2257.7 397.5 %reduce-scatter.16.cloned.1.call-start = ((), (), s32[]{:S(2)}) async-start(), calls=%async_computation.26 | async-start | bytes 18874368 | tf_op jit(solution)/shard_map/reduce_scatter | solution.py:289
  2281.1 374.1 %copy-start.21 = (bf16[512,2048]{1,0:T(8,128)(2,1)S(1)}, bf16[512,2048]{1,0:T(8,128)(2,1)}, u32[]{:S(2)}) copy-start(bf16[512,2048]{1,0:T(8,128)(2,1)} %param.63) | copy-start | bytes 6291460
  (131 other events, 1127.1 us)
Sparse Core Ops, SparseCore 0:
  9.6 19.1 all-gather.21
  30.4 16.7 all-gather.13
  48.7 16.7 all-gather.15
  66.9 16.7 all-gather.17
  85.6 226.8 all-gather.19
  314.5 123.7 all-gather.23
  439.8 33.6 all-gather.27
  475.0 34.4 all-gather.29
  578.8 231.4 all-gather.25
  811.7 33.4 all-gather.31
  894.0 281.2 reduce-scatter.11
  1183.6 226.1 all-gather.33
  1485.4 281.3 reduce-scatter.13
  1785.7 175.3 reduce-scatter.23
  1963.6 43.1 reduce-scatter.31
  2009.1 44.4 reduce-scatter.27
  2056.2 44.5 reduce-scatter.29
  2255.8 29.6 reduce-scatter.17
  2288.2 24.8 reduce-scatter.19
  2316.0 24.8 reduce-scatter.21
  2343.7 24.8 reduce-scatter.25
  2372.4 282.7 reduce-scatter.15
where the time goes:
time: 2680 us; the launch traced here: 2670 us
  waiting for transfers between devices  1730 us (65%)
  matrix products  504 us (19%)
  other arithmetic  215 us (8%)
  local copies, waits for them, and re-layouts  102 us (4%)
  blocking collectives  90.6 us (3%)
    reduce_scatter x1, waiting for transfers between devices, body(): lax.psum_scatter(contract_cols(proj_grad_all, proj_weight).astype(jnp.bfl...  285 us
    reduce_scatter x1, waiting for transfers between devices, body(): lax.psum_scatter(contract_cols(ff_grad, ff_weight).astype(jnp.bfloat16),...  281 us
    reduce_scatter x1, waiting for transfers between devices, body(): lax.psum_scatter(jnp.dot(activated, down_rows, preferred_element_type=jnp...  275 us
    all_gather x1, waiting for transfers between devices, body(): lax.all_gather(layer_input, 'row', axis=0, tiled=True)  227 us
    all_gather x1, waiting for transfers between devices, body(): shard_rows = lax.all_gather(mlp_grad, 'row', axis=0, tiled=True)  226 us
    all_gather x1, waiting for transfers between devices, body(): gathered_h = lax.all_gather(hidden_low, 'row', axis=0, tiled=True)  222 us
    dot_general x4, matrix products, contract_cols(): lax.dot_general(left, right, (((1,), (1,)), ((), ())), preferred_element_...  104 us
    dot_general x4, matrix products, contract_rows(): lax.dot_general(left, right, (((0,), (0,)), ((), ())), preferred_element_...  94.4 us
  transfers between devices with their start and end apart: 24, of which 13 were waited for; matrix products, arithmetic and copies ran while one was open for 25% of the time, Pallas kernels for 0%

commit v1 on v0

v1 whole, which is shorter than its diff:
```python
import functools

import jax
import jax.numpy as jnp
from jax import lax
from jax.experimental import pallas as pl
from jax.experimental.pallas import tpu as pltpu
from jax.sharding import PartitionSpec as P

HEADS = 16


EPS = 1e-06
THETA = 500000.0
MASKED = -1e30
LOG2E = 1.4426950408889634
BOTH = ("row", "col")
MESH = pl.DeviceIdType.MESH


class Plan:
    def __init__(self, mesh):
        self.rows, self.cols = mesh.shape["row"], mesh.shape["col"]
        self.half = self.rows // 2
        self.across = self.cols // 2
        self.places = [
            (zhi, rest, xx, core)
            for zhi in range(2)
            for rest in range(self.half)
            for xx in range(self.across)
            for core in range(2)
        ]
        self.token_groups = [
            [self.device(zhi, rest, xx, core) for core in range(2) for rest in range(self.half)]
            for xx in range(self.across)
            for zhi in range(2)
        ]

    def device(self, zhi, rest, xx, core):
        return (zhi * self.half + rest) * self.cols + xx * 2 + core

    def here(self):
        row, col = lax.axis_index("row"), lax.axis_index("col")
        return row // self.half, row % self.half, col // 2, col % 2

    def same(self):
        zhi, _, _, core = self.here()
        return zhi == core

    def block(self):
        _, rest, _, core = self.here()
        return core * self.half + rest

    def send(self, value, target):
        pairs = []
        for place in self.places:
            to = target(*place)
            if to is not None:
                pairs.append((self.device(*place), self.device(*to)))
        return lax.ppermute(value, BOTH, pairs)

    def swap(self, value):
        moved = self.send(
            value,
            lambda zhi, rest, xx, core: None if zhi == core else (core, rest, xx, zhi),
        )
        return jnp.where(self.same(), value, moved)

    def partner(self, value, flip):
        def target(zhi, rest, xx, core):
            to = (core * self.half + rest) ^ flip
            return zhi, to % self.half, xx, to // self.half

        return self.send(value, target)

    def token_gather(self, value):
        return lax.all_gather(
            value, BOTH, axis=0, tiled=True, axis_index_groups=self.token_groups
        )

    def token_sum(self, value):
        flip = 1
        while flip < self.rows:
            value = value + self.partner(value, flip)
            flip *= 2
        return value

    def weight_pair(self, value):
        def outward(zhi, rest, xx, core):
            return (1 - zhi, rest, xx, core) if zhi == core else (zhi, rest, xx, 1 - core)

        def over(zhi, rest, xx, core):
            return None if zhi == core else (1 - zhi, rest, xx, 1 - core)

        first = self.send(value, outward)
        second = self.send(value, over)
        same = self.same()
        return jnp.where(same, value, first), jnp.where(same, first, second)

    def weight_pieces(self, pair):
        _, _, xx, core = self.here()
        pieces = []
        for flip in range(self.across):
            for j, part in enumerate(pair):
                if flip:
                    part = self.send(part, lambda z, r, x, c: (z, r, x ^ flip, c))
                pieces.append(((xx ^ flip) * 2 + (core ^ j), part))
        return pieces

    def weight_exchange(self, value, axis):
        xx = self.here()[2]
        size = value.shape[axis] // self.across
        received = []
        for step in range(1, self.across):
            part = lax.dynamic_slice_in_dim(value, (xx + step) % self.across * size, size, axis)
            received.append(
                self.send(part, lambda z, r, x, c: (z, r, (x + step) % self.across, c))
            )
        return jnp.stack(received)

    def weight_sum(self, value, received, axis):
        size = value.shape[axis] // self.across
        total = lax.dynamic_slice_in_dim(value, self.here()[2] * size, size, axis)
        total = total.astype(jnp.float32)
        for step in range(self.across - 1):
            total = total + received[step].astype(jnp.float32)
        return total.astype(jnp.bfloat16)

    def weight_send(self, total, axis):
        core = self.here()[3]
        size = total.shape[axis] // 2
        near = lax.dynamic_slice_in_dim(total, core * size, size, axis)
        far = lax.dynamic_slice_in_dim(total, (1 - core) * size, size, axis)
        same = self.same()

        def outward(zhi, rest, xx, core):
            return (zhi, rest, xx, 1 - core) if zhi == core else (1 - zhi, rest, xx, core)

        def over(zhi, rest, xx, core):
            return None if zhi == core else (1 - zhi, rest, xx, 1 - core)

        first = self.send(jnp.where(same, far, near), outward)
        second = self.send(far, over)
        return jnp.where(same, near, second).astype(jnp.float32) + first.astype(jnp.float32)


def join(shape, pieces):
    whole = jnp.zeros(shape, pieces[0][2].dtype)
    for row, col, piece in pieces:
        whole = lax.dynamic_update_slice(whole, piece, (row, col))
    return whole


def after(value, *others):
    return lax.optimization_barrier((value, *others))[0]


def contract_rows(left, right):
    return lax.dot_general(
        left, right, (((0,), (0,)), ((), ())), preferred_element_type=jnp.float32
    )


def contract_cols(left, right):
    return lax.dot_general(
        left, right, (((1,), (1,)), ((), ())), preferred_element_type=jnp.float32
    )


def position(plan):
    row, col = lax.axis_index("row"), lax.axis_index("col")
    zhi, rest, core = row // plan.half, row % plan.half, col % 2
    return zhi, rest, col - core, core


def remote(source, target, send_sem, recv_sem, row, col):
    return pltpu.make_async_remote_copy(
        src_ref=source,
        dst_ref=target,
        send_sem=send_sem,
        recv_sem=recv_sem,
        device_id=(row, col),
        device_id_type=MESH,
    )


def gather_kernel(plan, own, weight, out, weights, *sems):
    have_sem, swap_sem, send_sem, recv_sem, near_sem, near_recv_sem = sems[:6]
    block_sem, block_recv_sem, side_sem, side_recv_sem = sems[6:]
    half, across = plan.half, plan.across
    zhi, rest, base, core = position(plan)
    xx = base // 2
    row, col = zhi * half + rest, base + core
    far_row, near_col = (1 - zhi) * half + rest, base + 1 - core
    rows = own.shape[0]
    part = rows // 2
    depth = weight.shape[0]
    moved, stays = zhi != core, zhi == core

    barrier = pltpu.get_barrier_semaphore()
    greeted = [(row, near_col), (far_row, col), (far_row, near_col)]
    greeted += [(zhi * half + (rest + step) % half, col) for step in range(1, half)]
    greeted += [(row, (xx + step) % across * 2 + core) for step in range(1, across)]
    for device in greeted:
        pl.semaphore_signal(barrier, 1, device_id=device, device_id_type=MESH)
    pl.semaphore_wait(barrier, len(greeted))

    def lines(block, h):
        return pl.ds(pl.multiple_of(block * rows + h * part, part), part)

    def entry_near(h):
        source = own.at[pl.ds(h * part, part)]
        return pltpu.make_async_copy(
            source, out.at[lines(core * half + rest, h)], have_sem.at[h]
        )

    def entry_far(h):
        return remote(
            own.at[pl.ds(h * part, part)],
            out.at[lines(zhi * half + rest, h)],
            swap_sem.at[h],
            have_sem.at[h],
            far_row,
            near_col,
        )

    def sibling(step, h):
        at = out.at[lines(core * half + (rest + half - step) % half, h)]
        return remote(
            at, at, near_sem.at[step, h], near_recv_sem.at[step, h], row, near_col
        )

    def outward(step, h):
        at = out.at[lines(core * half + rest, h)]
        chip = zhi * half + (rest + step) % half
        return remote(at, at, send_sem.at[step - 1, h], recv_sem.at[step - 1, h], chip, col)

    def place(other, j):
        return pl.ds(pl.multiple_of((other * 2 + j) * depth, depth), depth)

    def block_keep():
        return pltpu.make_async_copy(
            weight, weights.at[place(xx, core)], block_recv_sem.at[core]
        )

    def block_send(index, to_row, to_col):
        return remote(
            weight,
            weights.at[place(xx, core)],
            block_sem.at[index],
            block_recv_sem.at[core],
            to_row,
            to_col,
        )

    def side(step, j):
        at = weights.at[place(xx, j)]
        other = (xx + step) % across * 2 + core
        return remote(
            at, at, side_sem.at[step - 1, j], side_recv_sem.at[step - 1, j], row, other
        )

    @pl.when(moved)
    def _():
        for h in range(2):
            entry_far(h).start()
        block_send(0, row, near_col).start()
        block_send(1, far_row, near_col).start()

    @pl.when(stays)
    def _():
        for h in range(2):
            entry_near(h).start()
        block_keep().start()
        block_send(0, far_row, col).start()

    for h in range(2):

        @pl.when(moved)
        def _():
            entry_far(h).wait_recv()

        @pl.when(stays)
        def _():
            entry_near(h).wait()

        for step in range(1, half):
            outward(step, h).start()
        sibling(0, h).start()
        if h == 0:
            for j in range(2):
                pltpu.make_async_copy(weight, weights.at[place(xx, j)], block_recv_sem.at[j]).wait()
                for step in range(1, across):
                    side(step, j).start()
    for h in range(2):
        for step in range(1, half):
            outward(step, h).wait_recv()
            sibling(step, h).start()
    for h in range(2):
        for step in range(half):
            sibling(step, h).wait()
        for step in range(1, half):
            outward(step, h).wait_send()
    for j in range(2):
        for step in range(1, across):
            side(step, j).wait()

    @pl.when(moved)
    def _():
        for h in range(2):
            entry_far(h).wait_send()
        block_send(0, row, near_col).wait_send()
        block_send(1, far_row, near_col).wait_send()

    @pl.when(stays)
    def _():
        block_send(0, far_row, col).wait_send()


def swap_gather(plan, own, weight, collective_id):
    half = plan.half
    dma = pltpu.SemaphoreType.DMA
    shape = (own.shape[0] * plan.rows, own.shape[1])
    anywhere = pl.BlockSpec(memory_space=pl.ANY)
    return pl.pallas_call(
        functools.partial(gather_kernel, plan),
        in_specs=[anywhere] * 2,
        out_specs=[anywhere] * 2,
        out_shape=[
            jax.ShapeDtypeStruct(shape, own.dtype),
            jax.ShapeDtypeStruct((weight.shape[0] * plan.cols, weight.shape[1]), weight.dtype),
        ],
        scratch_shapes=[
            dma((2,)),
            dma((2,)),
            dma((half - 1, 2)),
            dma((half - 1, 2)),
            dma((half, 2)),
            dma((half, 2)),
            dma((2,)),
            dma((2,)),
            dma((plan.across - 1, 2)),
            dma((plan.across - 1, 2)),
        ],
        cost_estimate=pl.CostEstimate(
            flops=0, bytes_accessed=20 * shape[0] * shape[1], transcendentals=0
        ),
        compiler_params=pltpu.CompilerParams(collective_id=collective_id, has_side_effects=True),
    )(own, weight)


def scatter_kernel(plan, parts, axes, turned, last, *refs):
    half, across, count = plan.half, plan.across, len(axes)
    lefts, weight, refs = refs[:parts], refs[parts], refs[parts + 1 :]
    grads, refs = refs[:count], refs[count:]
    if last:
        residual, refs = refs[0], refs[1:]
    out, blocks, refs = refs[0], refs[1 : count + 1], refs[count + 1 :]
    if last:
        sums, refs = refs[0], refs[1:]
    loaded, near_out, near_in, far_out, far_in = refs[:5]
    load_sem, near_sem, near_recv_sem, far_sem, far_recv_sem, block_sem, block_recv_sem = refs[5:12]
    refs = refs[12:]
    zhi, rest, base, core = position(plan)
    xx = base // 2
    row, col = zhi * half + rest, base + core
    far_row, near_col = (1 - zhi) * half + rest, base + 1 - core
    moved, stays = zhi != core, zhi == core
    part, width = near_out.shape[1:]
    rows = 2 * part
    tile = min(512, width)

    barrier = pltpu.get_barrier_semaphore()
    greeted = [(row, near_col)]
    greeted += [(zhi * half + (rest + step) % half, col) for step in range(1, half)]
    if count:
        greeted += [(row, (xx + step) % across * 2 + core) for step in range(1, across)]
    if last:
        greeted += [(far_row, col), (far_row, near_col)]
    for device in greeted:
        pl.semaphore_signal(barrier, 1, device_id=device, device_id_type=MESH)

    def block(index, step):
        grad, axis = grads[index], axes[index]
        other = (xx + step) % across
        size = grad.shape[axis] // across
        at = pl.ds(pl.multiple_of(other * size, size), size)
        return remote(
            grad.at[at] if axis == 0 else grad.at[:, at],
            blocks[index].at[step - 1],
            block_sem.at[index, step - 1],
            block_recv_sem.at[index, step - 1],
            row,
            other * 2 + core,
        )

    def load(unit, whose, slot):
        h, step = unit // half, half - 1 - unit % half
        side = (1 - core) if whose == 0 else core
        index = side * half + (rest + step) % half
        target, sem = loaded.at[slot, whose], load_sem.at[slot, whose]
        if parts == 1:
            at = pl.ds(pl.multiple_of(index * rows + h * part, part), part)
            return [(None, pltpu.make_async_copy(lefts[0].at[at], target, sem))]
        at = pl.ds(pl.multiple_of(index * part, part), part)
        return [
            (h == k, pltpu.make_async_copy(lefts[k].at[at], target, sem)) for k in range(2)
        ]

    def start(copies):
        for when, copy in copies:
            if when is None:
                copy.start()
            else:
                pl.when(when)(copy.start)

    def near(unit, slot):
        return remote(
            near_out.at[slot],
            near_in.at[unit],
            near_sem.at[unit],
            near_recv_sem.at[unit],
            row,
            near_col,
        )

    def far(unit):
        step = half - 1 - unit % half
        chip = zhi * half + (rest + step) % half
        return remote(
            far_out.at[unit], far_in.at[unit], far_sem.at[unit], far_recv_sem.at[unit], chip, col
        )

    def product(left, cols):
        if turned:
            return contract_cols(left, weight[cols, :])
        return jnp.dot(left, weight[:, cols], preferred_element_type=jnp.float32)

    def columns(n):
        return pl.ds(pl.multiple_of(n * tile, tile), tile)

    start(load(0, 0, 0))
    pl.semaphore_wait(barrier, len(greeted))
    for index in range(count):
        for step in range(1, across):
            block(index, step).start()

    def body(unit, carry):
        slot = unit % 2
        before = unit - 1

        @pl.when(unit + 1 < 2 * half)
        def _():
            start(load(unit + 1, 0, 1 - slot))

        @pl.when(unit < 2 * half)
        def _():
            start(load(unit, 1, 1 - slot))
            load(unit, 0, slot)[0][1].wait()

            @pl.when(unit >= 2)
            def _():
                near(unit - 2, slot).wait_send()

            @pl.loop(0, width // tile)
            def _(n):
                value = product(loaded[slot, 0], columns(n))
                near_out[slot, :, columns(n)] = value.astype(near_out.dtype)

            near(unit, slot).start()

        @pl.when(unit >= 1)
        def _():
            load(before, 1, slot)[0][1].wait()
            near(before, 1 - slot).wait_recv()

            @pl.loop(0, width // tile)
            def _(n):
                value = product(loaded[slot, 1], columns(n))
                value = value + near_in[before, :, columns(n)].astype(jnp.float32)
                far_out[before, :, columns(n)] = value.astype(far_out.dtype)

            @pl.when(before % half < half - 1)
            def _():
                far(before).start()

        return carry

    lax.fori_loop(0, 2 * half + 1, body, 0)

    def total(h):
        for step in range(half - 1):
            far(h * half + step).wait_recv()
        value = far_out[h * half + half - 1].astype(jnp.float32)
        for step in range(half - 1):
            value = value + far_in[h * half + step].astype(jnp.float32)
        return value

    if last:
        finish_sum = finish(
            (zhi, rest, xx, core), (row, col, far_row, near_col), grads, blocks, block, sums, refs
        )
        final, final_sem, final_recv_sem = refs[:3]

        def swap_far(h):
            return remote(
                final.at[h],
                out.at[pl.ds(h * part, part)],
                final_sem.at[h],
                final_recv_sem.at[h],
                far_row,
                near_col,
            )

        def swap_near(h):
            return pltpu.make_async_copy(
                final.at[h], out.at[pl.ds(h * part, part)], final_recv_sem.at[h]
            )

        for h in range(2):
            value = total(h) + residual[h * part : (h + 1) * part, :]
            final[h] = value.astype(final.dtype)

            @pl.when(moved)
            def _():
                swap_far(h).start()

            @pl.when(stays)
            def _():
                swap_near(h).start()

            if h == 0:
                finish_sum()

        for h in range(2):

            @pl.when(moved)
            def _():
                swap_far(h).wait()

            @pl.when(stays)
            def _():
                swap_near(h).wait()

    else:
        for h in range(2):
            out[h * part : (h + 1) * part, :] = total(h)
        for index in range(count):
            for step in range(1, across):
                block(index, step).wait_recv()
    for h in range(2):
        for unit in range(h * half, h * half + half - 1):
            far(unit).wait_send()
    for unit in range(2 * half - 2, 2 * half):
        near(unit, unit % 2).wait_send()
    for index in range(count):
        for step in range(1, across):
            block(index, step).wait_send()


def finish(place, devices, grads, blocks, block, sums, refs):
    zhi, _, xx, core = place
    row, col, far_row, near_col = devices
    grad, blocks = grads[0], blocks[0]
    mine, others, pair, landed, mine_sem, pair_sem, landed_sem = refs[3:]
    size = pair.shape[1]
    across = blocks.shape[0] + 1
    own = pltpu.make_async_copy(
        grad.at[pl.ds(pl.multiple_of(xx * 2 * size, size), 2 * size)], mine, mine_sem.at[0]
    )
    rest = [
        pltpu.make_async_copy(blocks.at[step], others.at[step], mine_sem.at[step + 1])
        for step in range(across - 1)
    ]

    def give(index, slot, to_row, to_col, to_slot):
        return remote(
            pair.at[slot],
            landed.at[to_slot],
            pair_sem.at[index],
            landed_sem.at[to_slot],
            to_row,
            to_col,
        )

    to_sibling = give(0, 1 - core, row, near_col, 0)
    to_same = give(0, core, far_row, col, 0)
    to_cross = give(1, 1 - core, far_row, near_col, 1)
    own.start()

    def run():
        for step in range(1, across):
            block(0, step).wait_recv()
            rest[step - 1].start()
        own.wait()
        for copy in rest:
            copy.wait()
        value = mine[...].astype(jnp.float32)
        for step in range(across - 1):
            value = value + others[step].astype(jnp.float32)
        pair[0] = value[:size].astype(pair.dtype)
        pair[1] = value[size:].astype(pair.dtype)

        @pl.when(zhi == core)
        def _():
            to_sibling.start()
            to_sibling.wait_send()
            give(0, core, far_row, col, 0).wait_recv()
            sums[...] = pair[core].astype(jnp.float32) + landed[0].astype(jnp.float32)

        @pl.when(zhi != core)
        def _():
            to_same.start()
            to_cross.start()
            to_same.wait_send()
            to_cross.wait_send()
            to_same.wait_recv()
            to_cross.wait_recv()
            sums[...] = landed[1].astype(jnp.float32) + landed[0].astype(jnp.float32)

    return run


def cut(shape, axis, pieces):
    return tuple(size // pieces if dim == axis else size for dim, size in enumerate(shape))


def multiply_scatter(plan, lefts, weight, turned, collective_id, grads=(), axes=(), residual=None):
    half, across, count = plan.half, plan.across, len(grads)
    depth = lefts[0].shape[1]
    width = weight.shape[0 if turned else 1]
    rows = sum(left.shape[0] for left in lefts) // plan.rows
    part = rows // 2
    low = jnp.bfloat16
    dma = pltpu.SemaphoreType.DMA
    anywhere = pl.BlockSpec(memory_space=pl.ANY)
    inside = pl.BlockSpec(memory_space=pltpu.VMEM)
    last = residual is not None
    in_specs = [anywhere] * len(lefts) + [inside] + [anywhere] * count + [inside] * last
    out_specs = [anywhere if last else inside] + [anywhere] * count + [inside] * last
    out_shape = [jax.ShapeDtypeStruct((rows, width), low if last else jnp.float32)]
    out_shape += [
        jax.ShapeDtypeStruct((across - 1, *cut(grad.shape, axis, across)), low)
        for grad, axis in zip(grads, axes, strict=True)
    ]
    scratch = [
        pltpu.VMEM((2, 2, part, depth), low),
        pltpu.VMEM((2, part, width), low),
        pltpu.VMEM((2 * half, part, width), low),
        pltpu.VMEM((2 * half, part, width), low),
        pltpu.VMEM((2 * half, part, width), low),
        dma((2, 2)),
        dma((2 * half,)),
        dma((2 * half,)),
        dma((2 * half,)),
        dma((2 * half,)),
        dma((max(count, 1), across - 1)),
        dma((max(count, 1), across - 1)),
    ]
    if last:
        size, wide = grads[0].shape[0] // plan.cols, grads[0].shape[1]
        out_shape.append(jax.ShapeDtypeStruct((size, wide), jnp.float32))
        scratch += [
            pltpu.VMEM((2, part, width), low),
            dma((2,)),
            dma((2,)),
            pltpu.VMEM((2 * size, wide), low),
            pltpu.VMEM((across - 1, 2 * size, wide), low),
            pltpu.VMEM((2, size, wide), low),
            pltpu.VMEM((2, size, wide), low),
            dma((across,)),
            dma((2,)),
            dma((2,)),
        ]
    return pl.pallas_call(
        functools.partial(scatter_kernel, plan, len(lefts), axes, turned, last),
        in_specs=in_specs,
        out_specs=out_specs,
        out_shape=out_shape,
        scratch_shapes=scratch,
        cost_estimate=pl.CostEstimate(
            flops=2 * rows * plan.rows * depth * width,
            bytes_accessed=20 * rows * plan.rows * width,
            transcendentals=0,
        ),
        compiler_params=pltpu.CompilerParams(
            collective_id=collective_id, has_side_effects=True, vmem_limit_bytes=58 * 2**20
        ),
    )(*lefts, weight, *grads, *([residual] if last else []))


def full(rows, width):
    return pl.BlockSpec((rows, width), lambda *_: (0, 0))


def turn(values, cosine, sine):
    return values * cosine + pltpu.roll(values, values.shape[-1] // 2, 1) * sine


def column(row_vector, width):
    return jnp.transpose(jnp.broadcast_to(row_vector, (width, row_vector.shape[1])))


def prepare_kernel(
    head_size, proj, query_inv, key_inv, cosine, sine, query_gain, key_gain, query, key, value
):
    width = query.shape[1]
    turns = (cosine[...], sine[...])
    for source, inv, gain, target in (
        (0, query_inv, query_gain, query),
        (width, key_inv, key_gain, key),
    ):
        factor = column(inv[...], head_size)
        for start in range(0, width, head_size):
            part = proj[:, source + start : source + start + head_size]
            scaled = part * factor * gain[:, start : start + head_size]
            target[:, start : start + head_size] = turn(scaled, *turns).astype(target.dtype)
    value[...] = proj[:, 2 * width :].astype(value.dtype)


def prepare(proj, query_inv, key_inv, cosine, sine, query_gain, key_gain, head_size):
    seq_len, width = proj.shape[0], proj.shape[1] // 3
    rows = min(512, seq_len)
    return pl.pallas_call(
        functools.partial(prepare_kernel, head_size),
        grid=(seq_len // rows,),
        in_specs=[
            pl.BlockSpec((rows, 3 * width), lambda i: (i, 0)),
            pl.BlockSpec((1, rows), lambda i: (0, i)),
            pl.BlockSpec((1, rows), lambda i: (0, i)),
            pl.BlockSpec((rows, head_size), lambda i: (i, 0)),
            pl.BlockSpec((rows, head_size), lambda i: (i, 0)),
            full(1, width),
            full(1, width),
        ],
        out_specs=[pl.BlockSpec((rows, width), lambda i: (i, 0))] * 3,
        out_shape=[jax.ShapeDtypeStruct((seq_len, width), jnp.bfloat16)] * 3,
        cost_estimate=pl.CostEstimate(
            flops=10 * seq_len * width, bytes_accessed=seq_len * width * 20, transcendentals=0
        ),
        compiler_params=pltpu.CompilerParams(vmem_limit_bytes=40 * 2**20),
    )(proj, query_inv, key_inv, cosine, sine, query_gain, key_gain)


def allowed(first, key_block, query_block, key_rows, query_rows):
    key_index = key_block * key_rows + lax.broadcasted_iota(
        jnp.int32, (key_rows, query_rows), 0
    )
    query_index = query_block * query_rows + lax.broadcasted_iota(
        jnp.int32, (key_rows, query_rows), 1
    )
    return (key_index <= query_index) & (key_index >= first)


def attend_kernel(rows, low, first, query, key, value, *refs):
    out, log_sum = refs[-2:]
    step = pl.program_id(1)
    head_size = query.shape[1]
    factor = LOG2E * head_size**-0.5
    queries = query[...]
    starts = first[...]

    def one(index, carry):
        top, total, acc = carry
        at = pl.ds(pl.multiple_of(index * rows, rows), rows)
        scores = contract_cols(key[at, :], queries) * factor
        scores = jnp.where(allowed(starts, index, step, rows, rows), scores, MASKED)
        new_top = jnp.maximum(top, jnp.max(scores, axis=0, keepdims=True))
        probs = jnp.exp2(scores - new_top)
        fade = jnp.exp2(top - new_top)
        total = total * fade + jnp.sum(probs, axis=0, keepdims=True)
        acc = acc * fade + contract_rows(value[at, :], probs.astype(jnp.bfloat16))
        return new_top, total, acc

    top, total, acc = lax.fori_loop(
        low[step],
        step + 1,
        one,
        (
            jnp.full((1, rows), MASKED, jnp.float32),
            jnp.zeros((1, rows), jnp.float32),
            jnp.zeros((head_size, rows), jnp.float32),
        ),
    )
    out[...] = jnp.transpose(acc / total).astype(out.dtype)
    log_sum[0] = top + jnp.log2(total)


def attend(low, first, query, key, value, head_size, rows, more):
    seq_len, width = query.shape
    heads = width // head_size
    whole = pl.BlockSpec((seq_len, head_size), lambda h, i, *_: (0, h))
    block = pl.BlockSpec((rows, head_size), lambda h, i, *_: (i, h))
    return pl.pallas_call(
        functools.partial(attend_kernel, rows),
        grid_spec=pltpu.PrefetchScalarGridSpec(
            num_scalar_prefetch=1,
            grid=(heads, seq_len // rows),
            in_specs=[
                pl.BlockSpec((1, rows), lambda h, i, *_: (0, i)),
                block,
                whole,
                whole,
            ]
            + [pl.BlockSpec(memory_space=pl.ANY)] * len(more),
            out_specs=[block, pl.BlockSpec((1, 1, rows), lambda h, i, *_: (h, 0, i))],
        ),
        out_shape=[
            jax.ShapeDtypeStruct((seq_len, width), jnp.bfloat16),
            jax.ShapeDtypeStruct((heads, 1, seq_len), jnp.float32),
        ],
        cost_estimate=pl.CostEstimate(
            flops=seq_len * seq_len * width, bytes_accessed=seq_len * width * 8, transcendentals=0
        ),
        compiler_params=pltpu.CompilerParams(vmem_limit_bytes=40 * 2**20),
    )(low, first, query, key, value, *more)


def attend_back_kernel(
    rows,
    high,
    first,
    query,
    key,
    value,
    out,
    out_grad,
    log_sum,
    query_grad,
    key_grad,
    value_grad,
    delta,
):
    step = pl.program_id(1)
    seq_len, head_size = query.shape
    factor = LOG2E * head_size**-0.5

    @pl.when(step == 0)
    def _():
        query_grad[...] = jnp.zeros_like(query_grad)

        @pl.loop(0, seq_len // rows)
        def _(index):
            at = pl.ds(pl.multiple_of(index * rows, rows), rows)
            product = out_grad[at, :].astype(jnp.float32) * out[at, :].astype(jnp.float32)
            delta[:, at] = jnp.sum(jnp.transpose(product), axis=0, keepdims=True)

    keys = key[...]
    values = value[...]

    def one(index, carry):
        key_acc, value_acc = carry
        at = pl.ds(pl.multiple_of(index * rows, rows), rows)
        queries = query[at, :]
        grads = out_grad[at, :]
        scores = contract_cols(keys, queries) * factor
        mask = allowed(first[:, at], step, index, rows, rows)
        probs = jnp.exp2(jnp.where(mask, scores - log_sum[0, :, at], MASKED))
        value_acc = value_acc + jnp.dot(
            probs.astype(jnp.bfloat16), grads, preferred_element_type=jnp.float32
        )
        prob_grad = contract_cols(values, grads)
        score_grad = (probs * (prob_grad - delta[:, at])).astype(jnp.bfloat16)
        key_acc = key_acc + jnp.dot(score_grad, queries, preferred_element_type=jnp.float32)
        query_grad[at, :] += contract_rows(score_grad, keys)
        return key_acc, value_acc

    zeros = jnp.zeros((rows, head_size), jnp.float32)
    key_acc, value_acc = lax.fori_loop(step, high[step] + 1, one, (zeros, zeros))
    key_grad[...] = key_acc
    value_grad[...] = value_acc.astype(value_grad.dtype)


def attend_back(high, first, query, key, value, out, out_grad, log_sum, head_size, rows):
    seq_len, width = query.shape
    heads = width // head_size
    whole = pl.BlockSpec((seq_len, head_size), lambda h, j, *_: (0, h))
    block = pl.BlockSpec((rows, head_size), lambda h, j, *_: (j, h))
    return pl.pallas_call(
        functools.partial(attend_back_kernel, rows),
        grid_spec=pltpu.PrefetchScalarGridSpec(
            num_scalar_prefetch=1,
            grid=(heads, seq_len // rows),
            in_specs=[
                full(1, seq_len),
                whole,
                block,
                block,
                whole,
                whole,
                pl.BlockSpec((1, 1, seq_len), lambda h, j, *_: (h, 0, 0)),
            ],
            out_specs=[whole, block, block],
            scratch_shapes=[pltpu.VMEM((1, seq_len), jnp.float32)],
        ),
        out_shape=[
            jax.ShapeDtypeStruct((seq_len, width), jnp.float32),
            jax.ShapeDtypeStruct((seq_len, width), jnp.float32),
            jax.ShapeDtypeStruct((seq_len, width), jnp.bfloat16),
        ],
        cost_estimate=pl.CostEstimate(
            flops=3 * seq_len * seq_len * width,
            bytes_accessed=seq_len * width * 20,
            transcendentals=0,
        ),
        compiler_params=pltpu.CompilerParams(vmem_limit_bytes=48 * 2**20),
    )(high, first, query, key, value, out, out_grad, log_sum)


def norm_back_kernel(
    head_size,
    proj,
    query_inv,
    key_inv,
    cosine,
    sine,
    query_gain,
    key_gain,
    query_grad,
    key_grad,
    dots,
    gain_sums,
):
    width = query_grad.shape[1]
    turns = (cosine[...], -sine[...])
    scale = head_size**-0.5

    @pl.when(pl.program_id(0) == 0)
    def _():
        gain_sums[...] = jnp.zeros_like(gain_sums)

    for place, (source, inv, gain, grad) in enumerate(
        ((0, query_inv, query_gain, query_grad), (width, key_inv, key_gain, key_grad))
    ):
        factor = column(inv[...], head_size)
        row_part = None
        for start in range(0, width, head_size):
            cols = slice(start, start + head_size)
            hat = proj[:, source + start : source + start + head_size] * factor
            product = turn(grad[:, cols] * scale, *turns) * hat
            gain_sums[place : place + 1, cols] += jnp.sum(product, axis=0, keepdims=True)
            product = product * gain[:, cols]
            row_part = product if row_part is None else row_part + product
        dots[place : place + 1, :] = jnp.sum(jnp.transpose(row_part), axis=0, keepdims=True)


def norm_back(
    proj, query_inv, key_inv, cosine, sine, query_gain, key_gain, query_grad, key_grad, head_size
):
    seq_len, width = query_grad.shape
    rows = min(512, seq_len)
    wide = pl.BlockSpec((rows, width), lambda i: (i, 0))
    return pl.pallas_call(
        functools.partial(norm_back_kernel, head_size),
        grid=(seq_len // rows,),
        in_specs=[
            pl.BlockSpec((rows, 2 * width), lambda i: (i, 0)),
            pl.BlockSpec((1, rows), lambda i: (0, i)),
            pl.BlockSpec((1, rows), lambda i: (0, i)),
            pl.BlockSpec((rows, head_size), lambda i: (i, 0)),
            pl.BlockSpec((rows, head_size), lambda i: (i, 0)),
            full(1, width),
            full(1, width),
            wide,
            wide,
        ],
        out_specs=[pl.BlockSpec((2, rows), lambda i: (0, i)), full(2, width)],
        out_shape=[
            jax.ShapeDtypeStruct((2, seq_len), jnp.float32),
            jax.ShapeDtypeStruct((2, width), jnp.float32),
        ],
        cost_estimate=pl.CostEstimate(
            flops=20 * seq_len * width, bytes_accessed=seq_len * width * 20, transcendentals=0
        ),
        compiler_params=pltpu.CompilerParams(vmem_limit_bytes=40 * 2**20),
    )(proj, query_inv, key_inv, cosine, sine, query_gain, key_gain, query_grad, key_grad)


def proj_back_kernel(
    head_size,
    features,
    proj,
    query_inv,
    key_inv,
    cosine,
    sine,
    query_gain,
    key_gain,
    query_grad,
    key_grad,
    value_grad,
    dots,
    *rest,
):
    out = rest[-1]
    width = query_grad.shape[1]
    turns = (cosine[...], -sine[...])
    scale = head_size**-0.5
    for place, (source, inv, gain, grad) in enumerate(
        ((0, query_inv, query_gain, query_grad), (width, key_inv, key_gain, key_grad))
    ):
        factor = column(inv[...], head_size)
        mean = column(dots[place : place + 1, :] * (1.0 / features), head_size)
        for start in range(0, width, head_size):
            cols = slice(start, start + head_size)
            at = slice(source + start, source + start + head_size)
            hat = proj[:, at] * factor
            scaled = turn(grad[:, cols] * scale, *turns) * gain[:, cols]
            out[:, at] = (factor * (scaled - hat * mean)).astype(out.dtype)
    out[:, 2 * width :] = value_grad[...]


def proj_back(
    proj,
    query_inv,
    key_inv,
    cosine,
    sine,
    query_gain,
    key_gain,
    query_grad,
    key_grad,
    value_grad,
    dots,
    head_size,
    features,
    more,
):
    seq_len, width = query_grad.shape
    rows = min(512, seq_len)
    wide = pl.BlockSpec((rows, width), lambda i: (i, 0))
    return pl.pallas_call(
        functools.partial(proj_back_kernel, head_size, features),
        grid=(seq_len // rows,),
        in_specs=[
            pl.BlockSpec((rows, 2 * width), lambda i: (i, 0)),
            pl.BlockSpec((1, rows), lambda i: (0, i)),
            pl.BlockSpec((1, rows), lambda i: (0, i)),
            pl.BlockSpec((rows, head_size), lambda i: (i, 0)),
            pl.BlockSpec((rows, head_size), lambda i: (i, 0)),
            full(1, width),
            full(1, width),
            wide,
            wide,
            wide,
            pl.BlockSpec((2, rows), lambda i: (0, i)),
        ]
        + [pl.BlockSpec(memory_space=pl.ANY)] * len(more),
        out_specs=pl.BlockSpec((rows, 3 * width), lambda i: (i, 0)),
        out_shape=jax.ShapeDtypeStruct((seq_len, 3 * width), jnp.bfloat16),
        cost_estimate=pl.CostEstimate(
            flops=20 * seq_len * width, bytes_accessed=seq_len * width * 24, transcendentals=0
        ),
        compiler_params=pltpu.CompilerParams(vmem_limit_bytes=40 * 2**20),
    )(
        proj,
        query_inv,
        key_inv,
        cosine,
        sine,
        query_gain,
        key_gain,
        query_grad,
        key_grad,
        value_grad,
        dots,
        *more,
    )


def body(
    plan,
    layer_input,
    segments,
    w_query,
    w_key,
    w_value,
    w_out,
    query_gain,
    key_gain,
    attn_gain,
    w_gate,
    w_up,
    w_down,
    mlp_gain,
    cotangent,
):
    rows = plan.rows
    mine = plan.block()
    model_width = layer_input.shape[1]
    head_size = model_width // HEADS
    seq_len = segments.shape[0]
    own_tokens = seq_len // rows
    part = own_tokens // 2
    f32 = jnp.float32
    bf16 = jnp.bfloat16
    chunks = range(2)

    def chunk_of(value, k):
        return value[k * part : (k + 1) * part]

    qkv_own = jnp.concatenate([w_query, w_key, w_value], axis=1)
    own_depth, wide = qkv_own.shape
    small_own = jnp.concatenate([query_gain, key_gain, attn_gain, mlp_gain])
    gain_size, post_size = query_gain.shape[0], attn_gain.shape[0]
    cuts = (gain_size, 2 * gain_size, 2 * gain_size + post_size)
    small_size = small_own.shape[0]
    extra = 16

    def lines(vector):
        return jnp.pad(vector, (0, extra * wide - small_size)).reshape(extra, wide)

    own_weight = jnp.concatenate([qkv_own, lines(small_own)], axis=0)
    gathered_x, both = swap_gather(plan, layer_input, own_weight, 1)
    both = both.reshape(plan.cols, own_depth + extra, wide)
    proj_weight = both[:, :own_depth].reshape(-1, wide)
    small = both[:, own_depth:].reshape(plan.cols, extra * wide)[:, :small_size].astype(f32)
    query_scale, key_scale, attn_scale, mlp_scale = (
        value.reshape(1, -1) for value in jnp.split(small, cuts, axis=1)
    )

    own_x = lax.dynamic_slice_in_dim(gathered_x, mine * own_tokens, own_tokens)
    segments = plan.swap(segments)
    gate_pair = plan.weight_pair(after(w_gate, gathered_x))
    out_pair = plan.weight_pair(after(w_out, gathered_x))
    up_pair = plan.weight_pair(after(w_up, gathered_x))
    down_pair = plan.weight_pair(after(w_down, gathered_x))
    ff_width = w_gate.shape[1]

    local_width = wide // 3
    token_index = jnp.arange(seq_len, dtype=jnp.int32)
    change = jnp.concatenate([jnp.ones((1,), dtype=bool), segments[1:] != segments[:-1]])
    first = lax.cummax(jnp.where(change, token_index, 0), axis=0)
    places = (token_index - first).astype(f32)
    lane = jnp.arange(head_size, dtype=jnp.int32)
    half = head_size // 2
    freqs = THETA ** (-((lane % half).astype(f32) * 2.0) / head_size)
    angle = places[:, None] * freqs[None, :]
    cosine = jnp.cos(angle)
    sine = jnp.sin(angle) * jnp.where(lane < half, -1.0, 1.0)[None, :]
    tile = min(512, seq_len)
    low = first[::tile] // tile
    last = token_index[tile - 1 :: tile]
    ends = jnp.min(
        jnp.where(change[None, :] & (token_index[None, :] > last[:, None]), token_index, seq_len),
        axis=1,
    )
    high = (ends - 1) // tile
    first_row = first[None, :]

    proj = jnp.dot(gathered_x, proj_weight, preferred_element_type=f32)
    squares = jnp.stack(
        [
            jnp.sum(proj[:, start : start + local_width] ** 2, axis=-1)
            for start in (0, local_width)
        ]
    )
    invs = lax.rsqrt(plan.token_sum(squares) / model_width + EPS)
    query_inv, key_inv = invs[:1], invs[1:]
    query, key, value = prepare(
        proj, query_inv, key_inv, cosine, sine, query_scale, key_scale, head_size
    )
    attn_out, log_sum = attend(
        low, first_row, query, key, value, head_size, tile, (*gate_pair, *out_pair)
    )
    post_depth = w_out.shape[1]
    out_full = plan.token_gather(
        join(
            (local_width, model_width),
            [(0, c * post_depth, piece) for c, piece in plan.weight_pieces(out_pair)],
        )
    )
    own_cot = plan.swap(after(cotangent, attn_out))

    attn_tokens = jnp.zeros((own_tokens, model_width), bf16)
    for flip in range(rows):
        other = mine ^ flip
        piece = lax.dynamic_slice(attn_out, (other * own_tokens, 0), (own_tokens, local_width))
        if flip:
            piece = plan.partner(piece, flip)
        attn_tokens = lax.dynamic_update_slice(attn_tokens, piece, (0, other * local_width))

    attn_tokens, *up_pair = lax.optimization_barrier((attn_tokens, *up_pair))
    gate_pieces = plan.weight_pieces(gate_pair)
    places, gate_pieces = zip(*gate_pieces, strict=True)
    attn_tokens, *gate_pieces = lax.optimization_barrier((attn_tokens, *gate_pieces))
    gate_pieces = list(zip(places, gate_pieces, strict=True))
    ff_weight = join(
        (model_width, 2 * ff_width),
        [
            (c * own_depth, start, piece)
            for start, pieces in ((0, gate_pieces), (ff_width, plan.weight_pieces(up_pair)))
            for c, piece in pieces
        ],
    )
    down_rows = join(
        (ff_width, model_width),
        [(0, c * post_depth, piece) for c, piece in plan.weight_pieces(down_pair)],
    )

    def normed(value):
        inv = lax.rsqrt(jnp.mean(value * value, axis=-1, keepdims=True) + EPS)
        return inv, value * inv

    def norm_grad(inv, hat, scaled):
        mean = jnp.mean(scaled * hat, axis=-1, keepdims=True)
        return (inv * (scaled - hat * mean)).astype(bf16)

    attn_inv, attn_hat, hidden, gathered_h = [], [], [], []
    for k in chunks:
        out_proj = jnp.dot(chunk_of(attn_tokens, k), out_full, preferred_element_type=f32)
        inv, hat = normed(out_proj)
        attn_inv.append(inv)
        attn_hat.append(hat)
        hidden.append(chunk_of(own_x, k).astype(f32) + hat * attn_scale)
        gathered_h.append(plan.token_gather(hidden[k].astype(bf16)))

    gate, up, activated = [], [], []
    for k in chunks:
        both = jnp.dot(gathered_h[k], ff_weight, preferred_element_type=f32).astype(bf16)
        gate.append(both[:, :ff_width])
        up.append(both[:, ff_width:])
        activated.append((jax.nn.silu(gate[k].astype(f32)) * up[k].astype(f32)).astype(bf16))
    (mlp_out,) = multiply_scatter(plan, activated, down_rows, False, 2)

    outputs, upstream, shard_rows = [], [], []
    mlp_gain_part = 0.0
    for k in chunks:
        inv, hat = normed(chunk_of(mlp_out, k))
        outputs.append((hidden[k] + hat * mlp_scale).astype(bf16))
        upstream.append(chunk_of(own_cot, k).astype(f32))
        mlp_gain_part += jnp.sum(upstream[k] * hat, axis=0)
        shard_rows.append(plan.token_gather(norm_grad(inv, hat, upstream[k] * mlp_scale)))
    layer_output = plan.swap(jnp.concatenate(outputs))

    ff_grad = []
    for k in chunks:
        act_part = contract_cols(shard_rows[k], down_rows)
        gate_val, up_val = gate[k].astype(f32), up[k].astype(f32)
        gate_sigmoid = jax.nn.sigmoid(gate_val)
        gate_grad = act_part * up_val * gate_sigmoid * (1.0 + gate_val * (1.0 - gate_sigmoid))
        up_grad = act_part * gate_val * gate_sigmoid
        ff_grad.append(jnp.concatenate([gate_grad, up_grad], axis=1).astype(bf16))
    down_grad = sum(contract_rows(activated[k], shard_rows[k]) for k in chunks).astype(bf16)
    ff_weight_grad = sum(contract_rows(gathered_h[k], ff_grad[k]) for k in chunks).astype(bf16)
    hidden_grad_mlp, down_blocks, ff_blocks = multiply_scatter(
        plan, ff_grad, ff_weight, True, 3, (down_grad, ff_weight_grad), (1, 0)
    )
    hidden_grad = [upstream[k] + chunk_of(hidden_grad_mlp, k) for k in chunks]
    ff_sum = plan.weight_send(plan.weight_sum(ff_weight_grad, ff_blocks, 0), 0)
    down_sum = plan.weight_send(plan.weight_sum(down_grad, down_blocks, 1), 1)

    attn_gain_part = 0.0
    proj_grads, token_grads = [], []
    for k in chunks:
        attn_gain_part += jnp.sum(hidden_grad[k] * attn_hat[k], axis=0)
        proj_grads.append(norm_grad(attn_inv[k], attn_hat[k], hidden_grad[k] * attn_scale))
        token_grads.append(contract_cols(proj_grads[k], out_full).astype(bf16))
    out_token_grad = jnp.concatenate(token_grads)

    attn_grad = jnp.zeros((seq_len, local_width), bf16)
    for flip in range(rows):
        other = mine ^ flip
        piece = lax.dynamic_slice(
            out_token_grad, (0, other * local_width), (own_tokens, local_width)
        )
        if flip:
            piece = plan.partner(piece, flip)
        attn_grad = lax.dynamic_update_slice(attn_grad, piece, (other * own_tokens, 0))

    out_grad = sum(
        contract_rows(
            attn_out.reshape(rows, 2, part, local_width)[:, k].reshape(-1, local_width),
            plan.token_gather(after(proj_grads[k], attn_grad)),
        )
        for k in chunks
    ).astype(bf16)
    out_sum = plan.weight_sum(out_grad, plan.weight_exchange(out_grad, 1), 1)
    query_grad, key_grad, value_grad = attend_back(
        high, first_row, query, key, value, attn_out, attn_grad, log_sum, head_size, tile
    )
    shared = (proj, query_inv, key_inv, cosine, sine, query_scale, key_scale, query_grad, key_grad)
    dots, gain_sums = norm_back(*shared, head_size)
    dots = plan.token_sum(dots)
    proj_grad_all = proj_back(
        *shared, value_grad, dots, head_size, model_width, (ff_sum, down_sum)
    )
    proj_grad_all = after(proj_grad_all, out_sum)
    proj_weight_grad = contract_rows(gathered_x, proj_grad_all).astype(bf16)
    post_sums = plan.token_sum(jnp.stack([attn_gain_part, mlp_gain_part]))
    small = jnp.concatenate(
        [
            gain_sums[0].reshape(plan.cols, -1),
            gain_sums[1].reshape(plan.cols, -1),
            post_sums[0].reshape(plan.cols, -1),
            post_sums[1].reshape(plan.cols, -1),
        ],
        axis=1,
    )
    small = jnp.pad(small, ((0, 0), (0, extra * wide - small_size)))
    small = small.reshape(plan.cols, extra, wide).astype(bf16)
    stacked = jnp.concatenate(
        [proj_weight_grad.reshape(plan.cols, own_depth, wide), small], axis=1
    )
    stacked = stacked.reshape(-1, wide)
    out_sum = plan.weight_send(out_sum, 1)
    stacked = after(stacked, out_sum)
    input_grad, _, proj_sum = multiply_scatter(
        plan,
        [proj_grad_all],
        proj_weight,
        True,
        4,
        (stacked,),
        (0,),
        jnp.concatenate(hidden_grad),
    )
    small = proj_sum[own_depth:].reshape(-1)[:small_size]
    query_gain_sum, key_gain_sum, attn_gain_sum, mlp_gain_sum = jnp.split(small, cuts)
    proj_sum = proj_sum[:own_depth]
    own_ff = w_gate.shape[1]
    return (
        layer_output,
        input_grad,
        proj_sum[:, :local_width],
        proj_sum[:, local_width : 2 * local_width],
        proj_sum[:, 2 * local_width :],
        out_sum,
        query_gain_sum,
        key_gain_sum,
        attn_gain_sum,
        ff_sum[:, :own_ff],
        ff_sum[:, own_ff:],
        down_sum,
        mlp_gain_sum,
    )


def solution(mesh):
    tokens = P(("col", "row"), None)
    columns = P("col", "row")
    across = P("row", "col")
    vector = P(("row", "col"))
    return jax.shard_map(
        functools.partial(body, Plan(mesh)),
        mesh=mesh,
        in_specs=(
            tokens,
            P("col"),
            columns,
            columns,
            columns,
            across,
            vector,
            vector,
            P("col"),
            columns,
            columns,
            across,
            P("col"),
            tokens,
        ),
        out_specs=(
            tokens,
            tokens,
            columns,
            columns,
            columns,
            across,
            vector,
            vector,
            P("col"),
            columns,
            columns,
            across,
            P("col"),
        ),
        check_vma=False,
    )
```

time: 2680 us -> 1590 us (0.59)
  waiting for transfers between devices: 1730 us -> 364 us
  Pallas kernels: 0 us -> 676 us
  matrix products: 504 us -> 237 us
  other arithmetic: 215 us -> 109 us
  blocking collectives: 90.6 us -> 0 us
  starting transfers between devices: 9 us -> 93.3 us
    reduce_scatter x11 -> x0, waiting for transfers between devices: 915 us -> none  [the longest x1 285 us: body(): lax.psum_scatter(contract_cols(proj_grad_all, proj_weight).astype(jnp.bfl...]
    pallas_call x0 -> x9, Pallas kernels: none -> 676 us  [the longest x3 413 us: multiply_scatter(): pl.pallas_call(functools.partial(scatter_kernel, plan, len(lefts), axes,...]
    all_gather x11 -> x7, waiting for transfers between devices: 708 us -> 67.8 us  [token_gather(): lax.all_gather(value, BOTH, axis=0, tiled=True, axis_index_groups=self.to...]
    ppermute x0 -> x49, waiting for transfers between devices: none -> 294 us  [send(): return lax.ppermute(value, BOTH, pairs)]
    dot_general x52 -> x5, matrix products: 305 us -> 74.6 us  [the longest x2 44.7 us: body(): jnp.dot(gathered_h[k], ff_weight, preferred_element_type=f32).astype(bf16)]
    all_to_all x2 -> x0, waiting for transfers between devices: 98.4 us -> none  [the longest x1 68.3 us: body(): lax.all_to_all(out_token_grad, 'row', split_axis=1, concat_axis=0, tiled=...]
    ppermute x0 -> x49, starting transfers between devices: none -> 93 us  [send(): return lax.ppermute(value, BOTH, pairs)]
    convert_element_type x26 -> x10, other arithmetic: 100 us -> 25.3 us  [the longest x2 7.98 us: body(): (jax.nn.silu(gate[k].astype(f32)) * up[k].astype(f32)).astype(bf16)]
  transfers between devices with their start and end apart: 24 -> 56, of which waited for: 13 -> 24; matrix products, arithmetic and copies ran while one was open for 25% -> 14% of each run, Pallas kernels for 0% -> 7%
where the time goes in v1:
time: 1590 us; the launch traced here: 1580 us
  Pallas kernels  676 us (43%)
  waiting for transfers between devices  364 us (23%)
  matrix products  237 us (15%)
  other arithmetic  109 us (7%)
  starting transfers between devices  93.3 us (6%)
  local copies, waits for them, and re-layouts  80.3 us (5%)
  between operations  16.1 us (1%)
    pallas_call x3, Pallas kernels, multiply_scatter(): pl.pallas_call(functools.partial(scatter_kernel, plan, len(lefts), axes,...  413 us
    ppermute x49, waiting for transfers between devices, send(): return lax.ppermute(value, BOTH, pairs)  294 us
    pallas_call x1, Pallas kernels, swap_gather(): pl.pallas_call(functools.partial(gather_kernel, plan), in_specs=[anywhere...  153 us
    dot_general x7, matrix products, contract_rows(): lax.dot_general(left, right, (((0,), (0,)), ((), ())), preferred_element_...  108 us
    ppermute x49, starting transfers between devices, send(): return lax.ppermute(value, BOTH, pairs)  93 us
    all_gather x7, waiting for transfers between devices, token_gather(): lax.all_gather(value, BOTH, axis=0, tiled=True, axis_index_groups=self.to...  67.8 us
    dot_general x4, matrix products, contract_cols(): lax.dot_general(left, right, (((1,), (1,)), ((), ())), preferred_element_...  54.1 us
    pallas_call x1, Pallas kernels, attend_back(): pl.pallas_call(functools.partial(attend_back_kernel, rows), grid_spec=plt...  49.2 us
  transfers between devices with their start and end apart: 56, of which 24 were waited for; matrix products, arithmetic and copies ran while one was open for 14% of the time, Pallas kernels for 7%

profile of v1, /device:TPU:1, one launch (start us, length us, event | category | flops | bytes accessed | tf_op | source)
XLA Modules:
  0.0 1575.5 jit_solution(4768800077651111790)
XLA Ops:
  12.2 153.2 %shard_map.237 = (bf16[4096,2048]{1,0:T(8,128)(2,1)}, bf16[2112,768]{1,0:T(8,128)(2,1)}) custom-call(bf16[512,2048]{1,0:T(8,128)(2,1)} %own.1, bf16[528,768]{1,0:T(8,128)(2,1)} %pad_maximum_fusion.5.weight), custom_call_target="tpu_custom_call" | custom-call | bytes 167772160 | tf_op jit(solution)/shard_map/pallas_call | solution.py:325
  165.6 8.1 collective-permute-start.7
  203.3 21.1 %fusion.69 = f32[4096,768]{0,1:T(8,128)} fusion(bf16[4096,2048]{1,0:T(8,128)(2,1)} %get-tuple-element.47, bf16[2048,768]{1,0:T(8,128)(2,1)} %bitcast.72), kind=kOutput, calls=%fused_computation.238 | convolution fusion | flops 12884901888 | bytes 32505856 | tf_op jit(solution)/shard_map/dot_general | solution.py:1151
  229.4 12.7 copy.45.proj
  242.3 40.7 %collective-permute-done = s32[4096]{0:T(1024)S(1)} collective-permute-done((s32[4096]{0:T(1024)S(1)}, s32[4096]{0:T(1024)S(1)}, u32[]{:S(2)}, u32[]{:S(2)}) %collective-permute-start) | collective-permute-done | bytes 16416 | tf_op jit(solution)/shard_map/ppermute | solution.py:60
  282.9 10.8 collective-permute-start.1
  295.6 10.0 fusion.35
  309.5 8.9 shard_map.238
  323.6 31.6 %shard_map.239 = (bf16[4096,256]{1,0:T(8,128)(2,1)S(1)}, f32[2,1,4096]{2,1,0:T(1,128)S(1)}) custom-call(s32[8]{0:T(128)S(1)} %and_select_fusion.2.low, s32[1,4096]{1,0:T(1,128)S(1)} %bitcast.65, bf16[4096,256]{1,0:T(8,128)(2,1)S(1)} %get-tuple-element.49.query, bf16[4096,256]{1,0:T(8,128)(2,1)S(1)} %get-tuple-element.50.key, ...), custom_call_target="tpu_custom_call" | custom-call | flops 4294967296 | bytes 8388608 | tf_op jit(solution)/shard_map/pallas_call | solution.py:794
  361.6 9.0 collective-permute-done.8
  388.7 6.3 multiply_reduce_fusion.6
  403.6 5.1 collective-permute-start.24
  410.6 44.0 %collective-permute-done.23 = bf16[1024,512]{1,0:T(8,128)(2,1)S(1)} collective-permute-done((bf16[1024,512]{1,0:T(8,128)(2,1)}, bf16[1024,512]{1,0:T(8,128)(2,1)S(1)}, u32[]{:S(2)}, u32[]{:S(2)}) %collective-permute-start.23) | collective-permute-done | bytes 1048608 | tf_op jit(solution)/shard_map/ppermute | solution.py:60
  474.8 8.7 collective-permute-done.25
  484.7 21.4 %collective-permute-done.26 = bf16[1024,512]{1,0:T(8,128)(2,1)S(1)} collective-permute-done((bf16[1024,512]{1,0:T(8,128)(2,1)S(1)}, bf16[1024,512]{1,0:T(8,128)(2,1)S(1)}, u32[]{:S(2)}, u32[]{:S(2)}) %collective-permute-start.26) | collective-permute-done | bytes 1048608 | tf_op jit(solution)/shard_map/ppermute | solution.py:60
  507.2 21.4 %collective-permute-done.21 = bf16[512,1024]{1,0:T(8,128)(2,1)S(1)} collective-permute-done((bf16[512,1024]{1,0:T(8,128)(2,1)S(1)}, bf16[512,1024]{1,0:T(8,128)(2,1)S(1)}, u32[]{:S(2)}, u32[]{:S(2)}) %collective-permute-start.21) | collective-permute-done | bytes 1048608 | tf_op jit(solution)/shard_map/ppermute | solution.py:60
  529.8 10.2 collective-permute-done.22
  542.6 22.6 %convolution_convert_fusion.1 = bf16[2048,2048]{1,0:T(8,128)(2,1)S(1)} fusion(bf16[2048,2048]{1,0:T(8,128)(2,1)} %all-gather.10.cloned.1.call-done, bf16[2048,2048]{1,0:T(8,128)(2,1)} %constant_dynamic-update-slice_fusion.26.refs_2_), kind=kOutput, calls=%fused_computation.39 | convolution fusion | flops 17184063488 | bytes 25165824 | tf_op jit(solution)/shard_map/dot_general | solution.py:1220
  572.5 22.2 %convolution_convert_fusion = bf16[2048,2048]{1,0:T(8,128)(2,1)S(1)} fusion(bf16[2048,2048]{1,0:T(8,128)(2,1)} %all-gather.12.cloned.1.call-done, bf16[2048,2048]{1,0:T(8,128)(2,1)} %constant_dynamic-update-slice_fusion.26.refs_2_), kind=kOutput, calls=%fused_computation.38 | convolution fusion | flops 17184063488 | bytes 25165824 | tf_op jit(solution)/shard_map/dot_general | solution.py:1220
  601.9 109.3 %shard_map.240 = f32[512,2048]{1,0:T(8,128)} custom-call(bf16[2048,1024]{1,0:T(8,128)(2,1)} %fusion.refs_0_, bf16[2048,1024]{1,0:T(8,128)(2,1)} %fusion.4.refs_1_, bf16[1024,2048]{1,0:T(8,128)(2,1)} %constant_dynamic-update-slice_fusion.7.refs_2_), custom_call_target="tpu_custom_call" | custom-call | flops 17179869184 | bytes 167772160 | tf_op jit(solution)/shard_map/pallas_call | solution.py:675
  722.0 48.5 %all-gather.16.cloned.1.call-done = bf16[2048,2048]{1,0:T(8,128)(2,1)} async-done(((bf16[256,2048]{1,0:T(8,128)(2,1)}), bf16[2048,2048]{1,0:T(8,128)(2,1)}) %all-gather.16.cloned.1.call-update) | async-done | bytes 8388624 | tf_op jit(solution)/shard_map/all_gather | solution.py:77
  770.5 20.7 %fusion.7 = (bf16[2048,1024]{1,0:T(8,128)(2,1)}, bf16[2048,1024]{1,0:T(8,128)(2,1)}) fusion(bf16[2048,2048]{1,0:T(8,128)(2,1)} %copy-done.46, bf16[2048,2048]{1,0:T(8,128)(2,1)} %all-gather.16.cloned.1.call-done, bf16[1024,2048]{1,0:T(8,128)(2,1)} %constant_dynamic-update-slice_fusion.7.refs_2_), kind=kOutput, calls=%fused_computation.20 | convolution fusion | flops 8621391872 | bytes 29360128 | tf_op jit(solution)/shard_map/dot_general | solution.py:165
  791.1 8.5 pad_maximum_fusion.1.refs_1_
  799.6 19.3 %all-gather.14.cloned.1.call-done = bf16[2048,2048]{1,0:T(8,128)(2,1)} async-done(((bf16[256,2048]{1,0:T(8,128)(2,1)}), bf16[2048,2048]{1,0:T(8,128)(2,1)}) %all-gather.14.cloned.1.call-update) | async-done | bytes 8388624 | tf_op jit(solution)/shard_map/all_gather | solution.py:77
  818.9 20.9 %fusion.3 = (bf16[2048,1024]{1,0:T(8,128)(2,1)}, bf16[2048,1024]{1,0:T(8,128)(2,1)}) fusion(bf16[2048,2048]{1,0:T(8,128)(2,1)} %copy-done.45, bf16[2048,2048]{1,0:T(8,128)(2,1)} %all-gather.14.cloned.1.call-done, bf16[1024,2048]{1,0:T(8,128)(2,1)} %constant_dynamic-update-slice_fusion.7.refs_2_), kind=kOutput, calls=%fused_computation.16 | convolution fusion | flops 8621391872 | bytes 29360128 | tf_op jit(solution)/shard_map/dot_general | solution.py:165
  839.8 8.2 pad_maximum_fusion.refs_0_
  848.0 14.7 fusion.70
  862.7 22.6 %fusion.61 = f32[2048,2048]{1,0:T(8,128)} fusion(bf16[2048,2048]{1,0:T(8,128)(2,1)} %all-gather.10.cloned.1.call-done, bf16[2048,1024]{1,0:T(8,128)(2,1)S(1)} %copy-done.58, bf16[2048,1024]{1,0:T(8,128)(2,1)S(1)} %copy-done.57), kind=kOutput, calls=%fused_computation.230 | convolution fusion | flops 17196646400 | bytes 33554432 | tf_op jit(solution)/shard_map/dot_general | solution.py:159
  885.3 14.7 add_convert_fusion.1.refs_3_
  900.0 24.8 %add_convert_fusion.refs_4_ = bf16[2048,2048]{1,0:T(8,128)(2,1)} fusion(f32[2048,2048]{1,0:T(8,128)} %fusion.61, bf16[2048,2048]{1,0:T(8,128)(2,1)} %all-gather.12.cloned.1.call-done, bf16[2048,1024]{1,0:T(8,128)(2,1)S(1)} %copy-done.56, bf16[2048,1024]{1,0:T(8,128)(2,1)S(1)} %copy-done.55), kind=kOutput, calls=%fused_computation | convolution fusion | flops 17205035008 | bytes 41943040 | tf_op jit(solution)/shard_map/dot_general | solution.py:159
  924.8 144.1 %shard_map.241 = (f32[512,2048]{1,0:T(8,128)}, bf16[1,1024,1024]{2,1,0:T(8,128)(2,1)}, bf16[1,1024,2048]{2,1,0:T(8,128)(2,1)}) custom-call(bf16[2048,2048]{1,0:T(8,128)(2,1)} %pad_maximum_fusion.refs_0_, bf16[2048,2048]{1,0:T(8,128)(2,1)} %pad_maximum_fusion.1.refs_1_, bf16[2048,2048]{1,0:T(8,128)(2,1)} %constant_dynamic-update-slice_fusion.26.refs_2_, ...), custom_call_target="tpu_custom_call" | custom-call | flops 34359738368 | bytes 167772160 | tf_op jit(solution)/shard_map/pallas_call | solution.py:675
  1076.3 6.1 convolution_convert_fusion.4
  1082.4 6.4 convolution_convert_fusion.3
  1106.2 7.5 collective-permute-done.33
  1128.2 50.7 %collective-permute-done.27 = bf16[512,2048]{1,0:T(8,128)(2,1)} collective-permute-done((bf16[512,2048]{1,0:T(8,128)(2,1)}, bf16[512,2048]{1,0:T(8,128)(2,1)}, u32[]{:S(2)}, u32[]{:S(2)}) %collective-permute-start.27) | collective-permute-done | bytes 2097184 | tf_op jit(solution)/shard_map/ppermute | solution.py:60
  1198.0 5.9 collective-permute-start.41
  1207.1 5.0 collective-permute-start.39
  1212.1 36.0 %collective-permute-done.45 = f32[2,2048]{1,0:T(2,128)S(1)} collective-permute-done((f32[2,2048]{1,0:T(2,128)S(1)}, f32[2,2048]{1,0:T(2,128)S(1)}, u32[]{:S(2)}, u32[]{:S(2)}) %collective-permute-start.45) | collective-permute-done | bytes 16416 | tf_op jit(solution)/shard_map/ppermute | solution.py:60
  1248.2 49.2 %shard_map.242 = (f32[4096,256]{1,0:T(8,128)}, f32[4096,256]{1,0:T(8,128)}, bf16[4096,256]{1,0:T(8,128)(2,1)S(1)}) custom-call(s32[8]{0:T(128)S(1)} %and_select_fusion.high, s32[1,4096]{1,0:T(1,128)S(1)} %bitcast.66, bf16[4096,256]{1,0:T(8,128)(2,1)S(1)} %copy-done.23, bf16[4096,256]{1,0:T(8,128)(2,1)} %copy-done.24, bf16[4096,256]{1,0:T(8,128)(2,1)} %copy-done.25, ...), custom_call_target="tpu_custom_call" | custom-call | flops 12884901888 | bytes 20971520 | tf_op jit(solution)/shard_map/pallas_call | solution.py:879
  1302.6 8.9 shard_map.243
  1311.6 6.0 collective-permute-start.36
  1321.3 17.4 %collective-permute-done.37 = f32[2,4096]{1,0:T(2,128)S(1)} collective-permute-done((f32[2,4096]{1,0:T(2,128)S(1)}, f32[2,4096]{1,0:T(2,128)S(1)}, u32[]{:S(2)}, u32[]{:S(2)}) %collective-permute-start.37) | collective-permute-done | bytes 32800 | tf_op jit(solution)/shard_map/ppermute | solution.py:60
  1343.9 7.5 fusion.71
  1351.3 6.5 fusion.24
  1358.1 5.6 convert_add_fusion.2.rest_0_
  1364.6 11.7 shard_map.244.refs_0_
  1382.9 17.4 %convolution_convert_fusion.2 = bf16[2048,768]{1,0:T(8,128)(2,1)S(1)} fusion(bf16[4096,2048]{1,0:T(8,128)(2,1)} %get-tuple-element.47, bf16[4096,768]{1,0:T(8,128)(2,1)S(1)} %copy-done.48), kind=kOutput, calls=%fused_computation.64 | convolution fusion | flops 12886474752 | bytes 26214400 | tf_op jit(solution)/shard_map/dot_general | solution.py:159
  1403.1 159.2 %shard_map.245 = (bf16[512,2048]{1,0:T(8,128)(2,1)}, bf16[1,1056,768]{2,1,0:T(8,128)(2,1)}, f32[528,768]{1,0:T(8,128)}) custom-call(bf16[4096,768]{1,0:T(8,128)(2,1)} %shard_map.244.refs_0_, bf16[2048,768]{1,0:T(8,128)(2,1)} %bitcast.73, bf16[2112,768]{1,0:T(8,128)(2,1)} %bitcast.71, f32[512,2048]{1,0:T(8,128)} %pad_maximum_fusion.2.refs_3_), custom_call_target="tpu_custom_call" | custom-call | flops 12884901888 | bytes 167772160 | tf_op jit(solution)/shard_map/pallas_call | solution.py:675
  (402 shorter events, 228.5 us)
Async XLA Ops:
  7.2 381.5 %all-gather.8.cloned.1.call-start = ((), (), s32[]{:S(2)}) async-start(), calls=%async_computation | async-start | bytes 9437184 | tf_op jit(solution)/shard_map/all_gather | solution.py:77
  165.4 10.0 collective-permute-start.6
  165.6 15.2 collective-permute-start.7
  187.2 355.4 %all-gather.10.cloned.1.call-start = ((), (), s32[]{:S(2)}) async-start(), calls=%async_computation.1 | async-start | bytes 9437184 | tf_op jit(solution)/shard_map/all_gather | solution.py:77
  187.3 131.1 %collective-permute-start.5 = (bf16[512,1024]{1,0:T(8,128)(2,1)S(1)}, bf16[512,1024]{1,0:T(8,128)(2,1)}, u32[]{:S(2)}, u32[]{:S(2)}) collective-permute-start(bf16[512,1024]{1,0:T(8,128)(2,1)S(1)} %copy-done.68), channel_id=1, source_target_pairs={{1,16},{3,18},{5,20},{7,22},{9,24},{11,26},{13,28},{15,30},{16,1},... | collective-permute-start | bytes 3145736 | tf_op jit(solution)/shard_map/ppermute | solution.py:60
  191.9 126.6 %collective-permute-start.4 = (bf16[512,1024]{1,0:T(8,128)(2,1)S(1)}, bf16[512,1024]{1,0:T(8,128)(2,1)}, u32[]{:S(2)}, u32[]{:S(2)}) collective-permute-start(bf16[512,1024]{1,0:T(8,128)(2,1)S(1)} %copy-done.68), channel_id=1, source_target_pairs={{0,16},{1,0},{2,18},{3,2},{4,20},{5,4},{6,22},{7,6},{8,24},{9,8},{... | collective-permute-start | bytes 3145736 | tf_op jit(solution)/shard_map/ppermute | solution.py:60
  191.9 166.0 %collective-permute-start.16 = (bf16[512,1024]{1,0:T(8,128)(2,1)}, bf16[512,1024]{1,0:T(8,128)(2,1)}, u32[]{:S(2)}, u32[]{:S(2)}) collective-permute-start(bf16[512,1024]{1,0:T(8,128)(2,1)} %param.24), channel_id=1, source_target_pairs={{1,16},{3,18},{5,20},{7,22},{9,24},{11,26},{13,28},{15,30},{16,1},... | collective-permute-start | bytes 3145736 | tf_op jit(solution)/shard_map/ppermute | solution.py:60
  193.9 164.6 %collective-permute-start.15 = (bf16[512,1024]{1,0:T(8,128)(2,1)}, bf16[512,1024]{1,0:T(8,128)(2,1)}, u32[]{:S(2)}, u32[]{:S(2)}) collective-permute-start(bf16[512,1024]{1,0:T(8,128)(2,1)} %param.24), channel_id=1, source_target_pairs={{0,16},{1,0},{2,18},{3,2},{4,20},{5,4},{6,22},{7,6},{8,24},{9,8},{... | collective-permute-start | bytes 3145736 | tf_op jit(solution)/shard_map/ppermute | solution.py:60
  194.0 88.9 %collective-permute-start = (s32[4096]{0:T(1024)S(1)}, s32[4096]{0:T(1024)S(1)}, u32[]{:S(2)}, u32[]{:S(2)}) collective-permute-start(s32[4096]{0:T(1024)S(1)} %copy-done.82), channel_id=1, source_target_pairs={{1,16},{3,18},{5,20},{7,22},{9,24},{11,26},{13,28},{15,30},{16,1},... | collective-permute-start | bytes 49160 | tf_op jit(solution)/shard_map/ppermute | solution.py:60
  282.9 12.1 collective-permute-start.1
  295.1 10.6 collective-permute-start.2
  322.0 64.4 %collective-permute-start.18 = (bf16[512,1024]{1,0:T(8,128)(2,1)S(1)}, bf16[512,1024]{1,0:T(8,128)(2,1)S(1)}, u32[]{:S(2)}, u32[]{:S(2)}) collective-permute-start(bf16[512,1024]{1,0:T(8,128)(2,1)S(1)} %get-tuple-element.59.refs_1_), channel_id=1, source_target_pairs={{0,2},{1,3},{2,0},{3,1},{4,6},{5,7},{6,4},{7,5},{8,10},{9,11},{10,... | collective-permute-start | bytes 3145736 | tf_op jit(solution)/shard_map/ppermute | solution.py:60
  323.4 65.3 %collective-permute-start.17 = (bf16[512,1024]{1,0:T(8,128)(2,1)S(1)}, bf16[512,1024]{1,0:T(8,128)(2,1)}, u32[]{:S(2)}, u32[]{:S(2)}) collective-permute-start(bf16[512,1024]{1,0:T(8,128)(2,1)S(1)} %get-tuple-element.58.refs_0_), channel_id=1, source_target_pairs={{0,2},{1,3},{2,0},{3,1},{4,6},{5,7},{6,4},{7,5},{8,10},{9,11},{10,... | collective-permute-start | bytes 3145736 | tf_op jit(solution)/shard_map/ppermute | solution.py:60
  355.7 16.8 %collective-permute-start.10 = (bf16[512,256]{1,0:T(8,128)(2,1)S(1)}, bf16[512,256]{1,0:T(8,128)(2,1)S(1)}, u32[]{:S(2)}, u32[]{:S(2)}) collective-permute-start(bf16[512,256]{1,0:T(8,128)(2,1)S(1)} %get-tuple-element.146), channel_id=1, source_target_pairs={{0,12},{1,13},{2,14},{3,15},{4,8},{5,9},{6,10},{7,11},{8,4},{9,5},... | collective-permute-start | bytes 786440 | tf_op jit(solution)/shard_map/ppermute | solution.py:60
  357.9 13.1 collective-permute-start.9
  358.4 12.1 collective-permute-start.8
  371.1 8.5 collective-permute-start.12
  372.6 9.0 collective-permute-start.13
  374.0 12.4 collective-permute-start.14
  402.3 170.2 %all-gather.12.cloned.1.call-start = ((), (), s32[]{:S(2)}) async-start(), calls=%async_computation.2 | async-start | bytes 9437184 | tf_op jit(solution)/shard_map/all_gather | solution.py:77
  403.1 367.4 %all-gather.16.cloned.1.call-start = ((), (), s32[]{:S(2)}) async-start(), calls=%async_computation.4 | async-start | bytes 9437184 | tf_op jit(solution)/shard_map/all_gather | solution.py:77
  403.1 51.4 %collective-permute-start.23 = (bf16[1024,512]{1,0:T(8,128)(2,1)}, bf16[1024,512]{1,0:T(8,128)(2,1)S(1)}, u32[]{:S(2)}, u32[]{:S(2)}) collective-permute-start(bf16[1024,512]{1,0:T(8,128)(2,1)} %param.25), channel_id=1, source_target_pairs={{0,16},{1,0},{2,18},{3,2},{4,20},{5,4},{6,22},{7,6},{8,24},{9,8},{... | collective-permute-start | bytes 3145736 | tf_op jit(solution)/shard_map/ppermute | solution.py:60
  403.6 56.1 %collective-permute-start.24 = (bf16[1024,512]{1,0:T(8,128)(2,1)}, bf16[1024,512]{1,0:T(8,128)(2,1)S(1)}, u32[]{:S(2)}, u32[]{:S(2)}) collective-permute-start(bf16[1024,512]{1,0:T(8,128)(2,1)} %param.25), channel_id=1, source_target_pairs={{1,16},{3,18},{5,20},{7,22},{9,24},{11,26},{13,28},{15,30},{16,1},... | collective-permute-start | bytes 3145736 | tf_op jit(solution)/shard_map/ppermute | solution.py:60
  408.7 132.4 %collective-permute-start.28 = (bf16[512,2048]{1,0:T(8,128)(2,1)}, bf16[512,2048]{1,0:T(8,128)(2,1)S(1)}, u32[]{:S(2)}, u32[]{:S(2)}) collective-permute-start(bf16[512,2048]{1,0:T(8,128)(2,1)} %param.27), channel_id=1, source_target_pairs={{1,16},{3,18},{5,20},{7,22},{9,24},{11,26},{13,28},{15,30},{16,1},... | collective-permute-start | bytes 6291464 | tf_op jit(solution)/shard_map/ppermute | solution.py:60
  458.4 25.2 %collective-permute-start.25 = (bf16[1024,512]{1,0:T(8,128)(2,1)S(1)}, bf16[1024,512]{1,0:T(8,128)(2,1)S(1)}, u32[]{:S(2)}, u32[]{:S(2)}) collective-permute-start(bf16[1024,512]{1,0:T(8,128)(2,1)S(1)} %get-tuple-element.108), channel_id=1, source_target_pairs={{0,2},{1,3},{2,0},{3,1},{4,6},{5,7},{6,4},{7,5},{8,10},{9,11},{10,... | collective-permute-start | bytes 3145736 | tf_op jit(solution)/shard_map/ppermute | solution.py:60
  460.9 45.2 %collective-permute-start.26 = (bf16[1024,512]{1,0:T(8,128)(2,1)S(1)}, bf16[1024,512]{1,0:T(8,128)(2,1)S(1)}, u32[]{:S(2)}, u32[]{:S(2)}) collective-permute-start(bf16[1024,512]{1,0:T(8,128)(2,1)S(1)} %get-tuple-element.106), channel_id=1, source_target_pairs={{0,2},{1,3},{2,0},{3,1},{4,6},{5,7},{6,4},{7,5},{8,10},{9,11},{10,... | collective-permute-start | bytes 3145736 | tf_op jit(solution)/shard_map/ppermute | solution.py:60
  461.1 67.5 %collective-permute-start.21 = (bf16[512,1024]{1,0:T(8,128)(2,1)S(1)}, bf16[512,1024]{1,0:T(8,128)(2,1)S(1)}, u32[]{:S(2)}, u32[]{:S(2)}) collective-permute-start(bf16[512,1024]{1,0:T(8,128)(2,1)S(1)} %copy-done.54), channel_id=1, source_target_pairs={{0,2},{1,3},{2,0},{3,1},{4,6},{5,7},{6,4},{7,5},{8,10},{9,11},{10,... | collective-permute-start | bytes 3145736 | tf_op jit(solution)/shard_map/ppermute | solution.py:60
  462.5 77.5 %collective-permute-start.22 = (bf16[512,1024]{1,0:T(8,128)(2,1)S(1)}, bf16[512,1024]{1,0:T(8,128)(2,1)S(1)}, u32[]{:S(2)}, u32[]{:S(2)}) collective-permute-start(bf16[512,1024]{1,0:T(8,128)(2,1)S(1)} %copy-done.53), channel_id=1, source_target_pairs={{0,2},{1,3},{2,0},{3,1},{4,6},{5,7},{6,4},{7,5},{8,10},{9,11},{10,... | collective-permute-start | bytes 3145736 | tf_op jit(solution)/shard_map/ppermute | solution.py:60
  721.4 97.6 %all-gather.14.cloned.1.call-start = ((), (), s32[]{:S(2)}) async-start(), calls=%async_computation.3 | async-start | bytes 9437184 | tf_op jit(solution)/shard_map/all_gather | solution.py:77
  721.9 621.9 %all-gather.18.cloned.1.call-start = ((), (), s32[]{:S(2)}) async-start(), calls=%async_computation.5 | async-start | bytes 9437184 | tf_op jit(solution)/shard_map/all_gather | solution.py:77
  1092.0 10.0 collective-permute-start.30
  1092.7 12.1 collective-permute-start.31
  1095.0 19.5 %collective-permute-start.34 = (bf16[512,256]{1,0:T(8,128)(2,1)S(1)}, bf16[512,256]{1,0:T(8,128)(2,1)S(1)}, u32[]{:S(2)}, u32[]{:S(2)}) collective-permute-start(bf16[512,256]{1,0:T(8,128)(2,1)S(1)} %get-tuple-element.139), channel_id=1, source_target_pairs={{0,9},{1,8},{2,11},{3,10},{4,13},{5,12},{6,15},{7,14},{8,1},{9,0},... | collective-permute-start | bytes 786440 | tf_op jit(solution)/shard_map/ppermute | solution.py:60
  1098.0 15.7 collective-permute-start.33
  1102.0 15.3 collective-permute-start.35
  1118.0 233.3 %all-gather.20.cloned.1.call-start = ((), (), s32[]{:S(2)}) async-start(), calls=%async_computation.6 | async-start | bytes 9437184 | tf_op jit(solution)/shard_map/all_gather | solution.py:77
  1121.6 57.3 %collective-permute-start.27 = (bf16[512,2048]{1,0:T(8,128)(2,1)}, bf16[512,2048]{1,0:T(8,128)(2,1)}, u32[]{:S(2)}, u32[]{:S(2)}) collective-permute-start(bf16[512,2048]{1,0:T(8,128)(2,1)} %pad_maximum_fusion.4), channel_id=1, source_target_pairs={{1,16},{3,18},{5,20},{7,22},{9,24},{11,26},{13,28},{15,30},{16,1},... | collective-permute-start | bytes 6291464 | tf_op jit(solution)/shard_map/ppermute | solution.py:60
  1182.8 21.0 %collective-permute-start.44 = (f32[2,2048]{1,0:T(2,128)S(1)}, f32[2,2048]{1,0:T(2,128)S(1)}, u32[]{:S(2)}, u32[]{:S(2)}) collective-permute-start(f32[2,2048]{1,0:T(2,128)S(1)} %pad_maximum_fusion.7), channel_id=1, source_target_pairs={{0,4},{1,5},{2,6},{3,7},{4,0},{5,1},{6,2},{7,3},{8,12},{9,13},{10,... | collective-permute-start | bytes 49160 | tf_op jit(solution)/shard_map/ppermute | solution.py:60
  1198.0 142.3 %collective-permute-start.42 = (bf16[1024,512]{1,0:T(8,128)(2,1)}, bf16[1024,512]{1,0:T(8,128)(2,1)}, u32[]{:S(2)}, u32[]{:S(2)}) collective-permute-start(bf16[1024,512]{1,0:T(8,128)(2,1)} %get-tuple-element.99), channel_id=1, source_target_pairs={{0,1},{1,17},{2,3},{3,19},{4,5},{5,21},{6,7},{7,23},{8,9},{9,25},{... | collective-permute-start | bytes 3145736 | tf_op jit(solution)/shard_map/ppermute | solution.py:60
  1198.0 142.3 %collective-permute-start.41 = (bf16[1024,512]{1,0:T(8,128)(2,1)S(1)}, bf16[1024,512]{1,0:T(8,128)(2,1)}, u32[]{:S(2)}, u32[]{:S(2)}) collective-permute-start(bf16[1024,512]{1,0:T(8,128)(2,1)S(1)} %get-tuple-element.100), channel_id=1, source_target_pairs={{1,16},{3,18},{5,20},{7,22},{9,24},{11,26},{13,28},{15,30},{16,1},... | collective-permute-start | bytes 3145736 | tf_op jit(solution)/shard_map/ppermute | solution.py:60
  1203.9 44.2 %collective-permute-start.45 = (f32[2,2048]{1,0:T(2,128)S(1)}, f32[2,2048]{1,0:T(2,128)S(1)}, u32[]{:S(2)}, u32[]{:S(2)}) collective-permute-start(f32[2,2048]{1,0:T(2,128)S(1)} %fusion.59), channel_id=1, source_target_pairs={{0,8},{1,9},{2,10},{3,11},{4,12},{5,13},{6,14},{7,15},{8,0},{9,1},... | collective-permute-start | bytes 49160 | tf_op jit(solution)/shard_map/ppermute | solution.py:60
  1207.1 150.9 %collective-permute-start.40 = (bf16[512,2048]{1,0:T(8,128)(2,1)}, bf16[512,2048]{1,0:T(8,128)(2,1)}, u32[]{:S(2)}, u32[]{:S(2)}) collective-permute-start(bf16[512,2048]{1,0:T(8,128)(2,1)} %get-tuple-element.101), channel_id=1, source_target_pairs={{0,1},{1,17},{2,3},{3,19},{4,5},{5,21},{6,7},{7,23},{8,9},{9,25},{... | collective-permute-start | bytes 6291464 | tf_op jit(solution)/shard_map/ppermute | solution.py:60
  1207.1 150.9 %collective-permute-start.39 = (bf16[512,2048]{1,0:T(8,128)(2,1)}, bf16[512,2048]{1,0:T(8,128)(2,1)}, u32[]{:S(2)}, u32[]{:S(2)}) collective-permute-start(bf16[512,2048]{1,0:T(8,128)(2,1)} %get-tuple-element.102), channel_id=1, source_target_pairs={{1,16},{3,18},{5,20},{7,22},{9,24},{11,26},{13,28},{15,30},{16,1},... | collective-permute-start | bytes 6291464 | tf_op jit(solution)/shard_map/ppermute | solution.py:60
  1248.1 63.5 %collective-permute-start.46 = (f32[2,2048]{1,0:T(2,128)S(1)}, f32[2,2048]{1,0:T(2,128)S(1)}, u32[]{:S(2)}, u32[]{:S(2)}) collective-permute-start(f32[2,2048]{1,0:T(2,128)S(1)} %fusion.100), channel_id=1, source_target_pairs={{0,1},{1,0},{2,3},{3,2},{4,5},{5,4},{6,7},{7,6},{8,9},{9,8},{10,11... | collective-permute-start | bytes 49160 | tf_op jit(solution)/shard_map/ppermute | solution.py:60
  1318.9 19.9 %collective-permute-start.37 = (f32[2,4096]{1,0:T(2,128)S(1)}, f32[2,4096]{1,0:T(2,128)S(1)}, u32[]{:S(2)}, u32[]{:S(2)}) collective-permute-start(f32[2,4096]{1,0:T(2,128)S(1)} %add.384), channel_id=1, source_target_pairs={{0,8},{1,9},{2,10},{3,11},{4,12},{5,13},{6,14},{7,15},{8,0},{9,1},... | collective-permute-start | bytes 98312 | tf_op jit(solution)/shard_map/ppermute | solution.py:60
  1357.9 21.2 %collective-permute-start.43 = (bf16[256,1024]{1,0:T(8,128)(2,1)S(1)}, bf16[256,1024]{1,0:T(8,128)(2,1)S(1)}, u32[]{:S(2)}, u32[]{:S(2)}) collective-permute-start(bf16[256,1024]{1,0:T(8,128)(2,1)S(1)} %constant_dynamic-slice_fusion.1), channel_id=1, source_target_pairs={{0,2},{1,3},{2,0},{3,1},{4,6},{5,7},{6,4},{7,5},{8,10},{9,11},{10,... | collective-permute-start | bytes 1572872 | tf_op jit(solution)/shard_map/ppermute | solution.py:60
  1379.4 22.8 %collective-permute-start.48 = (bf16[256,512]{1,0:T(8,128)(2,1)S(1)}, bf16[256,512]{1,0:T(8,128)(2,1)S(1)}, u32[]{:S(2)}, u32[]{:S(2)}) collective-permute-start(bf16[256,512]{1,0:T(8,128)(2,1)S(1)} %get-tuple-element.97), channel_id=1, source_target_pairs={{0,1},{1,17},{2,3},{3,19},{4,5},{5,21},{6,7},{7,23},{8,9},{9,25},{... | collective-permute-start | bytes 786440 | tf_op jit(solution)/shard_map/ppermute | solution.py:60
  1379.5 22.7 %collective-permute-start.47 = (bf16[256,512]{1,0:T(8,128)(2,1)S(1)}, bf16[256,512]{1,0:T(8,128)(2,1)S(1)}, u32[]{:S(2)}, u32[]{:S(2)}) collective-permute-start(bf16[256,512]{1,0:T(8,128)(2,1)S(1)} %get-tuple-element.98), channel_id=1, source_target_pairs={{1,16},{3,18},{5,20},{7,22},{9,24},{11,26},{13,28},{15,30},{16,1},... | collective-permute-start | bytes 786440 | tf_op jit(solution)/shard_map/ppermute | solution.py:60
  (92 other events, 3657.8 us)
Sparse Core Ops, SparseCore 0:
  187.3 103.0 all-gather.7
  402.4 82.0 all-gather.9
  486.7 46.9 all-gather.11
  721.5 48.9 all-gather.15
  771.9 46.9 all-gather.13
  1118.1 67.8 all-gather.17
  1187.7 77.3 all-gather.19

commit v2 on v1

--- a/solution.py
+++ b/solution.py
@@ -78,13 +78,6 @@
             value, BOTH, axis=0, tiled=True, axis_index_groups=self.token_groups
         )
 
-    def token_sum(self, value):
-        flip = 1
-        while flip < self.rows:
-            value = value + self.partner(value, flip)
-            flip *= 2
-        return value
-
     def weight_pair(self, value):
         def outward(zhi, rest, xx, core):
             return (1 - zhi, rest, xx, core) if zhi == core else (zhi, rest, xx, 1 - core)
@@ -184,7 +177,9 @@
     )
 
 
-def gather_kernel(plan, own, weight, out, weights, *sems):
+def gather_kernel(plan, pieces, axes, own, *refs):
+    count = len(axes)
+    weights, out, wholes, sems = refs[:count], refs[count], refs[count + 1 :][:count], refs[2 * count + 1 :]
     have_sem, swap_sem, send_sem, recv_sem, near_sem, near_recv_sem = sems[:6]
     block_sem, block_recv_sem, side_sem, side_recv_sem = sems[6:]
     half, across = plan.half, plan.across
@@ -193,13 +188,17 @@
     row, col = zhi * half + rest, base + core
     far_row, near_col = (1 - zhi) * half + rest, base + 1 - core
     rows = own.shape[0]
-    part = rows // 2
-    depth = weight.shape[0]
+    part = rows // pieces
     moved, stays = zhi != core, zhi == core
 
     barrier = pltpu.get_barrier_semaphore()
+    side_y = half // 2
+    zlo, y = rest // side_y, rest % side_y
+    base_row = zhi * half
+
     greeted = [(row, near_col), (far_row, col), (far_row, near_col)]
-    greeted += [(zhi * half + (rest + step) % half, col) for step in range(1, half)]
+    greeted += [(base_row + (1 - zlo) * side_y + y, col)]
+    greeted += [(base_row + zlo * side_y + (y + step) % side_y, col) for step in range(1, side_y)]
     greeted += [(row, (xx + step) % across * 2 + core) for step in range(1, across)]
     for device in greeted:
         pl.semaphore_signal(barrier, 1, device_id=device, device_id_type=MESH)
@@ -224,57 +223,72 @@
             near_col,
         )
 
-    def sibling(step, h):
-        at = out.at[lines(core * half + (rest + half - step) % half, h)]
+    def block_at(over, step):
+        other = zlo + over * (1 - 2 * zlo)
+        return core * half + other * side_y + (y + side_y - step) % side_y
+
+    def sibling(over, step, h):
+        at = out.at[lines(block_at(over, step), h)]
         return remote(
-            at, at, near_sem.at[step, h], near_recv_sem.at[step, h], row, near_col
-        )
-
-    def outward(step, h):
-        at = out.at[lines(core * half + rest, h)]
-        chip = zhi * half + (rest + step) % half
-        return remote(at, at, send_sem.at[step - 1, h], recv_sem.at[step - 1, h], chip, col)
-
-    def place(other, j):
-        return pl.ds(pl.multiple_of((other * 2 + j) * depth, depth), depth)
-
-    def block_keep():
+            at,
+            at,
+            near_sem.at[over, step, h],
+            near_recv_sem.at[over, step, h],
+            row,
+            near_col,
+        )
+
+    def along_z(h):
+        at = out.at[lines(block_at(0, 0), h)]
+        chip = base_row + (1 - zlo) * side_y + y
+        return remote(at, at, send_sem.at[0, 0, h], recv_sem.at[1, 0, h], chip, col)
+
+    def along_y(over, step, h):
+        at = out.at[lines(block_at(over, 0), h)]
+        chip = base_row + zlo * side_y + (y + step) % side_y
+        return remote(at, at, send_sem.at[over, step, h], recv_sem.at[over, step, h], chip, col)
+
+    def place(index, other, j):
+        axis = axes[index]
+        size = weights[index].shape[axis]
+        at = pl.ds(pl.multiple_of((other * 2 + j) * size, size), size)
+        return wholes[index].at[at] if axis == 0 else wholes[index].at[:, at]
+
+    def block_keep(index, j):
         return pltpu.make_async_copy(
-            weight, weights.at[place(xx, core)], block_recv_sem.at[core]
-        )
-
-    def block_send(index, to_row, to_col):
+            weights[index], place(index, xx, j), block_recv_sem.at[index, j]
+        )
+
+    def block_send(index, way, to_row, to_col):
         return remote(
-            weight,
-            weights.at[place(xx, core)],
-            block_sem.at[index],
-            block_recv_sem.at[core],
+            weights[index],
+            place(index, xx, core),
+            block_sem.at[index, way],
+            block_recv_sem.at[index, core],
             to_row,
             to_col,
         )
 
-    def side(step, j):
-        at = weights.at[place(xx, j)]
+    def side(index, step, j):
+        at = place(index, xx, j)
         other = (xx + step) % across * 2 + core
         return remote(
-            at, at, side_sem.at[step - 1, j], side_recv_sem.at[step - 1, j], row, other
+            at, at, side_sem.at[index, step - 1, j], side_recv_sem.at[index, step - 1, j], row, other
         )
 
     @pl.when(moved)
     def _():
-        for h in range(2):
+        for h in range(pieces):
             entry_far(h).start()
-        block_send(0, row, near_col).start()
-        block_send(1, far_row, near_col).start()
 
     @pl.when(stays)
     def _():
-        for h in range(2):
+        for h in range(pieces):
             entry_near(h).start()
-        block_keep().start()
-        block_send(0, far_row, col).start()
-
-    for h in range(2):
+        for index in range(count):
+            block_keep(index, core).start()
+
+    for h in range(pieces):
 
         @pl.when(moved)
         def _():
@@ -284,80 +298,165 @@
         def _():
             entry_near(h).wait()
 
-        for step in range(1, half):
-            outward(step, h).start()
-        sibling(0, h).start()
-        if h == 0:
-            for j in range(2):
-                pltpu.make_async_copy(weight, weights.at[place(xx, j)], block_recv_sem.at[j]).wait()
-                for step in range(1, across):
-                    side(step, j).start()
-    for h in range(2):
-        for step in range(1, half):
-            outward(step, h).wait_recv()
-            sibling(step, h).start()
-    for h in range(2):
-        for step in range(half):
-            sibling(step, h).wait()
-        for step in range(1, half):
-            outward(step, h).wait_send()
-    for j in range(2):
-        for step in range(1, across):
-            side(step, j).wait()
+        along_z(h).start()
+        for step in range(1, side_y):
+            along_y(0, step, h).start()
+        sibling(0, 0, h).start()
+
+    for h in range(pieces):
+        along_z(h).wait_recv()
+        for step in range(1, side_y):
+            along_y(1, step, h).start()
+        sibling(1, 0, h).start()
+        sibling(0, 0, h).wait_recv()
+        if h == pieces // 2:
+            for index in range(count):
+
+                @pl.when(moved)
+                def _():
+                    block_send(index, 0, row, near_col).start()
+                    block_send(index, 1, far_row, near_col).start()
+
+                @pl.when(stays)
+                def _():
+                    block_send(index, 0, far_row, col).start()
+
+    for over in range(2):
+        for h in range(pieces):
+            for step in range(1, side_y):
+                along_y(over, step, h).wait_recv()
+                sibling(over, step, h).start()
+    for index in range(count):
+        for j in range(2):
+            block_keep(index, j).wait()
+            for step in range(1, across):
+                side(index, step, j).start()
+    for h in range(pieces):
+        along_z(h).wait_send()
+        for over in range(2):
+            sibling(over, 0, h).wait_send()
+            if over:
+                sibling(over, 0, h).wait_recv()
+            for step in range(1, side_y):
+                sibling(over, step, h).wait()
+                along_y(over, step, h).wait_send()
+    for index in range(count):
+        for j in range(2):
+            for step in range(1, across):
+                side(index, step, j).wait()
+
+        @pl.when(moved)
+        def _():
+            block_send(index, 0, row, near_col).wait_send()
+            block_send(index, 1, far_row, near_col).wait_send()
+
+        @pl.when(stays)
+        def _():
+            block_send(index, 0, far_row, col).wait_send()
 
     @pl.when(moved)
     def _():
-        for h in range(2):
+        for h in range(pieces):
             entry_far(h).wait_send()
-        block_send(0, row, near_col).wait_send()
-        block_send(1, far_row, near_col).wait_send()
-
-    @pl.when(stays)
-    def _():
-        block_send(0, far_row, col).wait_send()
-
-
-def swap_gather(plan, own, weight, collective_id):
-    half = plan.half
+
+
+def swap_gather(plan, own, weights, axes, collective_id):
+    half, count = plan.half, len(weights)
+    pieces = 4
     dma = pltpu.SemaphoreType.DMA
     shape = (own.shape[0] * plan.rows, own.shape[1])
     anywhere = pl.BlockSpec(memory_space=pl.ANY)
     return pl.pallas_call(
-        functools.partial(gather_kernel, plan),
-        in_specs=[anywhere] * 2,
-        out_specs=[anywhere] * 2,
-        out_shape=[
-            jax.ShapeDtypeStruct(shape, own.dtype),
-            jax.ShapeDtypeStruct((weight.shape[0] * plan.cols, weight.shape[1]), weight.dtype),
+        functools.partial(gather_kernel, plan, pieces, axes),
+        in_specs=[anywhere] * (1 + count),
+        out_specs=[anywhere] * (1 + count),
+        out_shape=[jax.ShapeDtypeStruct(shape, own.dtype)]
+        + [
+            jax.ShapeDtypeStruct(grow(weight.shape, axis, plan.cols), weight.dtype)
+            for weight, axis in zip(weights, axes, strict=True)
         ],
         scratch_shapes=[
-            dma((2,)),
-            dma((2,)),
-            dma((half - 1, 2)),
-            dma((half - 1, 2)),
-            dma((half, 2)),
-            dma((half, 2)),
-            dma((2,)),
-            dma((2,)),
-            dma((plan.across - 1, 2)),
-            dma((plan.across - 1, 2)),
+            dma((pieces,)),
+            dma((pieces,)),
+            dma((2, half // 2, pieces)),
+            dma((2, half // 2, pieces)),
+            dma((2, half // 2, pieces)),
+            dma((2, half // 2, pieces)),
+            dma((count, 2)),
+            dma((count, 2)),
+            dma((count, plan.across - 1, 2)),
+            dma((count, plan.across - 1, 2)),
         ],
         cost_estimate=pl.CostEstimate(
             flops=0, bytes_accessed=20 * shape[0] * shape[1], transcendentals=0
         ),
         compiler_params=pltpu.CompilerParams(collective_id=collective_id, has_side_effects=True),
-    )(own, weight)
-
-
-def scatter_kernel(plan, parts, axes, turned, last, *refs):
+    )(own, *weights)
+
+
+def sum_kernel(plan, own, out, landed, send_sem, recv_sem):
+    half, rows = plan.half, plan.rows
+    zhi, rest, base, core = position(plan)
+
+    def device(step):
+        block = (core * half + rest + step) % rows
+        return zhi * half + block % half, base + block // half
+
+    barrier = pltpu.get_barrier_semaphore()
+    for step in range(1, rows):
+        pl.semaphore_signal(barrier, 1, device_id=device(step), device_id_type=MESH)
+    pl.semaphore_wait(barrier, rows - 1)
+    copies = [
+        remote(
+            own, landed.at[step - 1], send_sem.at[step - 1], recv_sem.at[step - 1], *device(step)
+        )
+        for step in range(1, rows)
+    ]
+    for copy in copies:
+        copy.start()
+    total = own[...]
+    for step, copy in enumerate(copies):
+        copy.wait_recv()
+        total = total + landed[step]
+    out[...] = total
+    for copy in copies:
+        copy.wait_send()
+
+
+def group_sum(plan, value, collective_id):
+    others = plan.rows - 1
+    inside = pl.BlockSpec(memory_space=pltpu.VMEM)
+    dma = pltpu.SemaphoreType.DMA
+    return pl.pallas_call(
+        functools.partial(sum_kernel, plan),
+        in_specs=[inside],
+        out_specs=inside,
+        out_shape=jax.ShapeDtypeStruct(value.shape, value.dtype),
+        scratch_shapes=[
+            pltpu.VMEM((others, *value.shape), value.dtype),
+            dma((others,)),
+            dma((others,)),
+        ],
+        cost_estimate=pl.CostEstimate(
+            flops=value.size * others, bytes_accessed=2**24, transcendentals=0
+        ),
+        compiler_params=pltpu.CompilerParams(collective_id=collective_id, has_side_effects=True),
+    )(value)
+
+
+def scatter_kernel(plan, parts, axes, turned, last, swaps, *refs):
     half, across, count = plan.half, plan.across, len(axes)
     lefts, weight, refs = refs[:parts], refs[parts], refs[parts + 1 :]
     grads, refs = refs[:count], refs[count:]
     if last:
         residual, refs = refs[0], refs[1:]
+    if swaps:
+        given, refs = refs[0], refs[1:]
     out, blocks, refs = refs[0], refs[1 : count + 1], refs[count + 1 :]
     if last:
         sums, refs = refs[0], refs[1:]
+    if swaps:
+        taken, refs = refs[0], refs[1:]
     loaded, near_out, near_in, far_out, far_in = refs[:5]
     load_sem, near_sem, near_recv_sem, far_sem, far_recv_sem, block_sem, block_recv_sem = refs[5:12]
     refs = refs[12:]
@@ -371,12 +470,31 @@
     tile = min(512, width)
 
     barrier = pltpu.get_barrier_semaphore()
-    greeted = [(row, near_col)]
-    greeted += [(zhi * half + (rest + step) % half, col) for step in range(1, half)]
+    side_y = half // 2
+    zlo, y = rest // side_y, rest % side_y
+    base_row = zhi * half
+
+    def split(unit):
+        h, index = unit // half, unit % half
+        first = side_y + h * (2 - side_y)
+        second = half // first
+        ahead = first - 1 - index // second
+        aside = second - 1 - index % second
+        place = y + h * (zlo - y)
+        other = zlo + h * (y - zlo)
+        return h, (place + ahead) % first, (other + aside) % second, place, other, ahead
+
+    def chip_of(h, along, beside):
+        return (beside + h * (along - beside)) * side_y + along + h * (beside - along)
+
+    greeted = [(row, near_col), (base_row + (1 - zlo) * side_y + y, col)]
+    greeted += [(base_row + zlo * side_y + (y + step) % side_y, col) for step in range(1, side_y)]
     if count:
         greeted += [(row, (xx + step) % across * 2 + core) for step in range(1, across)]
     if last:
-        greeted += [(far_row, col), (far_row, near_col)]
+        greeted += [(far_row, col)]
+    if last or swaps:
+        greeted += [(far_row, near_col)]
     for device in greeted:
         pl.semaphore_signal(barrier, 1, device_id=device, device_id_type=MESH)
 
@@ -395,9 +513,9 @@
         )
 
     def load(unit, whose, slot):
-        h, step = unit // half, half - 1 - unit % half
+        h, along, beside = split(unit)[:3]
         side = (1 - core) if whose == 0 else core
-        index = side * half + (rest + step) % half
+        index = side * half + chip_of(h, along, beside)
         target, sem = loaded.at[slot, whose], load_sem.at[slot, whose]
         if parts == 1:
             at = pl.ds(pl.multiple_of(index * rows + h * part, part), part)
@@ -425,10 +543,16 @@
         )
 
     def far(unit):
-        step = half - 1 - unit % half
-        chip = zhi * half + (rest + step) % half
+        h, along, beside, place, other, ahead = split(unit)
+        straight = (ahead + half - 1) // half
+        chip = chip_of(h, along, beside + straight * (other - beside))
         return remote(
-            far_out.at[unit], far_in.at[unit], far_sem.at[unit], far_recv_sem.at[unit], chip, col
+            far_out.at[unit],
+            far_in.at[unit],
+            far_sem.at[unit],
+            far_recv_sem.at[unit],
+            base_row + chip,
+            col,
         )
 
     def product(left, cols):
@@ -439,8 +563,17 @@
     def columns(n):
         return pl.ds(pl.multiple_of(n * tile, tile), tile)
 
+    def exchange():
+        return remote(given, taken, refs[0], refs[1], far_row, near_col)
+
+    def keep():
+        return pltpu.make_async_copy(given, taken, refs[1])
+
     start(load(0, 0, 0))
     pl.semaphore_wait(barrier, len(greeted))
+    if swaps:
+        pl.when(moved)(lambda: exchange().start())
+        pl.when(stays)(lambda: keep().start())
     for index in range(count):
         for step in range(1, across):
             block(index, step).start()
@@ -480,7 +613,7 @@
                 value = value + near_in[before, :, columns(n)].astype(jnp.float32)
                 far_out[before, :, columns(n)] = value.astype(far_out.dtype)
 
-            @pl.when(before % half < half - 1)
+            @pl.when(split(before)[5] > 0)
             def _():
                 far(before).start()
 
@@ -488,12 +621,31 @@
 
     lax.fori_loop(0, 2 * half + 1, body, 0)
 
+    def line_sum(h, aside):
+        first = side_y if h == 0 else 2
+        second = half // first
+        at = h * half + second - 1 - aside
+        value = far_out[at + (first - 1) * second].astype(jnp.float32)
+        for ahead in range(first - 1):
+            unit = at + ahead * second
+            far(unit).wait_recv()
+            value = value + far_in[unit].astype(jnp.float32)
+        return value
+
+    for h in range(2):
+        second = 2 if h == 0 else side_y
+        for aside in range(second - 1, 0, -1):
+            unit = (h + 1) * half - 1 - aside
+            far_out[unit] = line_sum(h, aside).astype(far_out.dtype)
+            far(unit).start()
+
     def total(h):
-        for step in range(half - 1):
-            far(h * half + step).wait_recv()
-        value = far_out[h * half + half - 1].astype(jnp.float32)
-        for step in range(half - 1):
-            value = value + far_in[h * half + step].astype(jnp.float32)
+        value = line_sum(h, 0)
+        second = 2 if h == 0 else side_y
+        for aside in range(second - 1, 0, -1):
+            unit = (h + 1) * half - 1 - aside
+            far(unit).wait_recv()
+            value = value + far_in[unit].astype(jnp.float32)
         return value
 
     if last:
@@ -548,6 +700,9 @@
         for index in range(count):
             for step in range(1, across):
                 block(index, step).wait_recv()
+    if swaps:
+        pl.when(moved)(lambda: exchange().wait())
+        pl.when(stays)(lambda: keep().wait())
     for h in range(2):
         for unit in range(h * half, h * half + half - 1):
             far(unit).wait_send()
@@ -621,11 +776,17 @@
     return run
 
 
+def grow(shape, axis, pieces):
+    return tuple(size * pieces if dim == axis else size for dim, size in enumerate(shape))
+
+
 def cut(shape, axis, pieces):
     return tuple(size // pieces if dim == axis else size for dim, size in enumerate(shape))
 
 
-def multiply_scatter(plan, lefts, weight, turned, collective_id, grads=(), axes=(), residual=None):
+def multiply_scatter(
+    plan, lefts, weight, turned, collective_id, grads=(), axes=(), residual=None, swapped=None
+):
     half, across, count = plan.half, plan.across, len(grads)
     depth = lefts[0].shape[1]
     width = weight.shape[0 if turned else 1]
@@ -636,7 +797,9 @@
     anywhere = pl.BlockSpec(memory_space=pl.ANY)
     inside = pl.BlockSpec(memory_space=pltpu.VMEM)
     last = residual is not None
+    swaps = swapped is not None
     in_specs = [anywhere] * len(lefts) + [inside] + [anywhere] * count + [inside] * last
+    in_specs += [anywhere] * swaps
     out_specs = [anywhere if last else inside] + [anywhere] * count + [inside] * last
     out_shape = [jax.ShapeDtypeStruct((rows, width), low if last else jnp.float32)]
     out_shape += [
@@ -672,10 +835,13 @@
             dma((2,)),
             dma((2,)),
         ]
+    if swaps:
+        out_shape.append(jax.ShapeDtypeStruct(swapped.shape, swapped.dtype))
+        scratch += [dma, dma]
     return pl.pallas_call(
-        functools.partial(scatter_kernel, plan, len(lefts), axes, turned, last),
+        functools.partial(scatter_kernel, plan, len(lefts), axes, turned, last, swaps),
         in_specs=in_specs,
-        out_specs=out_specs,
+        out_specs=out_specs + [anywhere] * swaps,
         out_shape=out_shape,
         scratch_shapes=scratch,
         cost_estimate=pl.CostEstimate(
@@ -686,7 +852,7 @@
         compiler_params=pltpu.CompilerParams(
             collective_id=collective_id, has_side_effects=True, vmem_limit_bytes=58 * 2**20
         ),
-    )(*lefts, weight, *grads, *([residual] if last else []))
+    )(*lefts, weight, *grads, *([residual] if last else []), *([swapped] if swaps else []))
 
 
 def full(rows, width):
@@ -699,6 +865,43 @@
 
 def column(row_vector, width):
     return jnp.transpose(jnp.broadcast_to(row_vector, (width, row_vector.shape[1])))
+
+
+def project_kernel(head_size, left, weight, proj, squares):
+    value = jnp.dot(left[...], weight[...], preferred_element_type=jnp.float32)
+    proj[...] = value
+    width = proj.shape[1] // 3
+    for place in range(2):
+        total = None
+        for start in range(place * width, (place + 1) * width, head_size):
+            part = value[:, start : start + head_size] ** 2
+            total = part if total is None else total + part
+        squares[place : place + 1, :] = jnp.sum(jnp.transpose(total), axis=0, keepdims=True)
+
+
+def project(left, weight, head_size):
+    seq_len, depth = left.shape
+    rows = min(512, seq_len)
+    wide = weight.shape[1]
+    return pl.pallas_call(
+        functools.partial(project_kernel, head_size),
+        grid=(seq_len // rows,),
+        in_specs=[pl.BlockSpec((rows, depth), lambda i: (i, 0)), full(depth, wide)],
+        out_specs=[
+            pl.BlockSpec((rows, wide), lambda i: (i, 0)),
+            pl.BlockSpec((2, rows), lambda i: (0, i)),
+        ],
+        out_shape=[
+            jax.ShapeDtypeStruct((seq_len, wide), jnp.float32),
+            jax.ShapeDtypeStruct((2, seq_len), jnp.float32),
+        ],
+        cost_estimate=pl.CostEstimate(
+            flops=2 * seq_len * depth * wide,
+            bytes_accessed=2 * seq_len * depth + 4 * seq_len * wide,
+            transcendentals=0,
+        ),
+        compiler_params=pltpu.CompilerParams(vmem_limit_bytes=40 * 2**20),
+    )(left, weight)
 
 
 def prepare_kernel(
@@ -826,11 +1029,9 @@
     out,
     out_grad,
     log_sum,
-    query_grad,
-    key_grad,
-    value_grad,
-    delta,
+    *refs,
 ):
+    query_grad, key_grad, value_grad, delta = refs[-4:]
     step = pl.program_id(1)
     seq_len, head_size = query.shape
     factor = LOG2E * head_size**-0.5
@@ -871,7 +1072,7 @@
     value_grad[...] = value_acc.astype(value_grad.dtype)
 
 
-def attend_back(high, first, query, key, value, out, out_grad, log_sum, head_size, rows):
+def attend_back(high, first, query, key, value, out, out_grad, log_sum, head_size, rows, more):
     seq_len, width = query.shape
     heads = width // head_size
     whole = pl.BlockSpec((seq_len, head_size), lambda h, j, *_: (0, h))
@@ -889,7 +1090,8 @@
                 whole,
                 whole,
                 pl.BlockSpec((1, 1, seq_len), lambda h, j, *_: (h, 0, 0)),
-            ],
+            ]
+            + [pl.BlockSpec(memory_space=pl.ANY)] * len(more),
             out_specs=[whole, block, block],
             scratch_shapes=[pltpu.VMEM((1, seq_len), jnp.float32)],
         ),
@@ -904,7 +1106,7 @@
             transcendentals=0,
         ),
         compiler_params=pltpu.CompilerParams(vmem_limit_bytes=48 * 2**20),
-    )(high, first, query, key, value, out, out_grad, log_sum)
+    )(high, first, query, key, value, out, out_grad, log_sum, *more)
 
 
 def norm_back_kernel(
@@ -1111,7 +1313,9 @@
         return jnp.pad(vector, (0, extra * wide - small_size)).reshape(extra, wide)
 
     own_weight = jnp.concatenate([qkv_own, lines(small_own)], axis=0)
-    gathered_x, both = swap_gather(plan, layer_input, own_weight, 1)
+    gathered_x, both, out_rows = swap_gather(
+        plan, layer_input, (own_weight, w_out), (0, 1), 1
+    )
     both = both.reshape(plan.cols, own_depth + extra, wide)
     proj_weight = both[:, :own_depth].reshape(-1, wide)
     small = both[:, own_depth:].reshape(plan.cols, extra * wide)[:, :small_size].astype(f32)
@@ -1121,10 +1325,7 @@
 
     own_x = lax.dynamic_slice_in_dim(gathered_x, mine * own_tokens, own_tokens)
     segments = plan.swap(segments)
-    gate_pair = plan.weight_pair(after(w_gate, gathered_x))
-    out_pair = plan.weight_pair(after(w_out, gathered_x))
-    up_pair = plan.weight_pair(after(w_up, gathered_x))
-    down_pair = plan.weight_pair(after(w_down, gathered_x))
+    out_full = plan.token_gather(out_rows)
     ff_width = w_gate.shape[1]
 
     local_width = wide // 3
@@ -1148,29 +1349,18 @@
     high = (ends - 1) // tile
     first_row = first[None, :]
 
-    proj = jnp.dot(gathered_x, proj_weight, preferred_element_type=f32)
-    squares = jnp.stack(
-        [
-            jnp.sum(proj[:, start : start + local_width] ** 2, axis=-1)
-            for start in (0, local_width)
-        ]
-    )
-    invs = lax.rsqrt(plan.token_sum(squares) / model_width + EPS)
+    proj, squares = project(gathered_x, proj_weight, head_size)
+    invs = lax.rsqrt(group_sum(plan, squares, 5) / model_width + EPS)
     query_inv, key_inv = invs[:1], invs[1:]
     query, key, value = prepare(
         proj, query_inv, key_inv, cosine, sine, query_scale, key_scale, head_size
     )
+    gate_pair = plan.weight_pair(after(w_gate, invs))
+    up_pair = plan.weight_pair(after(w_up, query))
     attn_out, log_sum = attend(
-        low, first_row, query, key, value, head_size, tile, (*gate_pair, *out_pair)
+        low, first_row, query, key, value, head_size, tile, gate_pair
     )
     post_depth = w_out.shape[1]
-    out_full = plan.token_gather(
-        join(
-            (local_width, model_width),
-            [(0, c * post_depth, piece) for c, piece in plan.weight_pieces(out_pair)],
-        )
-    )
-    own_cot = plan.swap(after(cotangent, attn_out))
 
     attn_tokens = jnp.zeros((own_tokens, model_width), bf16)
     for flip in range(rows):
@@ -1180,16 +1370,16 @@
             piece = plan.partner(piece, flip)
         attn_tokens = lax.dynamic_update_slice(attn_tokens, piece, (0, other * local_width))
 
-    attn_tokens, *up_pair = lax.optimization_barrier((attn_tokens, *up_pair))
-    gate_pieces = plan.weight_pieces(gate_pair)
-    places, gate_pieces = zip(*gate_pieces, strict=True)
-    attn_tokens, *gate_pieces = lax.optimization_barrier((attn_tokens, *gate_pieces))
-    gate_pieces = list(zip(places, gate_pieces, strict=True))
+    places, gate_pieces = zip(*plan.weight_pieces(gate_pair), strict=True)
+    attn_tokens, *others = lax.optimization_barrier((attn_tokens, *gate_pieces, *up_pair))
+    gate_pieces, up_pair = zip(places, others[:-2], strict=True), others[-2:]
+    up_pieces = plan.weight_pieces(up_pair)
+    down_pair = plan.weight_pair(after(w_down, *(piece for _, piece in up_pieces)))
     ff_weight = join(
         (model_width, 2 * ff_width),
         [
             (c * own_depth, start, piece)
-            for start, pieces in ((0, gate_pieces), (ff_width, plan.weight_pieces(up_pair)))
+            for start, pieces in ((0, gate_pieces), (ff_width, up_pieces))
             for c, piece in pieces
         ],
     )
@@ -1221,7 +1411,9 @@
         gate.append(both[:, :ff_width])
         up.append(both[:, ff_width:])
         activated.append((jax.nn.silu(gate[k].astype(f32)) * up[k].astype(f32)).astype(bf16))
-    (mlp_out,) = multiply_scatter(plan, activated, down_rows, False, 2)
+    mlp_out, own_cot = multiply_scatter(
+        plan, activated, down_rows, False, 2, swapped=cotangent
+    )
 
     outputs, upstream, shard_rows = [], [], []
     mlp_gain_part = 0.0
@@ -1231,7 +1423,6 @@
         upstream.append(chunk_of(own_cot, k).astype(f32))
         mlp_gain_part += jnp.sum(upstream[k] * hat, axis=0)
         shard_rows.append(plan.token_gather(norm_grad(inv, hat, upstream[k] * mlp_scale)))
-    layer_output = plan.swap(jnp.concatenate(outputs))
 
     ff_grad = []
     for k in chunks:
@@ -1243,12 +1434,19 @@
         ff_grad.append(jnp.concatenate([gate_grad, up_grad], axis=1).astype(bf16))
     down_grad = sum(contract_rows(activated[k], shard_rows[k]) for k in chunks).astype(bf16)
     ff_weight_grad = sum(contract_rows(gathered_h[k], ff_grad[k]) for k in chunks).astype(bf16)
-    hidden_grad_mlp, down_blocks, ff_blocks = multiply_scatter(
-        plan, ff_grad, ff_weight, True, 3, (down_grad, ff_weight_grad), (1, 0)
+    hidden_grad_mlp, ff_blocks, layer_output = multiply_scatter(
+        plan,
+        ff_grad,
+        ff_weight,
+        True,
+        3,
+        (ff_weight_grad,),
+        (0,),
+        swapped=jnp.concatenate(outputs),
     )
     hidden_grad = [upstream[k] + chunk_of(hidden_grad_mlp, k) for k in chunks]
     ff_sum = plan.weight_send(plan.weight_sum(ff_weight_grad, ff_blocks, 0), 0)
-    down_sum = plan.weight_send(plan.weight_sum(down_grad, down_blocks, 1), 1)
+    down_blocks = plan.weight_exchange(after(down_grad, ff_blocks), 1)
 
     attn_gain_part = 0.0
     proj_grads, token_grads = [], []
@@ -1271,23 +1469,38 @@
     out_grad = sum(
         contract_rows(
             attn_out.reshape(rows, 2, part, local_width)[:, k].reshape(-1, local_width),
-            plan.token_gather(after(proj_grads[k], attn_grad)),
+            plan.token_gather(proj_grads[k]),
         )
         for k in chunks
     ).astype(bf16)
     out_sum = plan.weight_sum(out_grad, plan.weight_exchange(out_grad, 1), 1)
     query_grad, key_grad, value_grad = attend_back(
-        high, first_row, query, key, value, attn_out, attn_grad, log_sum, head_size, tile
-    )
+        high,
+        first_row,
+        query,
+        key,
+        value,
+        attn_out,
+        attn_grad,
+        log_sum,
+        head_size,
+        tile,
+        (down_blocks,),
+    )
+    down_sum = plan.weight_send(plan.weight_sum(down_grad, down_blocks, 1), 1)
     shared = (proj, query_inv, key_inv, cosine, sine, query_scale, key_scale, query_grad, key_grad)
     dots, gain_sums = norm_back(*shared, head_size)
-    dots = plan.token_sum(dots)
+    dots = group_sum(
+        plan,
+        jnp.concatenate([dots, jnp.stack([attn_gain_part, mlp_gain_part])], axis=1),
+        6,
+    )
+    dots, post_sums = dots[:, :seq_len], dots[:, seq_len:]
     proj_grad_all = proj_back(
-        *shared, value_grad, dots, head_size, model_width, (ff_sum, down_sum)
+        *shared, value_grad, dots, head_size, model_width, (ff_sum,)
     )
     proj_grad_all = after(proj_grad_all, out_sum)
     proj_weight_grad = contract_rows(gathered_x, proj_grad_all).astype(bf16)
-    post_sums = plan.token_sum(jnp.stack([attn_gain_part, mlp_gain_part]))
     small = jnp.concatenate(
         [
             gain_sums[0].reshape(plan.cols, -1),
@@ -1304,7 +1517,7 @@
     )
     stacked = stacked.reshape(-1, wide)
     out_sum = plan.weight_send(out_sum, 1)
-    stacked = after(stacked, out_sum)
+    stacked = after(stacked, out_sum, down_sum)
     input_grad, _, proj_sum = multiply_scatter(
         plan,
         [proj_grad_all],

time: 1590 us -> 1480 us (0.931)
  waiting for transfers between devices: 364 us -> 277 us
  Pallas kernels: 676 us -> 746 us
  starting transfers between devices: 93.3 us -> 60.1 us
  matrix products: 237 us -> 212 us
    ppermute x49 -> x35, waiting for transfers between devices: 294 us -> 208 us  [send(): return lax.ppermute(value, BOTH, pairs)]
    pallas_call x1 -> x4, Pallas kernels: 153 us -> 210 us  [the longest x1 157 us: swap_gather(): pl.pallas_call(functools.partial(gather_kernel, plan, pieces, axes), in_s...]
    ppermute x49 -> x35, starting transfers between devices: 93 us -> 59.8 us  [send(): return lax.ppermute(value, BOTH, pairs)]
    dot_general x1 -> x0, matrix products: 21.1 us -> none  [body(): proj = jnp.dot(gathered_x, proj_weight, preferred_element_type=f32)]
    unnamed x175 -> x194, local copies, waits for them, and re-layouts: 22.8 us -> 33 us
  transfers between devices with their start and end apart: 56 -> 42, of which waited for: 24 -> 18; matrix products, arithmetic and copies ran while one was open for 14% -> 13% of each run, Pallas kernels for 7% -> 11%
where the time goes in v2:
time: 1480 us
  Pallas kernels  746 us (50%)
  waiting for transfers between devices  277 us (19%)
  matrix products  212 us (14%)
  other arithmetic  97 us (7%)
  local copies, waits for them, and re-layouts  67.5 us (5%)
  starting transfers between devices  60.1 us (4%)
  between operations  16.1 us (1%)
    pallas_call x3, Pallas kernels, multiply_scatter(): pl.pallas_call(functools.partial(scatter_kernel, plan, len(lefts), axes,...  424 us
    ppermute x35, waiting for transfers between devices, send(): return lax.ppermute(value, BOTH, pairs)  208 us
    pallas_call x1, Pallas kernels, swap_gather(): pl.pallas_call(functools.partial(gather_kernel, plan, pieces, axes), in_s...  157 us
    dot_general x7, matrix products, contract_rows(): lax.dot_general(left, right, (((0,), (0,)), ((), ())), preferred_element_...  105 us
    all_gather x7, waiting for transfers between devices, token_gather(): lax.all_gather(value, BOTH, axis=0, tiled=True, axis_index_groups=self.to...  67 us
    ppermute x35, starting transfers between devices, send(): return lax.ppermute(value, BOTH, pairs)  59.8 us
    dot_general x4, matrix products, contract_cols(): lax.dot_general(left, right, (((1,), (1,)), ((), ())), preferred_element_...  53.5 us
    pallas_call x1, Pallas kernels, attend_back(): pl.pallas_call(functools.partial(attend_back_kernel, rows), grid_spec=plt...  49.6 us
  transfers between devices with their start and end apart: 42, of which 18 were waited for; matrix products, arithmetic and copies ran while one was open for 13% of the time, Pallas kernels for 11%

profile of v2, /device:TPU:1, one launch (start us, length us, event | category | flops | bytes accessed | tf_op | source)
XLA Modules:
  0.0 1476.1 jit_solution(1920078770546852524)
XLA Ops:
  12.1 157.1 %shard_map.237 = (bf16[4096,2048]{1,0:T(8,128)(2,1)}, bf16[2112,768]{1,0:T(8,128)(2,1)}, bf16[256,2048]{1,0:T(8,128)(2,1)}) custom-call(bf16[512,2048]{1,0:T(8,128)(2,1)} %own.1, bf16[528,768]{1,0:T(8,128)(2,1)} %pad_maximum_fusion.5.refs_0_, bf16[256,512]{1,0:T(8,128)(2,1)} %refs_1_.1), custom_call_target="tpu_custom_call" | custom-call | bytes 167772160 | tf_op jit(solution)/shard_map/pallas_call | solution.py:369
  171.4 19.8 %shard_map.238 = (f32[4096,768]{1,0:T(8,128)}, f32[2,4096]{1,0:T(2,128)S(1)}) custom-call(bf16[4096,2048]{1,0:T(8,128)(2,1)} %get-tuple-element.48.left, bf16[2048,768]{1,0:T(8,128)(2,1)S(1)} %bitcast.58), custom_call_target="tpu_custom_call" | custom-call | flops 12884901888 | bytes 29360128 | tf_op jit(solution)/shard_map/pallas_call | solution.py:886
  191.9 16.7 %shard_map.239 = f32[2,4096]{1,0:T(2,128)} custom-call(f32[2,4096]{1,0:T(2,128)} %copy-done.17), custom_call_target="tpu_custom_call" | custom-call | flops 57344 | bytes 16777216 | tf_op jit(solution)/shard_map/pallas_call | solution.py:430
  209.4 7.5 collective-permute-start.2
  220.6 41.5 %collective-permute-done = s32[4096]{0:T(1024)S(1)} collective-permute-done((s32[4096]{0:T(1024)S(1)}, s32[4096]{0:T(1024)S(1)}, u32[]{:S(2)}, u32[]{:S(2)}) %collective-permute-start) | collective-permute-done | bytes 16416 | tf_op jit(solution)/shard_map/ppermute | solution.py:60
  263.1 7.4 fusion.32
  270.5 10.1 shard_map.240
  293.4 31.4 %shard_map.241 = (bf16[4096,256]{1,0:T(8,128)(2,1)S(1)}, f32[2,1,4096]{2,1,0:T(1,128)S(1)}) custom-call(s32[8]{0:T(128)S(1)} %and_select_fusion.2.low, s32[1,4096]{1,0:T(1,128)S(1)} %bitcast.61, bf16[4096,256]{1,0:T(8,128)(2,1)S(1)} %copy-done.25, bf16[4096,256]{1,0:T(8,128)(2,1)S(1)} %copy-done.28, bf16[4096,256]{1,0:T(8,128)(2,1)S(1)} %copy-done.30, ...), custom_call_target="tpu_custom_call" | custom-call | flops 4294967296 | bytes 8388608 | tf_op jit(solution)/shard_map/pallas_call | solution.py:997
  325.2 5.5 collective-permute-start.5
  339.7 6.4 collective-permute-done.3
  350.3 5.2 collective-permute-done.7
  364.3 6.3 multiply_reduce_fusion.6
  380.3 23.5 %collective-permute-done.14 = bf16[512,1024]{1,0:T(8,128)(2,1)S(1)} collective-permute-done((bf16[512,1024]{1,0:T(8,128)(2,1)}, bf16[512,1024]{1,0:T(8,128)(2,1)S(1)}, u32[]{:S(2)}, u32[]{:S(2)}) %collective-permute-start.14) | collective-permute-done | bytes 1048608 | tf_op jit(solution)/shard_map/ppermute | solution.py:60
  403.7 22.4 %collective-permute-done.15 = bf16[512,1024]{1,0:T(8,128)(2,1)S(1)} collective-permute-done((bf16[512,1024]{1,0:T(8,128)(2,1)S(1)}, bf16[512,1024]{1,0:T(8,128)(2,1)S(1)}, u32[]{:S(2)}, u32[]{:S(2)}) %collective-permute-start.15) | collective-permute-done | bytes 1048608 | tf_op jit(solution)/shard_map/ppermute | solution.py:60
  436.1 38.0 %collective-permute-done.16 = bf16[1024,512]{1,0:T(8,128)(2,1)S(1)} collective-permute-done((bf16[1024,512]{1,0:T(8,128)(2,1)}, bf16[1024,512]{1,0:T(8,128)(2,1)S(1)}, u32[]{:S(2)}, u32[]{:S(2)}) %collective-permute-start.16) | collective-permute-done | bytes 1048608 | tf_op jit(solution)/shard_map/ppermute | solution.py:60
  489.7 13.4 collective-permute-done.18
  504.3 10.3 collective-permute-done.19
  515.7 22.6 %convolution_convert_fusion.1 = bf16[2048,2048]{1,0:T(8,128)(2,1)S(1)} fusion(bf16[2048,2048]{1,0:T(8,128)(2,1)} %all-gather.10.cloned.1.call-done, bf16[2048,2048]{1,0:T(8,128)(2,1)} %constant_dynamic-update-slice_fusion.22.refs_2_), kind=kOutput, calls=%fused_computation.39 | convolution fusion | flops 17184063488 | bytes 25165824 | tf_op jit(solution)/shard_map/dot_general | solution.py:1410
  545.6 22.2 %convolution_convert_fusion = bf16[2048,2048]{1,0:T(8,128)(2,1)S(1)} fusion(bf16[2048,2048]{1,0:T(8,128)(2,1)} %all-gather.12.cloned.1.call-done, bf16[2048,2048]{1,0:T(8,128)(2,1)} %constant_dynamic-update-slice_fusion.22.refs_2_), kind=kOutput, calls=%fused_computation.38 | convolution fusion | flops 17184063488 | bytes 25165824 | tf_op jit(solution)/shard_map/dot_general | solution.py:1410
  575.0 117.1 %shard_map.242 = (f32[512,2048]{1,0:T(8,128)}, bf16[512,2048]{1,0:T(8,128)(2,1)}) custom-call(bf16[2048,1024]{1,0:T(8,128)(2,1)} %fusion.refs_0_, bf16[2048,1024]{1,0:T(8,128)(2,1)} %fusion.4.refs_1_, bf16[1024,2048]{1,0:T(8,128)(2,1)} %constant_dynamic-update-slice_fusion.7.refs_2_, bf16[512,2048]{1,0:T(8,128)(2,1)} %refs_3_.1), custom_call_target="tpu_custom_call" | custom-call | flops 17179869184 | bytes 167772160 | tf_op jit(solution)/shard_map/pallas_call | solution.py:841
  705.8 47.7 %all-gather.16.cloned.1.call-done = bf16[2048,2048]{1,0:T(8,128)(2,1)} async-done(((bf16[256,2048]{1,0:T(8,128)(2,1)}), bf16[2048,2048]{1,0:T(8,128)(2,1)}) %all-gather.16.cloned.1.call-update) | async-done | bytes 8388624 | tf_op jit(solution)/shard_map/all_gather | solution.py:77
  753.5 20.7 %fusion.7 = (bf16[2048,1024]{1,0:T(8,128)(2,1)}, bf16[2048,1024]{1,0:T(8,128)(2,1)}) fusion(bf16[2048,2048]{1,0:T(8,128)(2,1)} %copy-done.49, bf16[2048,2048]{1,0:T(8,128)(2,1)} %all-gather.16.cloned.1.call-done, bf16[1024,2048]{1,0:T(8,128)(2,1)} %constant_dynamic-update-slice_fusion.7.refs_2_), kind=kOutput, calls=%fused_computation.20 | convolution fusion | flops 8621391872 | bytes 29360128 | tf_op jit(solution)/shard_map/dot_general | solution.py:158
  774.2 8.4 pad_maximum_fusion.1.refs_1_
  782.6 19.3 %all-gather.14.cloned.1.call-done = bf16[2048,2048]{1,0:T(8,128)(2,1)} async-done(((bf16[256,2048]{1,0:T(8,128)(2,1)}), bf16[2048,2048]{1,0:T(8,128)(2,1)}) %all-gather.14.cloned.1.call-update) | async-done | bytes 8388624 | tf_op jit(solution)/shard_map/all_gather | solution.py:77
  801.9 21.0 %fusion.3 = (bf16[2048,1024]{1,0:T(8,128)(2,1)}, bf16[2048,1024]{1,0:T(8,128)(2,1)}) fusion(bf16[2048,2048]{1,0:T(8,128)(2,1)} %copy-done.48, bf16[2048,2048]{1,0:T(8,128)(2,1)} %all-gather.14.cloned.1.call-done, bf16[1024,2048]{1,0:T(8,128)(2,1)} %constant_dynamic-update-slice_fusion.7.refs_2_), kind=kOutput, calls=%fused_computation.16 | convolution fusion | flops 8621391872 | bytes 29360128 | tf_op jit(solution)/shard_map/dot_general | solution.py:158
  822.9 8.1 pad_maximum_fusion.refs_0_
  831.1 24.8 %fusion.56 = f32[2048,2048]{1,0:T(8,128)} fusion(bf16[2048,2048]{1,0:T(8,128)(2,1)} %all-gather.10.cloned.1.call-done, bf16[2048,1024]{1,0:T(8,128)(2,1)} %get-tuple-element.118, bf16[2048,1024]{1,0:T(8,128)(2,1)} %get-tuple-element.117), kind=kOutput, calls=%fused_computation.214 | convolution fusion | flops 17196646400 | bytes 33554432 | tf_op jit(solution)/shard_map/dot_general | solution.py:152
  855.9 25.0 %add_convert_fusion.refs_3_ = bf16[2048,2048]{1,0:T(8,128)(2,1)} fusion(f32[2048,2048]{1,0:T(8,128)} %fusion.56, bf16[2048,2048]{1,0:T(8,128)(2,1)} %all-gather.12.cloned.1.call-done, bf16[2048,1024]{1,0:T(8,128)(2,1)S(1)} %copy-done.59, bf16[2048,1024]{1,0:T(8,128)(2,1)S(1)} %copy-done.58), kind=kOutput, calls=%fused_computation | convolution fusion | flops 17205035008 | bytes 41943040 | tf_op jit(solution)/shard_map/dot_general | solution.py:152
  880.9 124.5 %shard_map.243 = (f32[512,2048]{1,0:T(8,128)}, bf16[1,1024,2048]{2,1,0:T(8,128)(2,1)}, bf16[512,2048]{1,0:T(8,128)(2,1)}) custom-call(bf16[2048,2048]{1,0:T(8,128)(2,1)} %pad_maximum_fusion.refs_0_, bf16[2048,2048]{1,0:T(8,128)(2,1)} %pad_maximum_fusion.1.refs_1_, bf16[2048,2048]{1,0:T(8,128)(2,1)} %constant_dynamic-update-slice_fusion.22.refs_2_, ...), custom_call_target="tpu_custom_call" | custom-call | flops 34359738368 | bytes 167772160 | tf_op jit(solution)/shard_map/pallas_call | solution.py:841
  1015.4 14.1 fusion.64
  1029.6 11.7 add_convert_fusion.1
  1043.3 6.0 convolution_convert_fusion.4
  1049.4 5.8 convolution_convert_fusion.3
  1071.7 7.5 collective-permute-done.22
  1080.3 8.9 collective-permute-done.24
  1089.2 5.6 collective-permute-start.28
  1094.9 14.8 %collective-permute-done.26 = bf16[512,256]{1,0:T(8,128)(2,1)S(1)} collective-permute-done((bf16[512,256]{1,0:T(8,128)(2,1)S(1)}, bf16[512,256]{1,0:T(8,128)(2,1)S(1)}, u32[]{:S(2)}, u32[]{:S(2)}) %collective-permute-start.26) | collective-permute-done | bytes 262176 | tf_op jit(solution)/shard_map/ppermute | solution.py:60
  1111.8 49.6 %shard_map.244 = (f32[4096,256]{1,0:T(8,128)}, f32[4096,256]{1,0:T(8,128)}, bf16[4096,256]{1,0:T(8,128)(2,1)S(1)}) custom-call(s32[8]{0:T(128)S(1)} %and_select_fusion.high, s32[1,4096]{1,0:T(1,128)S(1)} %bitcast.62, bf16[4096,256]{1,0:T(8,128)(2,1)S(1)} %copy-done.26, bf16[4096,256]{1,0:T(8,128)(2,1)} %copy-done.27, bf16[4096,256]{1,0:T(8,128)(2,1)} %copy-done.29, ...), custom_call_target="tpu_custom_call" | custom-call | flops 12884901888 | bytes 20971520 | tf_op jit(solution)/shard_map/pallas_call | solution.py:1080
  1167.1 9.0 shard_map.245
  1176.8 16.6 %shard_map.246 = f32[2,6144]{1,0:T(2,128)} custom-call(f32[2,6144]{1,0:T(2,128)} %maximum_maximum_fusion.own), custom_call_target="tpu_custom_call" | custom-call | flops 86016 | bytes 16777216 | tf_op jit(solution)/shard_map/pallas_call | solution.py:430
  1200.6 5.3 collective-permute-start.33
  1206.4 6.2 convert_add_fusion.1.rest_0_
  1212.6 11.6 shard_map.247.refs_0_
  1224.2 6.1 fusion.65
  1230.3 5.9 fusion.21
  1236.3 7.7 collective-permute-start.30
  1258.3 17.6 %convolution_convert_fusion.2 = bf16[2048,768]{1,0:T(8,128)(2,1)S(1)} fusion(bf16[4096,2048]{1,0:T(8,128)(2,1)} %get-tuple-element.48.left, bf16[4096,768]{1,0:T(8,128)(2,1)S(1)} %copy-done.50), kind=kOutput, calls=%fused_computation.59 | convolution fusion | flops 12886474752 | bytes 26214400 | tf_op jit(solution)/shard_map/dot_general | solution.py:152
  1278.8 182.9 %shard_map.248 = (bf16[512,2048]{1,0:T(8,128)(2,1)}, bf16[1,1056,768]{2,1,0:T(8,128)(2,1)}, f32[528,768]{1,0:T(8,128)}) custom-call(bf16[4096,768]{1,0:T(8,128)(2,1)} %shard_map.247.refs_0_, bf16[2048,768]{1,0:T(8,128)(2,1)} %bitcast.59, bf16[2112,768]{1,0:T(8,128)(2,1)} %bitcast.67, f32[512,2048]{1,0:T(8,128)} %pad_maximum_fusion.2.refs_3_), custom_call_target="tpu_custom_call" | custom-call | flops 12884901888 | bytes 167772160 | tf_op jit(solution)/shard_map/pallas_call | solution.py:841
  (381 shorter events, 183.5 us)
Async XLA Ops:
  7.2 357.2 %all-gather.8.cloned.1.call-start = ((), (), s32[]{:S(2)}) async-start(), calls=%async_computation | async-start | bytes 9437184 | tf_op jit(solution)/shard_map/all_gather | solution.py:77
  169.3 346.4 %all-gather.10.cloned.1.call-start = ((), (), s32[]{:S(2)}) async-start(), calls=%async_computation.1 | async-start | bytes 9437184 | tf_op jit(solution)/shard_map/all_gather | solution.py:77
  209.4 77.5 %collective-permute-start.2 = (bf16[512,1024]{1,0:T(8,128)(2,1)S(1)}, bf16[512,1024]{1,0:T(8,128)(2,1)S(1)}, u32[]{:S(2)}, u32[]{:S(2)}) collective-permute-start(bf16[512,1024]{1,0:T(8,128)(2,1)S(1)} %copy-done.77), channel_id=1, source_target_pairs={{1,16},{3,18},{5,20},{7,22},{9,24},{11,26},{13,28},{15,30},{16,1},... | collective-permute-start | bytes 3145736 | tf_op jit(solution)/shard_map/ppermute | solution.py:60
  216.9 71.0 %collective-permute-start.1 = (bf16[512,1024]{1,0:T(8,128)(2,1)S(1)}, bf16[512,1024]{1,0:T(8,128)(2,1)}, u32[]{:S(2)}, u32[]{:S(2)}) collective-permute-start(bf16[512,1024]{1,0:T(8,128)(2,1)S(1)} %copy-done.77), channel_id=1, source_target_pairs={{0,16},{1,0},{2,18},{3,2},{4,20},{5,4},{6,22},{7,6},{8,24},{9,8},{... | collective-permute-start | bytes 3145736 | tf_op jit(solution)/shard_map/ppermute | solution.py:60
  217.0 45.1 %collective-permute-start = (s32[4096]{0:T(1024)S(1)}, s32[4096]{0:T(1024)S(1)}, u32[]{:S(2)}, u32[]{:S(2)}) collective-permute-start(s32[4096]{0:T(1024)S(1)} %copy-done.89), channel_id=1, source_target_pairs={{1,16},{3,18},{5,20},{7,22},{9,24},{11,26},{13,28},{15,30},{16,1},... | collective-permute-start | bytes 49160 | tf_op jit(solution)/shard_map/ppermute | solution.py:60
  220.5 478.6 %copy-start.79 = (f32[1,4,4,128]{3,1,2,0:T(4,128)}, f32[1,4,4,128]{3,1,2,0:T(4,128)S(1)}, u32[]{:S(2)}) copy-start(f32[1,4,4,128]{3,1,2,0:T(4,128)S(1)} %copy.50) | copy-start | bytes 24580
  284.6 51.0 %collective-permute-start.13 = (bf16[512,1024]{1,0:T(8,128)(2,1)}, bf16[512,1024]{1,0:T(8,128)(2,1)}, u32[]{:S(2)}, u32[]{:S(2)}) collective-permute-start(bf16[512,1024]{1,0:T(8,128)(2,1)} %param.24), channel_id=1, source_target_pairs={{1,16},{3,18},{5,20},{7,22},{9,24},{11,26},{13,28},{15,30},{16,1},... | collective-permute-start | bytes 3145736 | tf_op jit(solution)/shard_map/ppermute | solution.py:60
  286.5 49.1 %collective-permute-start.12 = (bf16[512,1024]{1,0:T(8,128)(2,1)}, bf16[512,1024]{1,0:T(8,128)(2,1)}, u32[]{:S(2)}, u32[]{:S(2)}) collective-permute-start(bf16[512,1024]{1,0:T(8,128)(2,1)} %param.24), channel_id=1, source_target_pairs={{0,16},{1,0},{2,18},{3,2},{4,20},{5,4},{6,22},{7,6},{8,24},{9,8},{... | collective-permute-start | bytes 3145736 | tf_op jit(solution)/shard_map/ppermute | solution.py:60
  290.2 71.8 %collective-permute-start.11 = (bf16[512,1024]{1,0:T(8,128)(2,1)S(1)}, bf16[512,1024]{1,0:T(8,128)(2,1)S(1)}, u32[]{:S(2)}, u32[]{:S(2)}) collective-permute-start(bf16[512,1024]{1,0:T(8,128)(2,1)S(1)} %get-tuple-element.61.refs_1_), channel_id=1, source_target_pairs={{0,2},{1,3},{2,0},{3,1},{4,6},{5,7},{6,4},{7,5},{8,10},{9,11},{10,... | collective-permute-start | bytes 3145736 | tf_op jit(solution)/shard_map/ppermute | solution.py:60
  290.3 71.7 %collective-permute-start.10 = (bf16[512,1024]{1,0:T(8,128)(2,1)S(1)}, bf16[512,1024]{1,0:T(8,128)(2,1)S(1)}, u32[]{:S(2)}, u32[]{:S(2)}) collective-permute-start(bf16[512,1024]{1,0:T(8,128)(2,1)S(1)} %get-tuple-element.60.refs_0_), channel_id=1, source_target_pairs={{0,2},{1,3},{2,0},{3,1},{4,6},{5,7},{6,4},{7,5},{8,10},{9,11},{10,... | collective-permute-start | bytes 3145736 | tf_op jit(solution)/shard_map/ppermute | solution.py:60
  325.2 23.3 %collective-permute-start.5 = (bf16[512,256]{1,0:T(8,128)(2,1)S(1)}, bf16[512,256]{1,0:T(8,128)(2,1)S(1)}, u32[]{:S(2)}, u32[]{:S(2)}) collective-permute-start(bf16[512,256]{1,0:T(8,128)(2,1)S(1)} %get-tuple-element.142), channel_id=1, source_target_pairs={{0,12},{1,13},{2,14},{3,15},{4,8},{5,9},{6,10},{7,11},{8,4},{9,5},... | collective-permute-start | bytes 786440 | tf_op jit(solution)/shard_map/ppermute | solution.py:60
  335.6 11.1 collective-permute-start.4
  335.6 10.5 collective-permute-start.3
  346.0 2.6 collective-permute-start.6
  346.7 8.7 collective-permute-start.7
  348.5 8.9 collective-permute-start.8
  348.7 13.3 collective-permute-start.9
  371.1 328.0 %copy-start.85 = (f32[256]{0:T(256)}, f32[256]{0:T(256)S(1)}, u32[]{:S(2)}) copy-start(f32[256]{0:T(256)S(1)} %add_rsqrt_fusion.3) | copy-start | bytes 3076
  373.6 325.5 %copy-start.87 = (f32[256]{0:T(256)}, f32[256]{0:T(256)S(1)}, u32[]{:S(2)}) copy-start(f32[256]{0:T(256)S(1)} %add_rsqrt_fusion.4) | copy-start | bytes 3076
  378.0 167.6 %all-gather.12.cloned.1.call-start = ((), (), s32[]{:S(2)}) async-start(), calls=%async_computation.2 | async-start | bytes 9437184 | tf_op jit(solution)/shard_map/all_gather | solution.py:77
  378.7 374.8 %all-gather.16.cloned.1.call-start = ((), (), s32[]{:S(2)}) async-start(), calls=%async_computation.4 | async-start | bytes 9437184 | tf_op jit(solution)/shard_map/all_gather | solution.py:77
  378.7 25.0 %collective-permute-start.14 = (bf16[512,1024]{1,0:T(8,128)(2,1)}, bf16[512,1024]{1,0:T(8,128)(2,1)S(1)}, u32[]{:S(2)}, u32[]{:S(2)}) collective-permute-start(bf16[512,1024]{1,0:T(8,128)(2,1)} %get-tuple-element.64), channel_id=1, source_target_pairs={{0,2},{1,3},{2,0},{3,1},{4,6},{5,7},{6,4},{7,5},{8,10},{9,11},{10,... | collective-permute-start | bytes 3145736 | tf_op jit(solution)/shard_map/ppermute | solution.py:60
  378.8 47.3 %collective-permute-start.15 = (bf16[512,1024]{1,0:T(8,128)(2,1)S(1)}, bf16[512,1024]{1,0:T(8,128)(2,1)S(1)}, u32[]{:S(2)}, u32[]{:S(2)}) collective-permute-start(bf16[512,1024]{1,0:T(8,128)(2,1)S(1)} %get-tuple-element.65), channel_id=1, source_target_pairs={{0,2},{1,3},{2,0},{3,1},{4,6},{5,7},{6,4},{7,5},{8,10},{9,11},{10,... | collective-permute-start | bytes 3145736 | tf_op jit(solution)/shard_map/ppermute | solution.py:60
  426.1 47.9 %collective-permute-start.16 = (bf16[1024,512]{1,0:T(8,128)(2,1)}, bf16[1024,512]{1,0:T(8,128)(2,1)S(1)}, u32[]{:S(2)}, u32[]{:S(2)}) collective-permute-start(bf16[1024,512]{1,0:T(8,128)(2,1)} %param.25), channel_id=1, source_target_pairs={{0,16},{1,0},{2,18},{3,2},{4,20},{5,4},{6,22},{7,6},{8,24},{9,8},{... | collective-permute-start | bytes 3145736 | tf_op jit(solution)/shard_map/ppermute | solution.py:60
  427.1 51.0 %collective-permute-start.17 = (bf16[1024,512]{1,0:T(8,128)(2,1)}, bf16[1024,512]{1,0:T(8,128)(2,1)}, u32[]{:S(2)}, u32[]{:S(2)}) collective-permute-start(bf16[1024,512]{1,0:T(8,128)(2,1)} %param.25), channel_id=1, source_target_pairs={{1,16},{3,18},{5,20},{7,22},{9,24},{11,26},{13,28},{15,30},{16,1},... | collective-permute-start | bytes 3145736 | tf_op jit(solution)/shard_map/ppermute | solution.py:60
  477.9 25.2 %collective-permute-start.18 = (bf16[1024,512]{1,0:T(8,128)(2,1)S(1)}, bf16[1024,512]{1,0:T(8,128)(2,1)S(1)}, u32[]{:S(2)}, u32[]{:S(2)}) collective-permute-start(bf16[1024,512]{1,0:T(8,128)(2,1)S(1)} %get-tuple-element.108), channel_id=1, source_target_pairs={{0,2},{1,3},{2,0},{3,1},{4,6},{5,7},{6,4},{7,5},{8,10},{9,11},{10,... | collective-permute-start | bytes 3145736 | tf_op jit(solution)/shard_map/ppermute | solution.py:60
  480.9 33.7 %collective-permute-start.19 = (bf16[1024,512]{1,0:T(8,128)(2,1)S(1)}, bf16[1024,512]{1,0:T(8,128)(2,1)S(1)}, u32[]{:S(2)}, u32[]{:S(2)}) collective-permute-start(bf16[1024,512]{1,0:T(8,128)(2,1)S(1)} %get-tuple-element.106), channel_id=1, source_target_pairs={{0,2},{1,3},{2,0},{3,1},{4,6},{5,7},{6,4},{7,5},{8,10},{9,11},{10,... | collective-permute-start | bytes 3145736 | tf_op jit(solution)/shard_map/ppermute | solution.py:60
  703.7 98.2 %all-gather.14.cloned.1.call-start = ((), (), s32[]{:S(2)}) async-start(), calls=%async_computation.3 | async-start | bytes 9437184 | tf_op jit(solution)/shard_map/all_gather | solution.py:77
  704.3 519.9 %all-gather.18.cloned.1.call-start = ((), (), s32[]{:S(2)}) async-start(), calls=%async_computation.5 | async-start | bytes 9437184 | tf_op jit(solution)/shard_map/all_gather | solution.py:77
  880.8 124.6 %copy-start.80 = (f32[1,4,4,128]{3,1,2,0:T(4,128)S(1)}, f32[1,4,4,128]{3,1,2,0:T(4,128)}, u32[]{:S(2)}) copy-start(f32[1,4,4,128]{3,1,2,0:T(4,128)} %copy-done.79) | copy-start | bytes 24580
  880.8 124.6 %copy-start.86 = (f32[256]{0:T(256)S(1)}, f32[256]{0:T(256)}, u32[]{:S(2)}) copy-start(f32[256]{0:T(256)} %copy-done.85) | copy-start | bytes 3076
  880.8 124.6 %copy-start.88 = (f32[256]{0:T(256)S(1)}, f32[256]{0:T(256)}, u32[]{:S(2)}) copy-start(f32[256]{0:T(256)} %copy-done.87) | copy-start | bytes 3076
  1011.9 218.4 %all-gather.20.cloned.1.call-start = ((), (), s32[]{:S(2)}) async-start(), calls=%async_computation.6 | async-start | bytes 9437184 | tf_op jit(solution)/shard_map/all_gather | solution.py:77
  1041.5 68.2 %collective-permute-start.27 = (bf16[1024,1024]{1,0:T(8,128)(2,1)S(1)}, bf16[1024,1024]{1,0:T(8,128)(2,1)S(1)}, u32[]{:S(2)}, u32[]{:S(2)}) collective-permute-start(bf16[1024,1024]{1,0:T(8,128)(2,1)S(1)} %constant_dynamic-slice_fusion.4), channel_id=1, source_target_pairs={{0,2},{1,3},{2,0},{3,1},{4,6},{5,7},{6,4},{7,5},{8,10},{9,11},{10,... | collective-permute-start | bytes 6291464 | tf_op jit(solution)/shard_map/ppermute | solution.py:60
  1055.3 39.5 %collective-permute-start.25 = (bf16[512,256]{1,0:T(8,128)(2,1)S(1)}, bf16[512,256]{1,0:T(8,128)(2,1)S(1)}, u32[]{:S(2)}, u32[]{:S(2)}) collective-permute-start(bf16[512,256]{1,0:T(8,128)(2,1)S(1)} %get-tuple-element.135), channel_id=1, source_target_pairs={{0,9},{1,8},{2,11},{3,10},{4,13},{5,12},{6,15},{7,14},{8,1},{9,0},... | collective-permute-start | bytes 786440 | tf_op jit(solution)/shard_map/ppermute | solution.py:60
  1055.8 14.9 %collective-permute-start.20 = (bf16[512,256]{1,0:T(8,128)(2,1)S(1)}, bf16[512,256]{1,0:T(8,128)(2,1)S(1)}, u32[]{:S(2)}, u32[]{:S(2)}) collective-permute-start(bf16[512,256]{1,0:T(8,128)(2,1)S(1)} %get-tuple-element.132), channel_id=1, source_target_pairs={{0,4},{1,5},{2,6},{3,7},{4,0},{5,1},{6,2},{7,3},{8,12},{9,13},{10,... | collective-permute-start | bytes 786440 | tf_op jit(solution)/shard_map/ppermute | solution.py:60
  1056.9 13.8 collective-permute-start.21
  1058.7 20.4 %collective-permute-start.22 = (bf16[512,256]{1,0:T(8,128)(2,1)S(1)}, bf16[512,256]{1,0:T(8,128)(2,1)S(1)}, u32[]{:S(2)}, u32[]{:S(2)}) collective-permute-start(bf16[512,256]{1,0:T(8,128)(2,1)S(1)} %get-tuple-element.134), channel_id=1, source_target_pairs={{0,12},{1,13},{2,14},{3,15},{4,8},{5,9},{6,10},{7,11},{8,4},{9,5},... | collective-permute-start | bytes 786440 | tf_op jit(solution)/shard_map/ppermute | solution.py:60
  1070.7 9.4 collective-permute-start.23
  1070.7 18.5 %collective-permute-start.24 = (bf16[512,256]{1,0:T(8,128)(2,1)S(1)}, bf16[512,256]{1,0:T(8,128)(2,1)S(1)}, u32[]{:S(2)}, u32[]{:S(2)}) collective-permute-start(bf16[512,256]{1,0:T(8,128)(2,1)S(1)} %get-tuple-element.137), channel_id=1, source_target_pairs={{0,5},{1,4},{2,7},{3,6},{4,1},{5,0},{6,3},{7,2},{8,13},{9,12},{10,... | collective-permute-start | bytes 786440 | tf_op jit(solution)/shard_map/ppermute | solution.py:60
  1079.1 30.6 %collective-permute-start.26 = (bf16[512,256]{1,0:T(8,128)(2,1)S(1)}, bf16[512,256]{1,0:T(8,128)(2,1)S(1)}, u32[]{:S(2)}, u32[]{:S(2)}) collective-permute-start(bf16[512,256]{1,0:T(8,128)(2,1)S(1)} %get-tuple-element.130), channel_id=1, source_target_pairs={{0,13},{1,12},{2,15},{3,14},{4,9},{5,8},{6,11},{7,10},{8,5},{9,4},... | collective-permute-start | bytes 786440 | tf_op jit(solution)/shard_map/ppermute | solution.py:60
  1080.1 126.3 %collective-permute-start.29 = (bf16[512,2048]{1,0:T(8,128)(2,1)}, bf16[512,2048]{1,0:T(8,128)(2,1)}, u32[]{:S(2)}, u32[]{:S(2)}) collective-permute-start(bf16[512,2048]{1,0:T(8,128)(2,1)} %get-tuple-element.101), channel_id=1, source_target_pairs={{0,1},{1,17},{2,3},{3,19},{4,5},{5,21},{6,7},{7,23},{8,9},{9,25},{... | collective-permute-start | bytes 6291464 | tf_op jit(solution)/shard_map/ppermute | solution.py:60
  1089.2 117.2 %collective-permute-start.28 = (bf16[512,2048]{1,0:T(8,128)(2,1)}, bf16[512,2048]{1,0:T(8,128)(2,1)}, u32[]{:S(2)}, u32[]{:S(2)}) collective-permute-start(bf16[512,2048]{1,0:T(8,128)(2,1)} %get-tuple-element.102), channel_id=1, source_target_pairs={{1,16},{3,18},{5,20},{7,22},{9,24},{11,26},{13,28},{15,30},{16,1},... | collective-permute-start | bytes 6291464 | tf_op jit(solution)/shard_map/ppermute | solution.py:60
  1200.1 46.2 %collective-permute-start.34 = (bf16[1024,512]{1,0:T(8,128)(2,1)}, bf16[1024,512]{1,0:T(8,128)(2,1)}, u32[]{:S(2)}, u32[]{:S(2)}) collective-permute-start(bf16[1024,512]{1,0:T(8,128)(2,1)} %get-tuple-element.97), channel_id=1, source_target_pairs={{0,1},{1,17},{2,3},{3,19},{4,5},{5,21},{6,7},{7,23},{8,9},{9,25},{... | collective-permute-start | bytes 3145736 | tf_op jit(solution)/shard_map/ppermute | solution.py:60
  1200.6 49.9 %collective-permute-start.33 = (bf16[1024,512]{1,0:T(8,128)(2,1)}, bf16[1024,512]{1,0:T(8,128)(2,1)}, u32[]{:S(2)}, u32[]{:S(2)}) collective-permute-start(bf16[1024,512]{1,0:T(8,128)(2,1)} %get-tuple-element.98), channel_id=1, source_target_pairs={{1,16},{3,18},{5,20},{7,22},{9,24},{11,26},{13,28},{15,30},{16,1},... | collective-permute-start | bytes 3145736 | tf_op jit(solution)/shard_map/ppermute | solution.py:60
  1236.3 17.6 %collective-permute-start.30 = (bf16[256,1024]{1,0:T(8,128)(2,1)S(1)}, bf16[256,1024]{1,0:T(8,128)(2,1)S(1)}, u32[]{:S(2)}, u32[]{:S(2)}) collective-permute-start(bf16[256,1024]{1,0:T(8,128)(2,1)S(1)} %constant_dynamic-slice_fusion.2), channel_id=1, source_target_pairs={{0,2},{1,3},{2,0},{3,1},{4,6},{5,7},{6,4},{7,5},{8,10},{9,11},{10,... | collective-permute-start | bytes 1572872 | tf_op jit(solution)/shard_map/ppermute | solution.py:60
  1254.2 23.7 %collective-permute-start.32 = (bf16[256,512]{1,0:T(8,128)(2,1)S(1)}, bf16[256,512]{1,0:T(8,128)(2,1)S(1)}, u32[]{:S(2)}, u32[]{:S(2)}) collective-permute-start(bf16[256,512]{1,0:T(8,128)(2,1)S(1)} %get-tuple-element.99), channel_id=1, source_target_pairs={{0,1},{1,17},{2,3},{3,19},{4,5},{5,21},{6,7},{7,23},{8,9},{9,25},{... | collective-permute-start | bytes 786440 | tf_op jit(solution)/shard_map/ppermute | solution.py:60
  1254.2 23.6 %collective-permute-start.31 = (bf16[256,512]{1,0:T(8,128)(2,1)S(1)}, bf16[256,512]{1,0:T(8,128)(2,1)S(1)}, u32[]{:S(2)}, u32[]{:S(2)}) collective-permute-start(bf16[256,512]{1,0:T(8,128)(2,1)S(1)} %get-tuple-element.100), channel_id=1, source_target_pairs={{1,16},{3,18},{5,20},{7,22},{9,24},{11,26},{13,28},{15,30},{16,1},... | collective-permute-start | bytes 786440 | tf_op jit(solution)/shard_map/ppermute | solution.py:60
  (87 other events, 1486.7 us)
Sparse Core Ops, SparseCore 0:
  169.4 66.4 all-gather.7
  378.1 45.0 all-gather.9
  424.8 68.9 all-gather.11
  703.8 49.6 all-gather.15
  754.9 46.9 all-gather.13
  1012.1 45.5 all-gather.17
  1059.3 86.4 all-gather.19

commit v3 on v2

--- a/solution.py
+++ b/solution.py
@@ -177,76 +177,54 @@
     )
 
 
-def gather_kernel(plan, pieces, axes, own, *refs):
+def swap_kernel(plan, given, taken, send_sem, recv_sem):
+    zhi, rest, base, core = position(plan)
+    far_row, near_col = (1 - zhi) * plan.half + rest, base + 1 - core
+    barrier = pltpu.get_barrier_semaphore()
+    pl.semaphore_signal(barrier, 1, device_id=(far_row, near_col), device_id_type=MESH)
+    pl.semaphore_wait(barrier, 1)
+
+    @pl.when(zhi != core)
+    def _():
+        remote(given, taken, send_sem, recv_sem, far_row, near_col).start()
+        remote(given, taken, send_sem, recv_sem, far_row, near_col).wait()
+
+    @pl.when(zhi == core)
+    def _():
+        pltpu.make_async_copy(given, taken, recv_sem).start()
+        pltpu.make_async_copy(given, taken, recv_sem).wait()
+
+
+def swap_tokens(plan, value, collective_id):
+    anywhere = pl.BlockSpec(memory_space=pl.ANY)
+    return pl.pallas_call(
+        functools.partial(swap_kernel, plan),
+        in_specs=[anywhere],
+        out_specs=anywhere,
+        out_shape=jax.ShapeDtypeStruct(value.shape, value.dtype),
+        scratch_shapes=[pltpu.SemaphoreType.DMA, pltpu.SemaphoreType.DMA],
+        cost_estimate=pl.CostEstimate(flops=0, bytes_accessed=2**27, transcendentals=0),
+        compiler_params=pltpu.CompilerParams(collective_id=collective_id, has_side_effects=True),
+    )(value)
+
+
+def gather_kernel(plan, axes, *refs):
     count = len(axes)
-    weights, out, wholes, sems = refs[:count], refs[count], refs[count + 1 :][:count], refs[2 * count + 1 :]
-    have_sem, swap_sem, send_sem, recv_sem, near_sem, near_recv_sem = sems[:6]
-    block_sem, block_recv_sem, side_sem, side_recv_sem = sems[6:]
+    weights, wholes, sems = refs[:count], refs[count : 2 * count], refs[2 * count :]
+    block_sem, block_recv_sem, side_sem, side_recv_sem = sems
     half, across = plan.half, plan.across
     zhi, rest, base, core = position(plan)
     xx = base // 2
     row, col = zhi * half + rest, base + core
     far_row, near_col = (1 - zhi) * half + rest, base + 1 - core
-    rows = own.shape[0]
-    part = rows // pieces
     moved, stays = zhi != core, zhi == core
 
     barrier = pltpu.get_barrier_semaphore()
-    side_y = half // 2
-    zlo, y = rest // side_y, rest % side_y
-    base_row = zhi * half
-
     greeted = [(row, near_col), (far_row, col), (far_row, near_col)]
-    greeted += [(base_row + (1 - zlo) * side_y + y, col)]
-    greeted += [(base_row + zlo * side_y + (y + step) % side_y, col) for step in range(1, side_y)]
     greeted += [(row, (xx + step) % across * 2 + core) for step in range(1, across)]
     for device in greeted:
         pl.semaphore_signal(barrier, 1, device_id=device, device_id_type=MESH)
     pl.semaphore_wait(barrier, len(greeted))
-
-    def lines(block, h):
-        return pl.ds(pl.multiple_of(block * rows + h * part, part), part)
-
-    def entry_near(h):
-        source = own.at[pl.ds(h * part, part)]
-        return pltpu.make_async_copy(
-            source, out.at[lines(core * half + rest, h)], have_sem.at[h]
-        )
-
-    def entry_far(h):
-        return remote(
-            own.at[pl.ds(h * part, part)],
-            out.at[lines(zhi * half + rest, h)],
-            swap_sem.at[h],
-            have_sem.at[h],
-            far_row,
-            near_col,
-        )
-
-    def block_at(over, step):
-        other = zlo + over * (1 - 2 * zlo)
-        return core * half + other * side_y + (y + side_y - step) % side_y
-
-    def sibling(over, step, h):
-        at = out.at[lines(block_at(over, step), h)]
-        return remote(
-            at,
-            at,
-            near_sem.at[over, step, h],
-            near_recv_sem.at[over, step, h],
-            row,
-            near_col,
-        )
-
-    def along_z(h):
-        at = out.at[lines(block_at(0, 0), h)]
-        chip = base_row + (1 - zlo) * side_y + y
-        return remote(at, at, send_sem.at[0, 0, h], recv_sem.at[1, 0, h], chip, col)
-
-    def along_y(over, step, h):
-        at = out.at[lines(block_at(over, 0), h)]
-        chip = base_row + zlo * side_y + (y + step) % side_y
-        return remote(at, at, send_sem.at[over, step, h], recv_sem.at[over, step, h], chip, col)
 
     def place(index, other, j):
         axis = axes[index]
@@ -276,70 +254,23 @@
             at, at, side_sem.at[index, step - 1, j], side_recv_sem.at[index, step - 1, j], row, other
         )
 
-    @pl.when(moved)
-    def _():
-        for h in range(pieces):
-            entry_far(h).start()
-
-    @pl.when(stays)
-    def _():
-        for h in range(pieces):
-            entry_near(h).start()
-        for index in range(count):
-            block_keep(index, core).start()
-
-    for h in range(pieces):
+    for index in range(count):
 
         @pl.when(moved)
         def _():
-            entry_far(h).wait_recv()
+            block_send(index, 0, row, near_col).start()
+            block_send(index, 1, far_row, near_col).start()
 
         @pl.when(stays)
         def _():
-            entry_near(h).wait()
-
-        along_z(h).start()
-        for step in range(1, side_y):
-            along_y(0, step, h).start()
-        sibling(0, 0, h).start()
-
-    for h in range(pieces):
-        along_z(h).wait_recv()
-        for step in range(1, side_y):
-            along_y(1, step, h).start()
-        sibling(1, 0, h).start()
-        sibling(0, 0, h).wait_recv()
-        if h == pieces // 2:
-            for index in range(count):
-
-                @pl.when(moved)
-                def _():
-                    block_send(index, 0, row, near_col).start()
-                    block_send(index, 1, far_row, near_col).start()
-
-                @pl.when(stays)
-                def _():
-                    block_send(index, 0, far_row, col).start()
-
-    for over in range(2):
-        for h in range(pieces):
-            for step in range(1, side_y):
-                along_y(over, step, h).wait_recv()
-                sibling(over, step, h).start()
+            block_keep(index, core).start()
+            block_send(index, 0, far_row, col).start()
+
     for index in range(count):
         for j in range(2):
             block_keep(index, j).wait()
             for step in range(1, across):
                 side(index, step, j).start()
-    for h in range(pieces):
-        along_z(h).wait_send()
-        for over in range(2):
-            sibling(over, 0, h).wait_send()
-            if over:
-                sibling(over, 0, h).wait_recv()
-            for step in range(1, side_y):
-                sibling(over, step, h).wait()
-                along_y(over, step, h).wait_send()
     for index in range(count):
         for j in range(2):
             for step in range(1, across):
@@ -354,44 +285,28 @@
         def _():
             block_send(index, 0, far_row, col).wait_send()
 
-    @pl.when(moved)
-    def _():
-        for h in range(pieces):
-            entry_far(h).wait_send()
-
-
-def swap_gather(plan, own, weights, axes, collective_id):
-    half, count = plan.half, len(weights)
-    pieces = 4
+
+def gather_weights(plan, weights, axes, collective_id):
+    count = len(weights)
     dma = pltpu.SemaphoreType.DMA
-    shape = (own.shape[0] * plan.rows, own.shape[1])
     anywhere = pl.BlockSpec(memory_space=pl.ANY)
     return pl.pallas_call(
-        functools.partial(gather_kernel, plan, pieces, axes),
-        in_specs=[anywhere] * (1 + count),
-        out_specs=[anywhere] * (1 + count),
-        out_shape=[jax.ShapeDtypeStruct(shape, own.dtype)]
-        + [
+        functools.partial(gather_kernel, plan, axes),
+        in_specs=[anywhere] * count,
+        out_specs=[anywhere] * count,
+        out_shape=[
             jax.ShapeDtypeStruct(grow(weight.shape, axis, plan.cols), weight.dtype)
             for weight, axis in zip(weights, axes, strict=True)
         ],
         scratch_shapes=[
-            dma((pieces,)),
-            dma((pieces,)),
-            dma((2, half // 2, pieces)),
-            dma((2, half // 2, pieces)),
-            dma((2, half // 2, pieces)),
-            dma((2, half // 2, pieces)),
             dma((count, 2)),
             dma((count, 2)),
             dma((count, plan.across - 1, 2)),
             dma((count, plan.across - 1, 2)),
         ],
-        cost_estimate=pl.CostEstimate(
-            flops=0, bytes_accessed=20 * shape[0] * shape[1], transcendentals=0
-        ),
+        cost_estimate=pl.CostEstimate(flops=0, bytes_accessed=2**28, transcendentals=0),
         compiler_params=pltpu.CompilerParams(collective_id=collective_id, has_side_effects=True),
-    )(own, *weights)
+    )(*weights)
 
 
 def sum_kernel(plan, own, out, landed, send_sem, recv_sem):
@@ -578,49 +493,6 @@
         for step in range(1, across):
             block(index, step).start()
 
-    def body(unit, carry):
-        slot = unit % 2
-        before = unit - 1
-
-        @pl.when(unit + 1 < 2 * half)
-        def _():
-            start(load(unit + 1, 0, 1 - slot))
-
-        @pl.when(unit < 2 * half)
-        def _():
-            start(load(unit, 1, 1 - slot))
-            load(unit, 0, slot)[0][1].wait()
-
-            @pl.when(unit >= 2)
-            def _():
-                near(unit - 2, slot).wait_send()
-
-            @pl.loop(0, width // tile)
-            def _(n):
-                value = product(loaded[slot, 0], columns(n))
-                near_out[slot, :, columns(n)] = value.astype(near_out.dtype)
-
-            near(unit, slot).start()
-
-        @pl.when(unit >= 1)
-        def _():
-            load(before, 1, slot)[0][1].wait()
-            near(before, 1 - slot).wait_recv()
-
-            @pl.loop(0, width // tile)
-            def _(n):
-                value = product(loaded[slot, 1], columns(n))
-                value = value + near_in[before, :, columns(n)].astype(jnp.float32)
-                far_out[before, :, columns(n)] = value.astype(far_out.dtype)
-
-            @pl.when(split(before)[5] > 0)
-            def _():
-                far(before).start()
-
-        return carry
-
-    lax.fori_loop(0, 2 * half + 1, body, 0)
-
     def line_sum(h, aside):
         first = side_y if h == 0 else 2
         second = half // first
@@ -632,12 +504,59 @@
             value = value + far_in[unit].astype(jnp.float32)
         return value
 
-    for h in range(2):
+    def second_stage(h):
         second = 2 if h == 0 else side_y
         for aside in range(second - 1, 0, -1):
             unit = (h + 1) * half - 1 - aside
             far_out[unit] = line_sum(h, aside).astype(far_out.dtype)
             far(unit).start()
+
+    def body(unit, carry):
+        slot = unit % 2
+        before = unit - 1
+
+        @pl.when(unit + 1 < 2 * half)
+        def _():
+            start(load(unit + 1, 0, 1 - slot))
+
+        @pl.when(unit < 2 * half)
+        def _():
+            start(load(unit, 1, 1 - slot))
+            load(unit, 0, slot)[0][1].wait()
+
+            @pl.when(unit >= 2)
+            def _():
+                near(unit - 2, slot).wait_send()
+
+            @pl.loop(0, width // tile)
+            def _(n):
+                value = product(loaded[slot, 0], columns(n))
+                near_out[slot, :, columns(n)] = value.astype(near_out.dtype)
+
+            near(unit, slot).start()
+
+        @pl.when(unit >= 1)
+        def _():
+            load(before, 1, slot)[0][1].wait()
+            near(before, 1 - slot).wait_recv()
+
+            @pl.loop(0, width // tile)
+            def _(n):
+                value = product(loaded[slot, 1], columns(n))
+                value = value + near_in[before, :, columns(n)].astype(jnp.float32)
+                far_out[before, :, columns(n)] = value.astype(far_out.dtype)
+
+            @pl.when(split(before)[5] > 0)
+            def _():
+                far(before).start()
+
+            @pl.when(unit == half + half // 2)
+            def _():
+                second_stage(0)
+
+        return carry
+
+    lax.fori_loop(0, 2 * half + 1, body, 0)
 
     def total(h):
         value = line_sum(h, 0)
@@ -682,6 +601,7 @@
                 swap_near(h).start()
 
             if h == 0:
+                second_stage(1)
                 finish_sum()
 
         for h in range(2):
@@ -695,6 +615,7 @@
                 swap_near(h).wait()
 
     else:
+        second_stage(1)
         for h in range(2):
             out[h * part : (h + 1) * part, :] = total(h)
         for index in range(count):
@@ -855,6 +776,37 @@
     )(*lefts, weight, *grads, *([residual] if last else []), *([swapped] if swaps else []))
 
 
+def unit_grad_kernel(left, weight, both, out):
+    width = weight.shape[0]
+    grad = contract_cols(left[...], weight[...])
+    gate = both[:, :width].astype(jnp.float32)
+    up = both[:, width:].astype(jnp.float32)
+    sigmoid = jax.nn.sigmoid(gate)
+    scaled = grad * sigmoid
+    out[:, :width] = (scaled * up * (1.0 + gate * (1.0 - sigmoid))).astype(out.dtype)
+    out[:, width:] = (scaled * gate).astype(out.dtype)
+
+
+def unit_grad(left, weight, both):
+    seq_len, depth = left.shape
+    rows = min(256, seq_len)
+    width = weight.shape[0]
+    wide = pl.BlockSpec((rows, 2 * width), lambda i: (i, 0))
+    return pl.pallas_call(
+        unit_grad_kernel,
+        grid=(seq_len // rows,),
+        in_specs=[pl.BlockSpec((rows, depth), lambda i: (i, 0)), full(width, depth), wide],
+        out_specs=wide,
+        out_shape=jax.ShapeDtypeStruct((seq_len, 2 * width), jnp.bfloat16),
+        cost_estimate=pl.CostEstimate(
+            flops=2 * seq_len * depth * width,
+            bytes_accessed=2 * seq_len * (depth + 4 * width),
+            transcendentals=seq_len * width,
+        ),
+        compiler_params=pltpu.CompilerParams(vmem_limit_bytes=40 * 2**20),
+    )(left, weight, both)
+
+
 def full(rows, width):
     return pl.BlockSpec((rows, width), lambda *_: (0, 0))
 
@@ -867,41 +819,44 @@
     return jnp.transpose(jnp.broadcast_to(row_vector, (width, row_vector.shape[1])))
 
 
-def project_kernel(head_size, left, weight, proj, squares):
-    value = jnp.dot(left[...], weight[...], preferred_element_type=jnp.float32)
-    proj[...] = value
+def project_kernel(head_size, first, second, weight, proj, squares):
     width = proj.shape[1] // 3
-    for place in range(2):
-        total = None
-        for start in range(place * width, (place + 1) * width, head_size):
-            part = value[:, start : start + head_size] ** 2
-            total = part if total is None else total + part
-        squares[place : place + 1, :] = jnp.sum(jnp.transpose(total), axis=0, keepdims=True)
-
-
-def project(left, weight, head_size):
-    seq_len, depth = left.shape
-    rows = min(512, seq_len)
+    rows = first.shape[0]
+    for chunk, left in enumerate((first, second)):
+        at = slice(chunk * rows, (chunk + 1) * rows)
+        value = jnp.dot(left[...], weight[...], preferred_element_type=jnp.float32)
+        proj[at, :] = value
+        for place in range(2):
+            total = None
+            for start in range(place * width, (place + 1) * width, head_size):
+                part = value[:, start : start + head_size] ** 2
+                total = part if total is None else total + part
+            squares[place : place + 1, at] = jnp.sum(jnp.transpose(total), axis=0, keepdims=True)
+
+
+def project(lefts, weight, head_size, own_tokens):
+    rows, depth = lefts[0].shape
     wide = weight.shape[1]
+    part = pl.BlockSpec((own_tokens // 2, depth), lambda i: (i, 0))
     return pl.pallas_call(
         functools.partial(project_kernel, head_size),
-        grid=(seq_len // rows,),
-        in_specs=[pl.BlockSpec((rows, depth), lambda i: (i, 0)), full(depth, wide)],
+        grid=(2 * rows // own_tokens,),
+        in_specs=[part, part, full(depth, wide)],
         out_specs=[
-            pl.BlockSpec((rows, wide), lambda i: (i, 0)),
-            pl.BlockSpec((2, rows), lambda i: (0, i)),
+            pl.BlockSpec((own_tokens, wide), lambda i: (i, 0)),
+            pl.BlockSpec((2, own_tokens), lambda i: (0, i)),
         ],
         out_shape=[
-            jax.ShapeDtypeStruct((seq_len, wide), jnp.float32),
-            jax.ShapeDtypeStruct((2, seq_len), jnp.float32),
+            jax.ShapeDtypeStruct((2 * rows, wide), jnp.float32),
+            jax.ShapeDtypeStruct((2, 2 * rows), jnp.float32),
         ],
         cost_estimate=pl.CostEstimate(
-            flops=2 * seq_len * depth * wide,
-            bytes_accessed=2 * seq_len * depth + 4 * seq_len * wide,
+            flops=4 * rows * depth * wide,
+            bytes_accessed=4 * rows * depth + 8 * rows * wide,
             transcendentals=0,
         ),
         compiler_params=pltpu.CompilerParams(vmem_limit_bytes=40 * 2**20),
-    )(left, weight)
+    )(*lefts, weight)
 
 
 def prepare_kernel(
@@ -1313,8 +1268,14 @@
         return jnp.pad(vector, (0, extra * wide - small_size)).reshape(extra, wide)
 
     own_weight = jnp.concatenate([qkv_own, lines(small_own)], axis=0)
-    gathered_x, both, out_rows = swap_gather(
-        plan, layer_input, (own_weight, w_out), (0, 1), 1
+    nearby = plan.send(
+        segments, lambda z, r, x, c: (z, r, x, 1 - c) if z == c else None
+    )
+    segments = jnp.where(plan.same(), segments, nearby)
+    own_x = swap_tokens(plan, after(layer_input, segments), 1)
+    gathered_x = [plan.token_gather(chunk_of(own_x, k)) for k in chunks]
+    both, out_rows, down_rows = gather_weights(
+        plan, (after(own_weight, own_x), w_out, w_down), (0, 1, 1), 7
     )
     both = both.reshape(plan.cols, own_depth + extra, wide)
     proj_weight = both[:, :own_depth].reshape(-1, wide)
@@ -1323,8 +1284,6 @@
         value.reshape(1, -1) for value in jnp.split(small, cuts, axis=1)
     )
 
-    own_x = lax.dynamic_slice_in_dim(gathered_x, mine * own_tokens, own_tokens)
-    segments = plan.swap(segments)
     out_full = plan.token_gather(out_rows)
     ff_width = w_gate.shape[1]
 
@@ -1349,7 +1308,7 @@
     high = (ends - 1) // tile
     first_row = first[None, :]
 
-    proj, squares = project(gathered_x, proj_weight, head_size)
+    proj, squares = project(gathered_x, proj_weight, head_size, own_tokens)
     invs = lax.rsqrt(group_sum(plan, squares, 5) / model_width + EPS)
     query_inv, key_inv = invs[:1], invs[1:]
     query, key, value = prepare(
@@ -1360,7 +1319,6 @@
     attn_out, log_sum = attend(
         low, first_row, query, key, value, head_size, tile, gate_pair
     )
-    post_depth = w_out.shape[1]
 
     attn_tokens = jnp.zeros((own_tokens, model_width), bf16)
     for flip in range(rows):
@@ -1374,7 +1332,6 @@
     attn_tokens, *others = lax.optimization_barrier((attn_tokens, *gate_pieces, *up_pair))
     gate_pieces, up_pair = zip(places, others[:-2], strict=True), others[-2:]
     up_pieces = plan.weight_pieces(up_pair)
-    down_pair = plan.weight_pair(after(w_down, *(piece for _, piece in up_pieces)))
     ff_weight = join(
         (model_width, 2 * ff_width),
         [
@@ -1383,11 +1340,6 @@
             for c, piece in pieces
         ],
     )
-    down_rows = join(
-        (ff_width, model_width),
-        [(0, c * post_depth, piece) for c, piece in plan.weight_pieces(down_pair)],
-    )
-
     def normed(value):
         inv = lax.rsqrt(jnp.mean(value * value, axis=-1, keepdims=True) + EPS)
         return inv, value * inv
@@ -1403,14 +1355,17 @@
         attn_inv.append(inv)
         attn_hat.append(hat)
         hidden.append(chunk_of(own_x, k).astype(f32) + hat * attn_scale)
-        gathered_h.append(plan.token_gather(hidden[k].astype(bf16)))
-
-    gate, up, activated = [], [], []
+        low = hidden[k].astype(bf16)
+        if k:
+            low = after(low, *(piece for _, piece in up_pieces))
+        gathered_h.append(plan.token_gather(low))
+
+    gate_up, activated = [], []
     for k in chunks:
         both = jnp.dot(gathered_h[k], ff_weight, preferred_element_type=f32).astype(bf16)
-        gate.append(both[:, :ff_width])
-        up.append(both[:, ff_width:])
-        activated.append((jax.nn.silu(gate[k].astype(f32)) * up[k].astype(f32)).astype(bf16))
+        gate_up.append(both)
+        gate, up = both[:, :ff_width].astype(f32), both[:, ff_width:].astype(f32)
+        activated.append((jax.nn.silu(gate) * up).astype(bf16))
     mlp_out, own_cot = multiply_scatter(
         plan, activated, down_rows, False, 2, swapped=cotangent
     )
@@ -1426,12 +1381,7 @@
 
     ff_grad = []
     for k in chunks:
-        act_part = contract_cols(shard_rows[k], down_rows)
-        gate_val, up_val = gate[k].astype(f32), up[k].astype(f32)
-        gate_sigmoid = jax.nn.sigmoid(gate_val)
-        gate_grad = act_part * up_val * gate_sigmoid * (1.0 + gate_val * (1.0 - gate_sigmoid))
-        up_grad = act_part * gate_val * gate_sigmoid
-        ff_grad.append(jnp.concatenate([gate_grad, up_grad], axis=1).astype(bf16))
+        ff_grad.append(unit_grad(shard_rows[k], down_rows, gate_up[k]))
     down_grad = sum(contract_rows(activated[k], shard_rows[k]) for k in chunks).astype(bf16)
     ff_weight_grad = sum(contract_rows(gathered_h[k], ff_grad[k]) for k in chunks).astype(bf16)
     hidden_grad_mlp, ff_blocks, layer_output = multiply_scatter(
@@ -1500,7 +1450,10 @@
         *shared, value_grad, dots, head_size, model_width, (ff_sum,)
     )
     proj_grad_all = after(proj_grad_all, out_sum)
-    proj_weight_grad = contract_rows(gathered_x, proj_grad_all).astype(bf16)
+    halves = proj_grad_all.reshape(rows, 2, part, wide)
+    proj_weight_grad = sum(
+        contract_rows(gathered_x[k], halves[:, k].reshape(-1, wide)) for k in chunks
+    ).astype(bf16)
     small = jnp.concatenate(
         [
             gain_sums[0].reshape(plan.cols, -1),

time: 1480 us -> 1420 us (0.959)
  matrix products: 212 us -> 164 us
  Pallas kernels: 746 us -> 794 us
  waiting for transfers between devices: 277 us -> 239 us
  other arithmetic: 97 us -> 74.9 us
  local copies, waits for them, and re-layouts: 67.5 us -> 83.1 us
  starting transfers between devices: 60.1 us -> 44.6 us
    pallas_call x2 -> x5, Pallas kernels: 177 us -> 235 us  [the longest x1 139 us: gather_weights(): pl.pallas_call(functools.partial(gather_kernel, plan, axes), in_specs=[an...]
    dot_general x4 -> x2, matrix products: 53.5 us -> 4.96 us  [contract_cols(): lax.dot_general(left, right, (((1,), (1,)), ((), ())), preferred_element_...]
    ppermute x35 -> x31, waiting for transfers between devices: 208 us -> 165 us  [send(): return lax.ppermute(value, BOTH, pairs)]
    concatenate x2 -> x0, other arithmetic: 16.6 us -> none  [body(): ff_grad.append(jnp.concatenate([gate_grad, up_grad], axis=1).astype(bf16))]
    ppermute x35 -> x31, starting transfers between devices: 59.8 us -> 44.3 us  [send(): return lax.ppermute(value, BOTH, pairs)]
    unnamed x194 -> x180, local copies, waits for them, and re-layouts: 33 us -> 45.6 us
    all_gather x7 -> x9, waiting for transfers between devices: 67 us -> 71.8 us  [token_gather(): lax.all_gather(value, BOTH, axis=0, tiled=True, axis_index_groups=self.to...]
    dot_general x7 -> x8, matrix products: 105 us -> 105 us  [contract_rows(): lax.dot_general(left, right, (((0,), (0,)), ((), ())), preferred_element_...]
  transfers between devices with their start and end apart: 42 -> 40, of which waited for: 18 -> 16; matrix products, arithmetic and copies ran while one was open for 13% -> 12% of each run, Pallas kernels for 11% -> 22%
where the time goes in v3:
time: 1420 us
  Pallas kernels  794 us (56%)
  waiting for transfers between devices  239 us (17%)
  matrix products  164 us (12%)
  local copies, waits for them, and re-layouts  83.1 us (6%)
  other arithmetic  74.9 us (5%)
  starting transfers between devices  44.6 us (3%)
  between operations  15.7 us (1%)
    pallas_call x3, Pallas kernels, multiply_scatter(): pl.pallas_call(functools.partial(scatter_kernel, plan, len(lefts), axes,...  424 us
    ppermute x31, waiting for transfers between devices, send(): return lax.ppermute(value, BOTH, pairs)  165 us
    pallas_call x1, Pallas kernels, gather_weights(): pl.pallas_call(functools.partial(gather_kernel, plan, axes), in_specs=[an...  139 us
    dot_general x8, matrix products, contract_rows(): lax.dot_general(left, right, (((0,), (0,)), ((), ())), preferred_element_...  105 us
    all_gather x9, waiting for transfers between devices, token_gather(): lax.all_gather(value, BOTH, axis=0, tiled=True, axis_index_groups=self.to...  71.8 us
    pallas_call x1, Pallas kernels, attend_back(): pl.pallas_call(functools.partial(attend_back_kernel, rows), grid_spec=plt...  51.6 us
    pallas_call x1, Pallas kernels, swap_tokens(): pl.pallas_call(functools.partial(swap_kernel, plan), in_specs=[anywhere],...  50.2 us
    unnamed x180, local copies, waits for them, and re-layouts  45.6 us
  transfers between devices with their start and end apart: 40, of which 16 were waited for; matrix products, arithmetic and copies ran while one was open for 12% of the time, Pallas kernels for 22%

profile of v3, /device:TPU:1, one launch (start us, length us, event | category | flops | bytes accessed | tf_op | source)
XLA Modules:
  0.0 1415.6 jit_solution(4171737052384284971)
XLA Ops:
  10.5 50.2 %shard_map.237 = bf16[512,2048]{1,0:T(8,128)(2,1)} custom-call(bf16[512,2048]{1,0:T(8,128)(2,1)} %given), custom_call_target="tpu_custom_call" | custom-call | bytes 134217728 | tf_op jit(solution)/shard_map/pallas_call | solution.py:200
  66.0 139.3 %shard_map.238 = (bf16[2112,768]{1,0:T(8,128)(2,1)}, bf16[256,2048]{1,0:T(8,128)(2,1)}, bf16[1024,2048]{1,0:T(8,128)(2,1)}) custom-call(bf16[528,768]{1,0:T(8,128)(2,1)} %pad_maximum_fusion.3.refs_0_, bf16[256,512]{1,0:T(8,128)(2,1)} %refs_1_.1, bf16[1024,512]{1,0:T(8,128)(2,1)} %refs_2_.1), custom_call_target="tpu_custom_call" | custom-call | bytes 268435456 | tf_op jit(solution)/shard_map/pallas_call | solution.py:293
  211.9 9.3 fusion.22
  223.3 4.3 copy-done.21
  227.6 17.4 %shard_map.239 = (f32[4096,768]{1,0:T(8,128)}, f32[2,4096]{1,0:T(2,128)S(1)}) custom-call(bf16[2048,2048]{1,0:T(8,128)(2,1)S(1)} %copy-done.21, bf16[2048,2048]{1,0:T(8,128)(2,1)} %all-gather.12.cloned.1.call-done.second, bf16[2048,768]{1,0:T(8,128)(2,1)S(1)} %bitcast.62), custom_call_target="tpu_custom_call" | custom-call | flops 12884901888 | bytes 29360128 | tf_op jit(solution)/shard_map/pallas_call | solution.py:841
  245.6 9.7 shard_map.240
  261.2 8.8 shard_map.241
  273.7 54.8 %collective-permute-done.2 = bf16[512,1024]{1,0:T(8,128)(2,1)S(1)} collective-permute-done((bf16[512,1024]{1,0:T(8,128)(2,1)S(1)}, bf16[512,1024]{1,0:T(8,128)(2,1)S(1)}, u32[]{:S(2)}, u32[]{:S(2)}) %collective-permute-start.2) | collective-permute-done | bytes 1048608 | tf_op jit(solution)/shard_map/ppermute | solution.py:60
  332.0 32.9 %shard_map.242 = (bf16[4096,256]{1,0:T(8,128)(2,1)S(1)}, f32[2,1,4096]{2,1,0:T(1,128)S(1)}) custom-call(s32[8]{0:T(128)S(1)} %and_select_fusion.2.low, s32[1,4096]{1,0:T(1,128)S(1)} %bitcast.64, bf16[4096,256]{1,0:T(8,128)(2,1)S(1)} %get-tuple-element.55.query, bf16[4096,256]{1,0:T(8,128)(2,1)S(1)} %get-tuple-element.56.key, ...), custom_call_target="tpu_custom_call" | custom-call | flops 4294967296 | bytes 8388608 | tf_op jit(solution)/shard_map/pallas_call | solution.py:952
  372.5 9.2 collective-permute-done.3
  385.7 4.9 collective-permute-done.7
  391.7 5.7 collective-permute-done.9
  399.7 6.3 multiply_reduce_fusion.6
  412.6 23.5 %collective-permute-done.14 = bf16[512,1024]{1,0:T(8,128)(2,1)} collective-permute-done((bf16[512,1024]{1,0:T(8,128)(2,1)}, bf16[512,1024]{1,0:T(8,128)(2,1)}, u32[]{:S(2)}, u32[]{:S(2)}) %collective-permute-start.14) | collective-permute-done | bytes 1048608 | tf_op jit(solution)/shard_map/ppermute | solution.py:60
  436.1 22.5 %collective-permute-done.15 = bf16[512,1024]{1,0:T(8,128)(2,1)} collective-permute-done((bf16[512,1024]{1,0:T(8,128)(2,1)}, bf16[512,1024]{1,0:T(8,128)(2,1)}, u32[]{:S(2)}, u32[]{:S(2)}) %collective-permute-start.15) | collective-permute-done | bytes 1048608 | tf_op jit(solution)/shard_map/ppermute | solution.py:60
  458.7 4.4 broadcast_in_dim.48
  474.4 22.9 %convolution_convert_fusion.1.both = bf16[2048,2048]{1,0:T(8,128)(2,1)S(1)} fusion(bf16[2048,2048]{1,0:T(8,128)(2,1)} %all-gather.16.cloned.1.call-done, bf16[2048,2048]{1,0:T(8,128)(2,1)} %constant_dynamic-update-slice_fusion.18.refs_2_), kind=kOutput, calls=%fused_computation.19 | convolution fusion | flops 17184063488 | bytes 25165824 | tf_op jit(solution)/shard_map/dot_general | solution.py:1365
  500.6 4.0 fusion.10.refs_0_
  505.2 22.2 %convolution_convert_fusion.both = bf16[2048,2048]{1,0:T(8,128)(2,1)S(1)} fusion(bf16[2048,2048]{1,0:T(8,128)(2,1)} %all-gather.18.cloned.1.call-done, bf16[2048,2048]{1,0:T(8,128)(2,1)} %constant_dynamic-update-slice_fusion.18.refs_2_), kind=kOutput, calls=%fused_computation.18 | convolution fusion | flops 17184063488 | bytes 25165824 | tf_op jit(solution)/shard_map/dot_general | solution.py:1365
  527.4 4.6 fusion.9.refs_1_
  531.9 119.5 %shard_map.243 = (f32[512,2048]{1,0:T(8,128)}, bf16[512,2048]{1,0:T(8,128)(2,1)}) custom-call(bf16[2048,1024]{1,0:T(8,128)(2,1)} %fusion.10.refs_0_, bf16[2048,1024]{1,0:T(8,128)(2,1)} %fusion.9.refs_1_, bf16[1024,2048]{1,0:T(8,128)(2,1)} %get-tuple-element.70.refs_2_.weight, bf16[512,2048]{1,0:T(8,128)(2,1)} %refs_3_.1), custom_call_target="tpu_custom_call" | custom-call | flops 17179869184 | bytes 167772160 | tf_op jit(solution)/shard_map/pallas_call | solution.py:762
  658.4 4.8 fusion.18
  666.7 42.4 %all-gather.22.cloned.1.call-done.left = bf16[2048,2048]{1,0:T(8,128)(2,1)} async-done(((bf16[256,2048]{1,0:T(8,128)(2,1)}), bf16[2048,2048]{1,0:T(8,128)(2,1)}) %all-gather.22.cloned.1.call-update) | async-done | bytes 8388624 | tf_op jit(solution)/shard_map/all_gather | solution.py:77
  711.3 14.3 %shard_map.245.refs_1_ = bf16[2048,2048]{1,0:T(8,128)(2,1)S(1)} custom-call(bf16[2048,2048]{1,0:T(8,128)(2,1)} %all-gather.22.cloned.1.call-done.left, bf16[1024,2048]{1,0:T(8,128)(2,1)S(1)} %copy-done.22, bf16[2048,2048]{1,0:T(8,128)(2,1)} %copy-done.48), custom_call_target="tpu_custom_call" | custom-call | flops 8589934592 | bytes 25165824 | tf_op jit(solution)/shard_map/pallas_call | solution.py:795
  729.0 28.8 %all-gather.20.cloned.1.call-done.left = bf16[2048,2048]{1,0:T(8,128)(2,1)} async-done(((bf16[256,2048]{1,0:T(8,128)(2,1)}), bf16[2048,2048]{1,0:T(8,128)(2,1)}) %all-gather.20.cloned.1.call-update) | async-done | bytes 8388624 | tf_op jit(solution)/shard_map/all_gather | solution.py:77
  759.9 13.8 shard_map.244.refs_0_
  776.9 21.9 %fusion.55 = f32[2048,2048]{1,0:T(8,128)} fusion(bf16[2048,2048]{1,0:T(8,128)(2,1)} %all-gather.16.cloned.1.call-done, bf16[2048,2048]{1,0:T(8,128)(2,1)S(1)} %shard_map.244.refs_0_), kind=kOutput, calls=%fused_computation.197 | convolution fusion | flops 17179869184 | bytes 33554432 | tf_op jit(solution)/shard_map/dot_general | solution.py:152
  798.8 27.3 %add_convert_fusion.refs_3_ = bf16[2048,2048]{1,0:T(8,128)(2,1)} fusion(f32[2048,2048]{1,0:T(8,128)} %fusion.55, bf16[2048,2048]{1,0:T(8,128)(2,1)} %all-gather.18.cloned.1.call-done, bf16[2048,2048]{1,0:T(8,128)(2,1)} %copy-done.28), kind=kOutput, calls=%fused_computation | convolution fusion | flops 17188257792 | bytes 41943040 | tf_op jit(solution)/shard_map/dot_general | solution.py:152
  826.2 124.5 %shard_map.246 = (f32[512,2048]{1,0:T(8,128)}, bf16[1,1024,2048]{2,1,0:T(8,128)(2,1)}, bf16[512,2048]{1,0:T(8,128)(2,1)}) custom-call(bf16[2048,2048]{1,0:T(8,128)(2,1)} %copy-done.29, bf16[2048,2048]{1,0:T(8,128)(2,1)} %copy-done.28, bf16[2048,2048]{1,0:T(8,128)(2,1)} %constant_dynamic-update-slice_fusion.18.refs_2_, ...), custom_call_target="tpu_custom_call" | custom-call | flops 34359738368 | bytes 167772160 | tf_op jit(solution)/shard_map/pallas_call | solution.py:762
  950.7 4.3 multiply_reduce_fusion.1
  961.8 14.3 %fusion.56 = f32[1024,2048]{1,0:T(8,128)} fusion(bf16[2048,1024]{1,0:T(8,128)(2,1)S(1)} %copy-done.49, bf16[2048,2048]{1,0:T(8,128)(2,1)} %all-gather.20.cloned.1.call-done.left), kind=kOutput, calls=%fused_computation.198 | convolution fusion | flops 8589934592 | bytes 20971520 | tf_op jit(solution)/shard_map/dot_general | solution.py:152
  976.1 13.5 add_convert_fusion.1
  1006.7 4.1 fusion.8
  1022.3 7.6 collective-permute-done.20
  1029.9 9.0 collective-permute-start.24
  1039.0 17.0 %collective-permute-done.22 = bf16[512,256]{1,0:T(8,128)(2,1)S(1)} collective-permute-done((bf16[512,256]{1,0:T(8,128)(2,1)S(1)}, bf16[512,256]{1,0:T(8,128)(2,1)S(1)}, u32[]{:S(2)}, u32[]{:S(2)}) %collective-permute-start.22) | collective-permute-done | bytes 262176 | tf_op jit(solution)/shard_map/ppermute | solution.py:60
  1058.1 51.6 %shard_map.247 = (f32[4096,256]{1,0:T(8,128)}, f32[4096,256]{1,0:T(8,128)}, bf16[4096,256]{1,0:T(8,128)(2,1)S(1)}) custom-call(s32[8]{0:T(128)S(1)} %and_select_fusion.high, s32[1,4096]{1,0:T(1,128)S(1)} %bitcast.65, bf16[4096,256]{1,0:T(8,128)(2,1)S(1)} %copy-done.25, bf16[4096,256]{1,0:T(8,128)(2,1)} %copy-done.26, bf16[4096,256]{1,0:T(8,128)(2,1)} %copy-done.27, ...), custom_call_target="tpu_custom_call" | custom-call | flops 12884901888 | bytes 20971520 | tf_op jit(solution)/shard_map/pallas_call | solution.py:1035
  1114.8 8.9 shard_map.248
  1124.4 11.6 shard_map.249
  1142.9 5.8 collective-permute-start.29
  1149.1 6.3 convert_add_fusion.1.rest_0_
  1155.4 11.6 shard_map.250.refs_0_
  1167.1 6.1 fusion.57
  1173.2 5.9 fusion.11
  1181.7 11.5 collective-permute-done.29
  1201.7 6.9 fusion.58
  1208.6 9.4 add_convert_fusion.2
  1220.9 179.6 %shard_map.251 = (bf16[512,2048]{1,0:T(8,128)(2,1)}, bf16[1,1056,768]{2,1,0:T(8,128)(2,1)}, f32[528,768]{1,0:T(8,128)}) custom-call(bf16[4096,768]{1,0:T(8,128)(2,1)} %shard_map.250.refs_0_, bf16[2048,768]{1,0:T(8,128)(2,1)} %bitcast.61, bf16[2112,768]{1,0:T(8,128)(2,1)} %bitcast.75, f32[512,2048]{1,0:T(8,128)} %pad_maximum_fusion.refs_3_), custom_call_target="tpu_custom_call" | custom-call | flops 12884901888 | bytes 167772160 | tf_op jit(solution)/shard_map/pallas_call | solution.py:762
  (364 shorter events, 160.9 us)
Async XLA Ops:
  7.2 214.0 %all-gather.12.cloned.1.call-start = ((), (), s32[]{:S(2)}) async-start(), calls=%async_computation.1 | async-start | bytes 9437184 | tf_op jit(solution)/shard_map/all_gather | solution.py:77
  7.2 3.3 collective-permute-start
  63.9 157.2 %all-gather.10.cloned.1.call-start = ((), (), s32[]{:S(2)}) async-start(), calls=%async_computation | async-start | bytes 9437184 | tf_op jit(solution)/shard_map/all_gather | solution.py:77
  64.7 335.0 %all-gather.14.cloned.1.call-start = ((), (), s32[]{:S(2)}) async-start(), calls=%async_computation.2 | async-start | bytes 9437184 | tf_op jit(solution)/shard_map/all_gather | solution.py:77
  205.3 269.1 %all-gather.16.cloned.1.call-start = ((), (), s32[]{:S(2)}) async-start(), calls=%async_computation.3 | async-start | bytes 9437184 | tf_op jit(solution)/shard_map/all_gather | solution.py:77
  256.2 72.3 %collective-permute-start.2 = (bf16[512,1024]{1,0:T(8,128)(2,1)S(1)}, bf16[512,1024]{1,0:T(8,128)(2,1)S(1)}, u32[]{:S(2)}, u32[]{:S(2)}) collective-permute-start(bf16[512,1024]{1,0:T(8,128)(2,1)S(1)} %copy-done.67), channel_id=1, source_target_pairs={{1,16},{3,18},{5,20},{7,22},{9,24},{11,26},{13,28},{15,30},{16,1},... | collective-permute-start | bytes 3145736 | tf_op jit(solution)/shard_map/ppermute | solution.py:60
  259.5 70.8 %collective-permute-start.1 = (bf16[512,1024]{1,0:T(8,128)(2,1)S(1)}, bf16[512,1024]{1,0:T(8,128)(2,1)S(1)}, u32[]{:S(2)}, u32[]{:S(2)}) collective-permute-start(bf16[512,1024]{1,0:T(8,128)(2,1)S(1)} %copy-done.67), channel_id=1, source_target_pairs={{0,16},{1,0},{2,18},{3,2},{4,20},{5,4},{6,22},{7,6},{8,24},{9,8},{... | collective-permute-start | bytes 3145736 | tf_op jit(solution)/shard_map/ppermute | solution.py:60
  261.2 69.0 %copy-start.68 = (bf16[512,1024]{1,0:T(8,128)(2,1)S(1)}, bf16[512,1024]{1,0:T(8,128)(2,1)}, u32[]{:S(2)}) copy-start(bf16[512,1024]{1,0:T(8,128)(2,1)} %param.23) | copy-start | bytes 3145732
  270.0 61.9 %copy-start.24 = (bf16[4096,256]{1,0:T(8,128)(2,1)}, bf16[4096,256]{1,0:T(8,128)(2,1)S(1)}, u32[]{:S(2)}) copy-start(bf16[4096,256]{1,0:T(8,128)(2,1)S(1)} %get-tuple-element.55.query) | copy-start | bytes 6291460
  270.0 61.9 %copy-start.26 = (bf16[4096,256]{1,0:T(8,128)(2,1)}, bf16[4096,256]{1,0:T(8,128)(2,1)S(1)}, u32[]{:S(2)}) copy-start(bf16[4096,256]{1,0:T(8,128)(2,1)S(1)} %get-tuple-element.56.key) | copy-start | bytes 6291460
  270.1 97.5 %collective-permute-start.13 = (bf16[512,1024]{1,0:T(8,128)(2,1)S(1)}, bf16[512,1024]{1,0:T(8,128)(2,1)S(1)}, u32[]{:S(2)}, u32[]{:S(2)}) collective-permute-start(bf16[512,1024]{1,0:T(8,128)(2,1)S(1)} %copy-done.69), channel_id=1, source_target_pairs={{1,16},{3,18},{5,20},{7,22},{9,24},{11,26},{13,28},{15,30},{16,1},... | collective-permute-start | bytes 3145736 | tf_op jit(solution)/shard_map/ppermute | solution.py:60
  273.3 97.7 %collective-permute-start.12 = (bf16[512,1024]{1,0:T(8,128)(2,1)S(1)}, bf16[512,1024]{1,0:T(8,128)(2,1)S(1)}, u32[]{:S(2)}, u32[]{:S(2)}) collective-permute-start(bf16[512,1024]{1,0:T(8,128)(2,1)S(1)} %copy-done.69), channel_id=1, source_target_pairs={{0,16},{1,0},{2,18},{3,2},{4,20},{5,4},{6,22},{7,6},{8,24},{9,8},{... | collective-permute-start | bytes 3145736 | tf_op jit(solution)/shard_map/ppermute | solution.py:60
  330.4 67.0 %collective-permute-start.11 = (bf16[512,1024]{1,0:T(8,128)(2,1)S(1)}, bf16[512,1024]{1,0:T(8,128)(2,1)S(1)}, u32[]{:S(2)}, u32[]{:S(2)}) collective-permute-start(bf16[512,1024]{1,0:T(8,128)(2,1)S(1)} %get-tuple-element.64.refs_1_), channel_id=1, source_target_pairs={{0,2},{1,3},{2,0},{3,1},{4,6},{5,7},{6,4},{7,5},{8,10},{9,11},{10,... | collective-permute-start | bytes 3145736 | tf_op jit(solution)/shard_map/ppermute | solution.py:60
  330.9 66.6 %collective-permute-start.10 = (bf16[512,1024]{1,0:T(8,128)(2,1)S(1)}, bf16[512,1024]{1,0:T(8,128)(2,1)S(1)}, u32[]{:S(2)}, u32[]{:S(2)}) collective-permute-start(bf16[512,1024]{1,0:T(8,128)(2,1)S(1)} %get-tuple-element.63.refs_0_), channel_id=1, source_target_pairs={{0,2},{1,3},{2,0},{3,1},{4,6},{5,7},{6,4},{7,5},{8,10},{9,11},{10,... | collective-permute-start | bytes 3145736 | tf_op jit(solution)/shard_map/ppermute | solution.py:60
  367.5 15.2 %collective-permute-start.5 = (bf16[512,256]{1,0:T(8,128)(2,1)S(1)}, bf16[512,256]{1,0:T(8,128)(2,1)S(1)}, u32[]{:S(2)}, u32[]{:S(2)}) collective-permute-start(bf16[512,256]{1,0:T(8,128)(2,1)S(1)} %get-tuple-element.140), channel_id=1, source_target_pairs={{0,12},{1,13},{2,14},{3,15},{4,8},{5,9},{6,10},{7,11},{8,4},{9,5},... | collective-permute-start | bytes 786440 | tf_op jit(solution)/shard_map/ppermute | solution.py:60
  367.5 14.6 %collective-permute-start.4 = (bf16[512,256]{1,0:T(8,128)(2,1)S(1)}, bf16[512,256]{1,0:T(8,128)(2,1)S(1)}, u32[]{:S(2)}, u32[]{:S(2)}) collective-permute-start(bf16[512,256]{1,0:T(8,128)(2,1)S(1)} %get-tuple-element.141), channel_id=1, source_target_pairs={{0,8},{1,9},{2,10},{3,11},{4,12},{5,13},{6,14},{7,15},{8,0},{9,1},... | collective-permute-start | bytes 786440 | tf_op jit(solution)/shard_map/ppermute | solution.py:60
  371.0 10.7 collective-permute-start.3
  381.7 2.4 collective-permute-start.6
  382.1 8.4 collective-permute-start.7
  382.7 9.0 collective-permute-start.8
  384.1 13.3 collective-permute-start.9
  411.0 94.2 %all-gather.18.cloned.1.call-start = ((), (), s32[]{:S(2)}) async-start(), calls=%async_computation.4 | async-start | bytes 9437184 | tf_op jit(solution)/shard_map/all_gather | solution.py:77
  411.1 25.0 %collective-permute-start.14 = (bf16[512,1024]{1,0:T(8,128)(2,1)}, bf16[512,1024]{1,0:T(8,128)(2,1)}, u32[]{:S(2)}, u32[]{:S(2)}) collective-permute-start(bf16[512,1024]{1,0:T(8,128)(2,1)} %get-tuple-element.67), channel_id=1, source_target_pairs={{0,2},{1,3},{2,0},{3,1},{4,6},{5,7},{6,4},{7,5},{8,10},{9,11},{10,... | collective-permute-start | bytes 3145736 | tf_op jit(solution)/shard_map/ppermute | solution.py:60
  411.2 47.4 %collective-permute-start.15 = (bf16[512,1024]{1,0:T(8,128)(2,1)}, bf16[512,1024]{1,0:T(8,128)(2,1)}, u32[]{:S(2)}, u32[]{:S(2)}) collective-permute-start(bf16[512,1024]{1,0:T(8,128)(2,1)} %get-tuple-element.68), channel_id=1, source_target_pairs={{0,2},{1,3},{2,0},{3,1},{4,6},{5,7},{6,4},{7,5},{8,10},{9,11},{10,... | collective-permute-start | bytes 3145736 | tf_op jit(solution)/shard_map/ppermute | solution.py:60
  458.6 250.6 %all-gather.22.cloned.1.call-start = ((), (), s32[]{:S(2)}) async-start(), calls=%async_computation.6 | async-start | bytes 9437184 | tf_op jit(solution)/shard_map/all_gather | solution.py:77
  663.2 94.5 %all-gather.20.cloned.1.call-start = ((), (), s32[]{:S(2)}) async-start(), calls=%async_computation.5 | async-start | bytes 9437184 | tf_op jit(solution)/shard_map/all_gather | solution.py:77
  664.0 503.1 %all-gather.24.cloned.1.call-start = ((), (), s32[]{:S(2)}) async-start(), calls=%async_computation.7 | async-start | bytes 9437184 | tf_op jit(solution)/shard_map/all_gather | solution.py:77
  826.1 124.5 %copy-start.36 = (f32[256,2048]{1,0:T(8,128)S(1)}, f32[256,2048]{1,0:T(8,128)}, u32[]{:S(2)}) copy-start(f32[256,2048]{1,0:T(8,128)} %copy-done.34) | copy-start | bytes 6291460
  957.7 215.5 %all-gather.26.cloned.1.call-start = ((), (), s32[]{:S(2)}) async-start(), calls=%async_computation.8 | async-start | bytes 9437184 | tf_op jit(solution)/shard_map/all_gather | solution.py:77
  992.3 63.8 %collective-permute-start.23 = (bf16[1024,1024]{1,0:T(8,128)(2,1)}, bf16[1024,1024]{1,0:T(8,128)(2,1)S(1)}, u32[]{:S(2)}, u32[]{:S(2)}) collective-permute-start(bf16[1024,1024]{1,0:T(8,128)(2,1)} %constant_dynamic-slice_fusion.4), channel_id=1, source_target_pairs={{0,2},{1,3},{2,0},{3,1},{4,6},{5,7},{6,4},{7,5},{8,10},{9,11},{10,... | collective-permute-start | bytes 6291464 | tf_op jit(solution)/shard_map/ppermute | solution.py:60
  998.5 40.5 %collective-permute-start.21 = (bf16[512,256]{1,0:T(8,128)(2,1)S(1)}, bf16[512,256]{1,0:T(8,128)(2,1)S(1)}, u32[]{:S(2)}, u32[]{:S(2)}) collective-permute-start(bf16[512,256]{1,0:T(8,128)(2,1)S(1)} %get-tuple-element.133), channel_id=1, source_target_pairs={{0,9},{1,8},{2,11},{3,10},{4,13},{5,12},{6,15},{7,14},{8,1},{9,0},... | collective-permute-start | bytes 786440 | tf_op jit(solution)/shard_map/ppermute | solution.py:60
  999.7 14.5 %collective-permute-start.16 = (bf16[512,256]{1,0:T(8,128)(2,1)S(1)}, bf16[512,256]{1,0:T(8,128)(2,1)S(1)}, u32[]{:S(2)}, u32[]{:S(2)}) collective-permute-start(bf16[512,256]{1,0:T(8,128)(2,1)S(1)} %get-tuple-element.130), channel_id=1, source_target_pairs={{0,4},{1,5},{2,6},{3,7},{4,0},{5,1},{6,2},{7,3},{8,12},{9,13},{10,... | collective-permute-start | bytes 786440 | tf_op jit(solution)/shard_map/ppermute | solution.py:60
  999.8 15.5 %collective-permute-start.17 = (bf16[512,256]{1,0:T(8,128)(2,1)}, bf16[512,256]{1,0:T(8,128)(2,1)S(1)}, u32[]{:S(2)}, u32[]{:S(2)}) collective-permute-start(bf16[512,256]{1,0:T(8,128)(2,1)} %get-tuple-element.131), channel_id=1, source_target_pairs={{0,8},{1,9},{2,10},{3,11},{4,12},{5,13},{6,14},{7,15},{8,0},{9,1},... | collective-permute-start | bytes 786440 | tf_op jit(solution)/shard_map/ppermute | solution.py:60
  1001.8 17.5 %collective-permute-start.18 = (bf16[512,256]{1,0:T(8,128)(2,1)}, bf16[512,256]{1,0:T(8,128)(2,1)S(1)}, u32[]{:S(2)}, u32[]{:S(2)}) collective-permute-start(bf16[512,256]{1,0:T(8,128)(2,1)} %get-tuple-element.132), channel_id=1, source_target_pairs={{0,12},{1,13},{2,14},{3,15},{4,8},{5,9},{6,10},{7,11},{8,4},{9,5},... | collective-permute-start | bytes 786440 | tf_op jit(solution)/shard_map/ppermute | solution.py:60
  1014.2 5.5 collective-permute-start.19
  1015.3 14.6 %collective-permute-start.20 = (bf16[512,256]{1,0:T(8,128)(2,1)S(1)}, bf16[512,256]{1,0:T(8,128)(2,1)S(1)}, u32[]{:S(2)}, u32[]{:S(2)}) collective-permute-start(bf16[512,256]{1,0:T(8,128)(2,1)S(1)} %get-tuple-element.135), channel_id=1, source_target_pairs={{0,5},{1,4},{2,7},{3,6},{4,1},{5,0},{6,3},{7,2},{8,13},{9,12},{10,... | collective-permute-start | bytes 786440 | tf_op jit(solution)/shard_map/ppermute | solution.py:60
  1019.4 36.6 %collective-permute-start.22 = (bf16[512,256]{1,0:T(8,128)(2,1)S(1)}, bf16[512,256]{1,0:T(8,128)(2,1)S(1)}, u32[]{:S(2)}, u32[]{:S(2)}) collective-permute-start(bf16[512,256]{1,0:T(8,128)(2,1)S(1)} %get-tuple-element.128), channel_id=1, source_target_pairs={{0,13},{1,12},{2,15},{3,14},{4,9},{5,8},{6,11},{7,10},{8,5},{9,4},... | collective-permute-start | bytes 786440 | tf_op jit(solution)/shard_map/ppermute | solution.py:60
  1019.8 129.3 %collective-permute-start.25 = (bf16[512,2048]{1,0:T(8,128)(2,1)}, bf16[512,2048]{1,0:T(8,128)(2,1)}, u32[]{:S(2)}, u32[]{:S(2)}) collective-permute-start(bf16[512,2048]{1,0:T(8,128)(2,1)} %get-tuple-element.105), channel_id=1, source_target_pairs={{0,1},{1,17},{2,3},{3,19},{4,5},{5,21},{6,7},{7,23},{8,9},{9,25},{... | collective-permute-start | bytes 6291464 | tf_op jit(solution)/shard_map/ppermute | solution.py:60
  1029.9 119.2 %collective-permute-start.24 = (bf16[512,2048]{1,0:T(8,128)(2,1)}, bf16[512,2048]{1,0:T(8,128)(2,1)}, u32[]{:S(2)}, u32[]{:S(2)}) collective-permute-start(bf16[512,2048]{1,0:T(8,128)(2,1)} %get-tuple-element.106), channel_id=1, source_target_pairs={{1,16},{3,18},{5,20},{7,22},{9,24},{11,26},{13,28},{15,30},{16,1},... | collective-permute-start | bytes 6291464 | tf_op jit(solution)/shard_map/ppermute | solution.py:60
  1058.0 51.6 %copy-start.13 = (f32[1,4096]{1,0:T(1,128)S(1)}, f32[1,4096]{1,0:T(1,128)}, u32[]{:S(2)}) copy-start(f32[1,4096]{1,0:T(1,128)} %copy-done.12) | copy-start | bytes 49156
  1058.0 51.7 %copy-start.15 = (f32[1,4096]{1,0:T(1,128)S(1)}, f32[1,4096]{1,0:T(1,128)}, u32[]{:S(2)}) copy-start(f32[1,4096]{1,0:T(1,128)} %copy-done.14) | copy-start | bytes 49156
  1058.0 51.7 %copy-start.18 = (f32[1,256]{1,0:T(1,128)S(1)}, f32[1,256]{1,0:T(1,128)}, u32[]{:S(2)}) copy-start(f32[1,256]{1,0:T(1,128)} %copy-done.17) | copy-start | bytes 3076
  1058.1 51.7 %copy-start.20 = (f32[1,256]{1,0:T(1,128)S(1)}, f32[1,256]{1,0:T(1,128)}, u32[]{:S(2)}) copy-start(f32[1,256]{1,0:T(1,128)} %copy-done.19) | copy-start | bytes 3076
  1142.9 38.8 %collective-permute-start.30 = (bf16[1024,512]{1,0:T(8,128)(2,1)}, bf16[1024,512]{1,0:T(8,128)(2,1)}, u32[]{:S(2)}, u32[]{:S(2)}) collective-permute-start(bf16[1024,512]{1,0:T(8,128)(2,1)} %get-tuple-element.101), channel_id=1, source_target_pairs={{0,1},{1,17},{2,3},{3,19},{4,5},{5,21},{6,7},{7,23},{8,9},{9,25},{... | collective-permute-start | bytes 3145736 | tf_op jit(solution)/shard_map/ppermute | solution.py:60
  1142.9 50.4 %collective-permute-start.29 = (bf16[1024,512]{1,0:T(8,128)(2,1)}, bf16[1024,512]{1,0:T(8,128)(2,1)}, u32[]{:S(2)}, u32[]{:S(2)}) collective-permute-start(bf16[1024,512]{1,0:T(8,128)(2,1)} %get-tuple-element.102), channel_id=1, source_target_pairs={{1,16},{3,18},{5,20},{7,22},{9,24},{11,26},{13,28},{15,30},{16,1},... | collective-permute-start | bytes 3145736 | tf_op jit(solution)/shard_map/ppermute | solution.py:60
  1179.2 17.6 %collective-permute-start.26 = (bf16[256,1024]{1,0:T(8,128)(2,1)S(1)}, bf16[256,1024]{1,0:T(8,128)(2,1)S(1)}, u32[]{:S(2)}, u32[]{:S(2)}) collective-permute-start(bf16[256,1024]{1,0:T(8,128)(2,1)S(1)} %constant_dynamic-slice_fusion.2), channel_id=1, source_target_pairs={{0,2},{1,3},{2,0},{3,1},{4,6},{5,7},{6,4},{7,5},{8,10},{9,11},{10,... | collective-permute-start | bytes 1572872 | tf_op jit(solution)/shard_map/ppermute | solution.py:60
  1197.1 22.9 %collective-permute-start.28 = (bf16[256,512]{1,0:T(8,128)(2,1)S(1)}, bf16[256,512]{1,0:T(8,128)(2,1)S(1)}, u32[]{:S(2)}, u32[]{:S(2)}) collective-permute-start(bf16[256,512]{1,0:T(8,128)(2,1)S(1)} %get-tuple-element.103), channel_id=1, source_target_pairs={{0,1},{1,17},{2,3},{3,19},{4,5},{5,21},{6,7},{7,23},{8,9},{9,25},{... | collective-permute-start | bytes 786440 | tf_op jit(solution)/shard_map/ppermute | solution.py:60
  1197.2 22.8 %collective-permute-start.27 = (bf16[256,512]{1,0:T(8,128)(2,1)S(1)}, bf16[256,512]{1,0:T(8,128)(2,1)S(1)}, u32[]{:S(2)}, u32[]{:S(2)}) collective-permute-start(bf16[256,512]{1,0:T(8,128)(2,1)S(1)} %get-tuple-element.104), channel_id=1, source_target_pairs={{1,16},{3,18},{5,20},{7,22},{9,24},{11,26},{13,28},{15,30},{16,1},... | collective-permute-start | bytes 786440 | tf_op jit(solution)/shard_map/ppermute | solution.py:60
  (78 other events, 594.8 us)
Sparse Core Ops, SparseCore 0:
  64.1 96.1 all-gather.11
  162.4 52.9 all-gather.9
  216.9 50.2 all-gather.13
  411.1 44.9 all-gather.15
  458.7 46.4 all-gather.17
  663.3 45.7 all-gather.21
  710.7 46.9 all-gather.19
  957.8 45.5 all-gather.23
  1005.0 93.4 all-gather.25

commit v4 on v3

--- a/solution.py
+++ b/solution.py
@@ -568,7 +568,7 @@
         return value
 
     if last:
-        finish_sum = finish(
+        send_sum, take_sum = finish(
             (zhi, rest, xx, core), (row, col, far_row, near_col), grads, blocks, block, sums, refs
         )
         final, final_sem, final_recv_sem = refs[:3]
@@ -602,7 +602,9 @@
 
             if h == 0:
                 second_stage(1)
-                finish_sum()
+                send_sum()
+
+        take_sum()
 
         for h in range(2):
 
@@ -664,7 +666,7 @@
     to_cross = give(1, 1 - core, far_row, near_col, 1)
     own.start()
 
-    def run():
+    def send_sum():
         for step in range(1, across):
             block(0, step).wait_recv()
             rest[step - 1].start()
@@ -680,21 +682,28 @@
         @pl.when(zhi == core)
         def _():
             to_sibling.start()
-            to_sibling.wait_send()
-            give(0, core, far_row, col, 0).wait_recv()
-            sums[...] = pair[core].astype(jnp.float32) + landed[0].astype(jnp.float32)
 
         @pl.when(zhi != core)
         def _():
             to_same.start()
             to_cross.start()
+
+    def take_sum():
+        @pl.when(zhi == core)
+        def _():
+            to_sibling.wait_send()
+            give(0, core, far_row, col, 0).wait_recv()
+            sums[...] = pair[core].astype(jnp.float32) + landed[0].astype(jnp.float32)
+
+        @pl.when(zhi != core)
+        def _():
             to_same.wait_send()
             to_cross.wait_send()
             to_same.wait_recv()
             to_cross.wait_recv()
             sums[...] = landed[1].astype(jnp.float32) + landed[0].astype(jnp.float32)
 
-    return run
+    return send_sum, take_sum
 
 
 def grow(shape, axis, pieces):
@@ -1314,7 +1323,7 @@
     query, key, value = prepare(
         proj, query_inv, key_inv, cosine, sine, query_scale, key_scale, head_size
     )
-    gate_pair = plan.weight_pair(after(w_gate, invs))
+    gate_pair = plan.weight_pair(after(w_gate, out_rows))
     up_pair = plan.weight_pair(after(w_up, query))
     attn_out, log_sum = attend(
         low, first_row, query, key, value, head_size, tile, gate_pair

time: 1420 us -> 1450 us (1.021)
    unnamed x180 -> x168, local copies, waits for them, and re-layouts: 45.6 us -> 44.3 us
  transfers between devices with their start and end apart: 40 -> 40, of which waited for: 16 -> 17; matrix products, arithmetic and copies ran while one was open for 12% -> 12% of each run, Pallas kernels for 22% -> 22%
where the time goes in v4:
time: 1450 us
  Pallas kernels  802 us (55%)
  waiting for transfers between devices  252 us (17%)
  matrix products  170 us (12%)
  local copies, waits for them, and re-layouts  89.6 us (6%)
  other arithmetic  76.3 us (5%)
  starting transfers between devices  41.1 us (3%)
  between operations  15.8 us (1%)
    pallas_call x3, Pallas kernels, multiply_scatter(): pl.pallas_call(functools.partial(scatter_kernel, plan, len(lefts), axes,...  422 us
    ppermute x31, waiting for transfers between devices, send(): return lax.ppermute(value, BOTH, pairs)  170 us
    pallas_call x1, Pallas kernels, gather_weights(): pl.pallas_call(functools.partial(gather_kernel, plan, axes), in_specs=[an...  139 us
    dot_general x8, matrix products, contract_rows(): lax.dot_general(left, right, (((0,), (0,)), ((), ())), preferred_element_...  104 us
    all_gather x9, waiting for transfers between devices, token_gather(): lax.all_gather(value, BOTH, axis=0, tiled=True, axis_index_groups=self.to...  80.1 us
    pallas_call x1, Pallas kernels, attend_back(): pl.pallas_call(functools.partial(attend_back_kernel, rows), grid_spec=plt...  51.5 us
    pallas_call x1, Pallas kernels, swap_tokens(): pl.pallas_call(functools.partial(swap_kernel, plan), in_specs=[anywhere],...  50.2 us
    dot_general x2, matrix products, body(): jnp.dot(gathered_h[k], ff_weight, preferred_element_type=f32).astype(bf16)  45.7 us
  transfers between devices with their start and end apart: 40, of which 17 were waited for; matrix products, arithmetic and copies ran while one was open for 12% of the time, Pallas kernels for 22%

profile of v4, /device:TPU:1, one launch (start us, length us, event | category | flops | bytes accessed | tf_op | source)
XLA Modules:
  0.0 1446.4 jit_solution(8709734112131085848)
XLA Ops:
  10.5 50.2 %shard_map.237 = bf16[512,2048]{1,0:T(8,128)(2,1)} custom-call(bf16[512,2048]{1,0:T(8,128)(2,1)} %given), custom_call_target="tpu_custom_call" | custom-call | bytes 134217728 | tf_op jit(solution)/shard_map/pallas_call | solution.py:200
  66.0 139.3 %shard_map.238 = (bf16[2112,768]{1,0:T(8,128)(2,1)}, bf16[256,2048]{1,0:T(8,128)(2,1)}, bf16[1024,2048]{1,0:T(8,128)(2,1)}) custom-call(bf16[528,768]{1,0:T(8,128)(2,1)} %pad_maximum_fusion.3.refs_0_, bf16[256,512]{1,0:T(8,128)(2,1)} %refs_1_.1, bf16[1024,512]{1,0:T(8,128)(2,1)} %refs_2_.1), custom_call_target="tpu_custom_call" | custom-call | bytes 268435456 | tf_op jit(solution)/shard_map/pallas_call | solution.py:293
  213.5 9.2 fusion.22
  222.8 33.1 %collective-permute-done.2 = bf16[512,1024]{1,0:T(8,128)(2,1)} collective-permute-done((bf16[512,1024]{1,0:T(8,128)(2,1)S(1)}, bf16[512,1024]{1,0:T(8,128)(2,1)}, u32[]{:S(2)}, u32[]{:S(2)}) %collective-permute-start.2) | collective-permute-done | bytes 1048608 | tf_op jit(solution)/shard_map/ppermute | solution.py:60
  264.1 17.7 %shard_map.239 = (f32[4096,768]{1,0:T(8,128)}, f32[2,4096]{1,0:T(2,128)S(1)}) custom-call(bf16[2048,2048]{1,0:T(8,128)(2,1)S(1)} %copy-done.17, bf16[2048,2048]{1,0:T(8,128)(2,1)} %all-gather.12.cloned.1.call-done.second, bf16[2048,768]{1,0:T(8,128)(2,1)S(1)} %bitcast.62), custom_call_target="tpu_custom_call" | custom-call | flops 12884901888 | bytes 29360128 | tf_op jit(solution)/shard_map/pallas_call | solution.py:850
  282.5 6.6 shard_map.240
  291.6 9.0 shard_map.241
  300.6 33.1 %shard_map.242 = (bf16[4096,256]{1,0:T(8,128)(2,1)S(1)}, f32[2,1,4096]{2,1,0:T(1,128)S(1)}) custom-call(s32[8]{0:T(128)S(1)} %and_select_fusion.2.low, s32[1,4096]{1,0:T(1,128)S(1)} %bitcast.64, bf16[4096,256]{1,0:T(8,128)(2,1)S(1)} %get-tuple-element.55.query, bf16[4096,256]{1,0:T(8,128)(2,1)S(1)} %get-tuple-element.56.key, ...), custom_call_target="tpu_custom_call" | custom-call | flops 4294967296 | bytes 8388608 | tf_op jit(solution)/shard_map/pallas_call | solution.py:961
  348.5 9.1 collective-permute-done.3
  360.5 11.7 collective-permute-done.5
  372.8 5.1 collective-permute-done.4
  388.5 9.2 collective-permute-done.9
  400.9 15.8 %collective-permute-done.10 = bf16[512,1024]{1,0:T(8,128)(2,1)S(1)} collective-permute-done((bf16[512,1024]{1,0:T(8,128)(2,1)}, bf16[512,1024]{1,0:T(8,128)(2,1)S(1)}, u32[]{:S(2)}, u32[]{:S(2)}) %collective-permute-start.10) | collective-permute-done | bytes 1048608 | tf_op jit(solution)/shard_map/ppermute | solution.py:60
  417.7 6.3 multiply_reduce_fusion.6
  430.6 19.9 %collective-permute-done.14 = bf16[512,1024]{1,0:T(8,128)(2,1)} collective-permute-done((bf16[512,1024]{1,0:T(8,128)(2,1)}, bf16[512,1024]{1,0:T(8,128)(2,1)}, u32[]{:S(2)}, u32[]{:S(2)}) %collective-permute-start.14) | collective-permute-done | bytes 1048608 | tf_op jit(solution)/shard_map/ppermute | solution.py:60
  450.5 22.5 %collective-permute-done.15 = bf16[512,1024]{1,0:T(8,128)(2,1)} collective-permute-done((bf16[512,1024]{1,0:T(8,128)(2,1)}, bf16[512,1024]{1,0:T(8,128)(2,1)}, u32[]{:S(2)}, u32[]{:S(2)}) %collective-permute-start.15) | collective-permute-done | bytes 1048608 | tf_op jit(solution)/shard_map/ppermute | solution.py:60
  488.7 23.5 %convolution_convert_fusion.1.both = bf16[2048,2048]{1,0:T(8,128)(2,1)S(1)} fusion(bf16[2048,2048]{1,0:T(8,128)(2,1)} %all-gather.16.cloned.1.call-done, bf16[2048,2048]{1,0:T(8,128)(2,1)} %constant_dynamic-update-slice_fusion.18.refs_2_), kind=kOutput, calls=%fused_computation.19 | convolution fusion | flops 17184063488 | bytes 25165824 | tf_op jit(solution)/shard_map/dot_general | solution.py:1374
  519.5 9.3 all-gather.18.cloned.1.call-done
  528.8 22.2 %convolution_convert_fusion.both = bf16[2048,2048]{1,0:T(8,128)(2,1)S(1)} fusion(bf16[2048,2048]{1,0:T(8,128)(2,1)} %all-gather.18.cloned.1.call-done, bf16[2048,2048]{1,0:T(8,128)(2,1)} %constant_dynamic-update-slice_fusion.18.refs_2_), kind=kOutput, calls=%fused_computation.18 | convolution fusion | flops 17184063488 | bytes 25165824 | tf_op jit(solution)/shard_map/dot_general | solution.py:1374
  555.6 119.6 %shard_map.243 = (f32[512,2048]{1,0:T(8,128)}, bf16[512,2048]{1,0:T(8,128)(2,1)}) custom-call(bf16[2048,1024]{1,0:T(8,128)(2,1)} %fusion.10.refs_0_, bf16[2048,1024]{1,0:T(8,128)(2,1)} %fusion.9.refs_1_, bf16[1024,2048]{1,0:T(8,128)(2,1)} %get-tuple-element.70.refs_2_.weight, bf16[512,2048]{1,0:T(8,128)(2,1)} %refs_3_.1), custom_call_target="tpu_custom_call" | custom-call | flops 17179869184 | bytes 167772160 | tf_op jit(solution)/shard_map/pallas_call | solution.py:771
  682.1 4.9 fusion.18
  690.7 42.1 %all-gather.22.cloned.1.call-done.left = bf16[2048,2048]{1,0:T(8,128)(2,1)} async-done(((bf16[256,2048]{1,0:T(8,128)(2,1)}), bf16[2048,2048]{1,0:T(8,128)(2,1)}) %all-gather.22.cloned.1.call-update) | async-done | bytes 8388624 | tf_op jit(solution)/shard_map/all_gather | solution.py:77
  735.1 14.4 shard_map.245.refs_1_
  752.9 28.6 %all-gather.20.cloned.1.call-done.left = bf16[2048,2048]{1,0:T(8,128)(2,1)} async-done(((bf16[256,2048]{1,0:T(8,128)(2,1)}), bf16[2048,2048]{1,0:T(8,128)(2,1)}) %all-gather.20.cloned.1.call-update) | async-done | bytes 8388624 | tf_op jit(solution)/shard_map/all_gather | solution.py:77
  783.7 13.9 shard_map.244.refs_0_
  800.8 22.6 %fusion.55 = f32[2048,2048]{1,0:T(8,128)} fusion(bf16[2048,2048]{1,0:T(8,128)(2,1)} %all-gather.16.cloned.1.call-done, bf16[2048,2048]{1,0:T(8,128)(2,1)S(1)} %shard_map.244.refs_0_), kind=kOutput, calls=%fused_computation.197 | convolution fusion | flops 17179869184 | bytes 33554432 | tf_op jit(solution)/shard_map/dot_general | solution.py:152
  823.4 27.4 %add_convert_fusion.refs_3_ = bf16[2048,2048]{1,0:T(8,128)(2,1)} fusion(f32[2048,2048]{1,0:T(8,128)} %fusion.55, bf16[2048,2048]{1,0:T(8,128)(2,1)} %all-gather.18.cloned.1.call-done, bf16[2048,2048]{1,0:T(8,128)(2,1)} %copy-done.24), kind=kOutput, calls=%fused_computation | convolution fusion | flops 17188257792 | bytes 41943040 | tf_op jit(solution)/shard_map/dot_general | solution.py:152
  850.8 124.5 %shard_map.246 = (f32[512,2048]{1,0:T(8,128)}, bf16[1,1024,2048]{2,1,0:T(8,128)(2,1)}, bf16[512,2048]{1,0:T(8,128)(2,1)}) custom-call(bf16[2048,2048]{1,0:T(8,128)(2,1)} %copy-done.25, bf16[2048,2048]{1,0:T(8,128)(2,1)} %copy-done.24, bf16[2048,2048]{1,0:T(8,128)(2,1)} %constant_dynamic-update-slice_fusion.18.refs_2_, ...), custom_call_target="tpu_custom_call" | custom-call | flops 34359738368 | bytes 167772160 | tf_op jit(solution)/shard_map/pallas_call | solution.py:771
  986.5 12.5 fusion.56
  999.0 12.2 add_convert_fusion.1
  1014.3 5.9 convolution_convert_fusion.3
  1020.3 5.8 convolution_convert_fusion.2
  1042.1 7.0 collective-permute-done.18
  1051.4 8.7 collective-permute-done.20
  1060.1 5.0 collective-permute-start.24
  1065.2 11.3 collective-permute-done.22
  1078.6 51.5 %shard_map.247 = (f32[4096,256]{1,0:T(8,128)}, f32[4096,256]{1,0:T(8,128)}, bf16[4096,256]{1,0:T(8,128)(2,1)S(1)}) custom-call(s32[8]{0:T(128)S(1)} %and_select_fusion.high, s32[1,4096]{1,0:T(1,128)S(1)} %bitcast.65, bf16[4096,256]{1,0:T(8,128)(2,1)S(1)} %copy-done.21, bf16[4096,256]{1,0:T(8,128)(2,1)} %copy-done.22, bf16[4096,256]{1,0:T(8,128)(2,1)} %copy-done.23, ...), custom_call_target="tpu_custom_call" | custom-call | flops 12884901888 | bytes 20971520 | tf_op jit(solution)/shard_map/pallas_call | solution.py:1044
  1135.3 9.0 shard_map.248
  1144.9 22.8 %shard_map.249 = f32[2,6144]{1,0:T(2,128)} custom-call(f32[2,6144]{1,0:T(2,128)} %maximum_maximum_fusion.own), custom_call_target="tpu_custom_call" | custom-call | flops 86016 | bytes 16777216 | tf_op jit(solution)/shard_map/pallas_call | solution.py:345
  1175.1 5.3 collective-permute-start.29
  1180.8 6.3 convert_add_fusion.1.rest_0_
  1187.1 12.1 shard_map.250.refs_0_
  1199.3 6.1 fusion.57
  1205.4 5.9 fusion.11
  1213.9 11.0 collective-permute-done.29
  1233.2 7.3 fusion.58
  1240.6 9.9 add_convert_fusion.2
  1253.3 177.7 %shard_map.251 = (bf16[512,2048]{1,0:T(8,128)(2,1)}, bf16[1,1056,768]{2,1,0:T(8,128)(2,1)}, f32[528,768]{1,0:T(8,128)}) custom-call(bf16[4096,768]{1,0:T(8,128)(2,1)} %shard_map.250.refs_0_, bf16[2048,768]{1,0:T(8,128)(2,1)} %bitcast.61, bf16[2112,768]{1,0:T(8,128)(2,1)} %bitcast.75, f32[512,2048]{1,0:T(8,128)} %pad_maximum_fusion.refs_3_), custom_call_target="tpu_custom_call" | custom-call | flops 12884901888 | bytes 167772160 | tf_op jit(solution)/shard_map/pallas_call | solution.py:771
  (351 shorter events, 186.4 us)
Async XLA Ops:
  7.2 251.4 %all-gather.12.cloned.1.call-start = ((), (), s32[]{:S(2)}) async-start(), calls=%async_computation.1 | async-start | bytes 9437184 | tf_op jit(solution)/shard_map/all_gather | solution.py:77
  7.2 3.3 collective-permute-start
  63.9 194.7 %all-gather.10.cloned.1.call-start = ((), (), s32[]{:S(2)}) async-start(), calls=%async_computation | async-start | bytes 9437184 | tf_op jit(solution)/shard_map/all_gather | solution.py:77
  64.7 353.0 %all-gather.14.cloned.1.call-start = ((), (), s32[]{:S(2)}) async-start(), calls=%async_computation.2 | async-start | bytes 9437184 | tf_op jit(solution)/shard_map/all_gather | solution.py:77
  65.0 140.4 %copy-start.63 = (bf16[512,1024]{1,0:T(8,128)(2,1)S(1)}, bf16[512,1024]{1,0:T(8,128)(2,1)}, u32[]{:S(2)}) copy-start(bf16[512,1024]{1,0:T(8,128)(2,1)} %param.23) | copy-start | bytes 3145732
  205.3 283.4 %all-gather.16.cloned.1.call-start = ((), (), s32[]{:S(2)}) async-start(), calls=%async_computation.3 | async-start | bytes 9437184 | tf_op jit(solution)/shard_map/all_gather | solution.py:77
  205.4 50.5 %collective-permute-start.2 = (bf16[512,1024]{1,0:T(8,128)(2,1)S(1)}, bf16[512,1024]{1,0:T(8,128)(2,1)}, u32[]{:S(2)}, u32[]{:S(2)}) collective-permute-start(bf16[512,1024]{1,0:T(8,128)(2,1)S(1)} %copy-done.63), channel_id=1, source_target_pairs={{1,16},{3,18},{5,20},{7,22},{9,24},{11,26},{13,28},{15,30},{16,1},... | collective-permute-start | bytes 3145736 | tf_op jit(solution)/shard_map/ppermute | solution.py:60
  207.4 48.5 %collective-permute-start.1 = (bf16[512,1024]{1,0:T(8,128)(2,1)S(1)}, bf16[512,1024]{1,0:T(8,128)(2,1)}, u32[]{:S(2)}, u32[]{:S(2)}) collective-permute-start(bf16[512,1024]{1,0:T(8,128)(2,1)S(1)} %copy-done.63), channel_id=1, source_target_pairs={{0,16},{1,0},{2,18},{3,2},{4,20},{5,4},{6,22},{7,6},{8,24},{9,8},{... | collective-permute-start | bytes 3145736 | tf_op jit(solution)/shard_map/ppermute | solution.py:60
  213.5 42.4 %copy-start.64 = (bf16[512,1024]{1,0:T(8,128)(2,1)S(1)}, bf16[512,1024]{1,0:T(8,128)(2,1)}, u32[]{:S(2)}) copy-start(bf16[512,1024]{1,0:T(8,128)(2,1)} %param.23) | copy-start | bytes 3145732
  336.9 8.9 collective-permute-start.8
  338.8 9.1 collective-permute-start.7
  339.7 17.9 %collective-permute-start.3 = (bf16[512,256]{1,0:T(8,128)(2,1)}, bf16[512,256]{1,0:T(8,128)(2,1)}, u32[]{:S(2)}, u32[]{:S(2)}) collective-permute-start(bf16[512,256]{1,0:T(8,128)(2,1)} %get-tuple-element.142), channel_id=1, source_target_pairs={{0,4},{1,5},{2,6},{3,7},{4,0},{5,1},{6,2},{7,3},{8,12},{9,13},{10,... | collective-permute-start | bytes 786440 | tf_op jit(solution)/shard_map/ppermute | solution.py:60
  340.0 58.4 %copy-start.65 = (bf16[512,1024]{1,0:T(8,128)(2,1)S(1)}, bf16[512,1024]{1,0:T(8,128)(2,1)}, u32[]{:S(2)}) copy-start(bf16[512,1024]{1,0:T(8,128)(2,1)} %param.24) | copy-start | bytes 3145732
  340.0 58.4 %collective-permute-start.13 = (bf16[512,1024]{1,0:T(8,128)(2,1)}, bf16[512,1024]{1,0:T(8,128)(2,1)S(1)}, u32[]{:S(2)}, u32[]{:S(2)}) collective-permute-start(bf16[512,1024]{1,0:T(8,128)(2,1)} %param.24), channel_id=1, source_target_pairs={{1,16},{3,18},{5,20},{7,22},{9,24},{11,26},{13,28},{15,30},{16,1},... | collective-permute-start | bytes 3145736 | tf_op jit(solution)/shard_map/ppermute | solution.py:60
  342.1 56.4 %collective-permute-start.12 = (bf16[512,1024]{1,0:T(8,128)(2,1)}, bf16[512,1024]{1,0:T(8,128)(2,1)S(1)}, u32[]{:S(2)}, u32[]{:S(2)}) collective-permute-start(bf16[512,1024]{1,0:T(8,128)(2,1)} %param.24), channel_id=1, source_target_pairs={{0,16},{1,0},{2,18},{3,2},{4,20},{5,4},{6,22},{7,6},{8,24},{9,8},{... | collective-permute-start | bytes 3145736 | tf_op jit(solution)/shard_map/ppermute | solution.py:60
  345.8 26.4 %collective-permute-start.5 = (bf16[512,256]{1,0:T(8,128)(2,1)}, bf16[512,256]{1,0:T(8,128)(2,1)S(1)}, u32[]{:S(2)}, u32[]{:S(2)}) collective-permute-start(bf16[512,256]{1,0:T(8,128)(2,1)} %get-tuple-element.140), channel_id=1, source_target_pairs={{0,12},{1,13},{2,14},{3,15},{4,8},{5,9},{6,10},{7,11},{8,4},{9,5},... | collective-permute-start | bytes 786440 | tf_op jit(solution)/shard_map/ppermute | solution.py:60
  348.0 29.9 %collective-permute-start.4 = (bf16[512,256]{1,0:T(8,128)(2,1)}, bf16[512,256]{1,0:T(8,128)(2,1)S(1)}, u32[]{:S(2)}, u32[]{:S(2)}) collective-permute-start(bf16[512,256]{1,0:T(8,128)(2,1)} %get-tuple-element.141), channel_id=1, source_target_pairs={{0,8},{1,9},{2,10},{3,11},{4,12},{5,13},{6,14},{7,15},{8,0},{9,1},... | collective-permute-start | bytes 786440 | tf_op jit(solution)/shard_map/ppermute | solution.py:60
  357.6 22.2 %collective-permute-start.6 = (bf16[512,256]{1,0:T(8,128)(2,1)}, bf16[512,256]{1,0:T(8,128)(2,1)S(1)}, u32[]{:S(2)}, u32[]{:S(2)}) collective-permute-start(bf16[512,256]{1,0:T(8,128)(2,1)} %get-tuple-element.139), channel_id=1, source_target_pairs={{0,1},{1,0},{2,3},{3,2},{4,5},{5,4},{6,7},{7,6},{8,9},{9,8},{10,11... | collective-permute-start | bytes 786440 | tf_op jit(solution)/shard_map/ppermute | solution.py:60
  372.2 27.7 %collective-permute-start.11 = (bf16[512,1024]{1,0:T(8,128)(2,1)S(1)}, bf16[512,1024]{1,0:T(8,128)(2,1)S(1)}, u32[]{:S(2)}, u32[]{:S(2)}) collective-permute-start(bf16[512,1024]{1,0:T(8,128)(2,1)S(1)} %get-tuple-element.64.refs_1_), channel_id=1, source_target_pairs={{0,2},{1,3},{2,0},{3,1},{4,6},{5,7},{6,4},{7,5},{8,10},{9,11},{10,... | collective-permute-start | bytes 3145736 | tf_op jit(solution)/shard_map/ppermute | solution.py:60
  377.9 38.8 %collective-permute-start.10 = (bf16[512,1024]{1,0:T(8,128)(2,1)}, bf16[512,1024]{1,0:T(8,128)(2,1)S(1)}, u32[]{:S(2)}, u32[]{:S(2)}) collective-permute-start(bf16[512,1024]{1,0:T(8,128)(2,1)} %get-tuple-element.63.refs_0_), channel_id=1, source_target_pairs={{0,2},{1,3},{2,0},{3,1},{4,6},{5,7},{6,4},{7,5},{8,10},{9,11},{10,... | collective-permute-start | bytes 3145736 | tf_op jit(solution)/shard_map/ppermute | solution.py:60
  379.8 17.9 %collective-permute-start.9 = (bf16[512,256]{1,0:T(8,128)(2,1)S(1)}, bf16[512,256]{1,0:T(8,128)(2,1)S(1)}, u32[]{:S(2)}, u32[]{:S(2)}) collective-permute-start(bf16[512,256]{1,0:T(8,128)(2,1)S(1)} %get-tuple-element.136), channel_id=1, source_target_pairs={{0,13},{1,12},{2,15},{3,14},{4,9},{5,8},{6,11},{7,10},{8,5},{9,4},... | collective-permute-start | bytes 786440 | tf_op jit(solution)/shard_map/ppermute | solution.py:60
  429.0 99.8 %all-gather.18.cloned.1.call-start = ((), (), s32[]{:S(2)}) async-start(), calls=%async_computation.4 | async-start | bytes 9437184 | tf_op jit(solution)/shard_map/all_gather | solution.py:77
  429.1 21.4 %collective-permute-start.14 = (bf16[512,1024]{1,0:T(8,128)(2,1)}, bf16[512,1024]{1,0:T(8,128)(2,1)}, u32[]{:S(2)}, u32[]{:S(2)}) collective-permute-start(bf16[512,1024]{1,0:T(8,128)(2,1)} %get-tuple-element.67), channel_id=1, source_target_pairs={{0,2},{1,3},{2,0},{3,1},{4,6},{5,7},{6,4},{7,5},{8,10},{9,11},{10,... | collective-permute-start | bytes 3145736 | tf_op jit(solution)/shard_map/ppermute | solution.py:60
  430.2 42.7 %collective-permute-start.15 = (bf16[512,1024]{1,0:T(8,128)(2,1)}, bf16[512,1024]{1,0:T(8,128)(2,1)}, u32[]{:S(2)}, u32[]{:S(2)}) collective-permute-start(bf16[512,1024]{1,0:T(8,128)(2,1)} %get-tuple-element.68), channel_id=1, source_target_pairs={{0,2},{1,3},{2,0},{3,1},{4,6},{5,7},{6,4},{7,5},{8,10},{9,11},{10,... | collective-permute-start | bytes 3145736 | tf_op jit(solution)/shard_map/ppermute | solution.py:60
  473.0 259.9 %all-gather.22.cloned.1.call-start = ((), (), s32[]{:S(2)}) async-start(), calls=%async_computation.6 | async-start | bytes 9437184 | tf_op jit(solution)/shard_map/all_gather | solution.py:77
  687.0 94.5 %all-gather.20.cloned.1.call-start = ((), (), s32[]{:S(2)}) async-start(), calls=%async_computation.5 | async-start | bytes 9437184 | tf_op jit(solution)/shard_map/all_gather | solution.py:77
  687.8 511.5 %all-gather.24.cloned.1.call-start = ((), (), s32[]{:S(2)}) async-start(), calls=%async_computation.7 | async-start | bytes 9437184 | tf_op jit(solution)/shard_map/all_gather | solution.py:77
  850.8 124.5 %copy-start.32 = (f32[256,2048]{1,0:T(8,128)S(1)}, f32[256,2048]{1,0:T(8,128)}, u32[]{:S(2)}) copy-start(f32[256,2048]{1,0:T(8,128)} %copy-done.30) | copy-start | bytes 6291460
  982.4 223.0 %all-gather.26.cloned.1.call-start = ((), (), s32[]{:S(2)}) async-start(), calls=%async_computation.8 | async-start | bytes 9437184 | tf_op jit(solution)/shard_map/all_gather | solution.py:77
  1013.2 63.4 %collective-permute-start.23 = (bf16[1024,1024]{1,0:T(8,128)(2,1)S(1)}, bf16[1024,1024]{1,0:T(8,128)(2,1)S(1)}, u32[]{:S(2)}, u32[]{:S(2)}) collective-permute-start(bf16[1024,1024]{1,0:T(8,128)(2,1)S(1)} %constant_dynamic-slice_fusion.4), channel_id=1, source_target_pairs={{0,2},{1,3},{2,0},{3,1},{4,6},{5,7},{6,4},{7,5},{8,10},{9,11},{10,... | collective-permute-start | bytes 6291464 | tf_op jit(solution)/shard_map/ppermute | solution.py:60
  1026.2 39.0 %collective-permute-start.21 = (bf16[512,256]{1,0:T(8,128)(2,1)S(1)}, bf16[512,256]{1,0:T(8,128)(2,1)S(1)}, u32[]{:S(2)}, u32[]{:S(2)}) collective-permute-start(bf16[512,256]{1,0:T(8,128)(2,1)S(1)} %get-tuple-element.133), channel_id=1, source_target_pairs={{0,9},{1,8},{2,11},{3,10},{4,13},{5,12},{6,15},{7,14},{8,1},{9,0},... | collective-permute-start | bytes 786440 | tf_op jit(solution)/shard_map/ppermute | solution.py:60
  1026.7 14.4 collective-permute-start.16
  1026.9 15.1 %collective-permute-start.17 = (bf16[512,256]{1,0:T(8,128)(2,1)S(1)}, bf16[512,256]{1,0:T(8,128)(2,1)S(1)}, u32[]{:S(2)}, u32[]{:S(2)}) collective-permute-start(bf16[512,256]{1,0:T(8,128)(2,1)S(1)} %get-tuple-element.131), channel_id=1, source_target_pairs={{0,8},{1,9},{2,10},{3,11},{4,12},{5,13},{6,14},{7,15},{8,0},{9,1},... | collective-permute-start | bytes 786440 | tf_op jit(solution)/shard_map/ppermute | solution.py:60
  1029.0 20.2 %collective-permute-start.18 = (bf16[512,256]{1,0:T(8,128)(2,1)S(1)}, bf16[512,256]{1,0:T(8,128)(2,1)S(1)}, u32[]{:S(2)}, u32[]{:S(2)}) collective-permute-start(bf16[512,256]{1,0:T(8,128)(2,1)S(1)} %get-tuple-element.132), channel_id=1, source_target_pairs={{0,12},{1,13},{2,14},{3,15},{4,8},{5,9},{6,10},{7,11},{8,4},{9,5},... | collective-permute-start | bytes 786440 | tf_op jit(solution)/shard_map/ppermute | solution.py:60
  1041.1 37.5 %copy-start.21 = (bf16[4096,256]{1,0:T(8,128)(2,1)S(1)}, bf16[4096,256]{1,0:T(8,128)(2,1)}, u32[]{:S(2)}) copy-start(bf16[4096,256]{1,0:T(8,128)(2,1)} %copy-done.20) | copy-start | bytes 6291460
  1041.1 10.2 collective-permute-start.19
  1042.0 18.1 %collective-permute-start.20 = (bf16[512,256]{1,0:T(8,128)(2,1)S(1)}, bf16[512,256]{1,0:T(8,128)(2,1)S(1)}, u32[]{:S(2)}, u32[]{:S(2)}) collective-permute-start(bf16[512,256]{1,0:T(8,128)(2,1)S(1)} %get-tuple-element.135), channel_id=1, source_target_pairs={{0,5},{1,4},{2,7},{3,6},{4,1},{5,0},{6,3},{7,2},{8,13},{9,12},{10,... | collective-permute-start | bytes 786440 | tf_op jit(solution)/shard_map/ppermute | solution.py:60
  1049.1 27.5 %collective-permute-start.22 = (bf16[512,256]{1,0:T(8,128)(2,1)S(1)}, bf16[512,256]{1,0:T(8,128)(2,1)S(1)}, u32[]{:S(2)}, u32[]{:S(2)}) collective-permute-start(bf16[512,256]{1,0:T(8,128)(2,1)S(1)} %get-tuple-element.128), channel_id=1, source_target_pairs={{0,13},{1,12},{2,15},{3,14},{4,9},{5,8},{6,11},{7,10},{8,5},{9,4},... | collective-permute-start | bytes 786440 | tf_op jit(solution)/shard_map/ppermute | solution.py:60
  1051.3 129.5 %collective-permute-start.25 = (bf16[512,2048]{1,0:T(8,128)(2,1)}, bf16[512,2048]{1,0:T(8,128)(2,1)}, u32[]{:S(2)}, u32[]{:S(2)}) collective-permute-start(bf16[512,2048]{1,0:T(8,128)(2,1)} %get-tuple-element.105), channel_id=1, source_target_pairs={{0,1},{1,17},{2,3},{3,19},{4,5},{5,21},{6,7},{7,23},{8,9},{9,25},{... | collective-permute-start | bytes 6291464 | tf_op jit(solution)/shard_map/ppermute | solution.py:60
  1060.1 120.6 %collective-permute-start.24 = (bf16[512,2048]{1,0:T(8,128)(2,1)}, bf16[512,2048]{1,0:T(8,128)(2,1)}, u32[]{:S(2)}, u32[]{:S(2)}) collective-permute-start(bf16[512,2048]{1,0:T(8,128)(2,1)} %get-tuple-element.106), channel_id=1, source_target_pairs={{1,16},{3,18},{5,20},{7,22},{9,24},{11,26},{13,28},{15,30},{16,1},... | collective-permute-start | bytes 6291464 | tf_op jit(solution)/shard_map/ppermute | solution.py:60
  1078.6 51.5 %copy-start.1 = (f32[4096,128]{1,0:T(8,128)S(1)}, f32[4096,128]{1,0:T(8,128)}, u32[]{:S(2)}) copy-start(f32[4096,128]{1,0:T(8,128)} %get-tuple-element.164.cosine) | copy-start | bytes 6291460
  1078.6 51.5 %copy-start.13 = (f32[1,4096]{1,0:T(1,128)S(1)}, f32[1,4096]{1,0:T(1,128)}, u32[]{:S(2)}) copy-start(f32[1,4096]{1,0:T(1,128)} %copy-done.12) | copy-start | bytes 49156
  1078.6 51.5 %copy-start.15 = (f32[1,4096]{1,0:T(1,128)S(1)}, f32[1,4096]{1,0:T(1,128)}, u32[]{:S(2)}) copy-start(f32[1,4096]{1,0:T(1,128)} %copy-done.14) | copy-start | bytes 49156
  1174.5 39.4 %collective-permute-start.30 = (bf16[1024,512]{1,0:T(8,128)(2,1)}, bf16[1024,512]{1,0:T(8,128)(2,1)}, u32[]{:S(2)}, u32[]{:S(2)}) collective-permute-start(bf16[1024,512]{1,0:T(8,128)(2,1)} %get-tuple-element.101), channel_id=1, source_target_pairs={{0,1},{1,17},{2,3},{3,19},{4,5},{5,21},{6,7},{7,23},{8,9},{9,25},{... | collective-permute-start | bytes 3145736 | tf_op jit(solution)/shard_map/ppermute | solution.py:60
  1175.1 49.9 %collective-permute-start.29 = (bf16[1024,512]{1,0:T(8,128)(2,1)}, bf16[1024,512]{1,0:T(8,128)(2,1)}, u32[]{:S(2)}, u32[]{:S(2)}) collective-permute-start(bf16[1024,512]{1,0:T(8,128)(2,1)} %get-tuple-element.102), channel_id=1, source_target_pairs={{1,16},{3,18},{5,20},{7,22},{9,24},{11,26},{13,28},{15,30},{16,1},... | collective-permute-start | bytes 3145736 | tf_op jit(solution)/shard_map/ppermute | solution.py:60
  1211.4 17.1 %collective-permute-start.26 = (bf16[256,1024]{1,0:T(8,128)(2,1)S(1)}, bf16[256,1024]{1,0:T(8,128)(2,1)S(1)}, u32[]{:S(2)}, u32[]{:S(2)}) collective-permute-start(bf16[256,1024]{1,0:T(8,128)(2,1)S(1)} %constant_dynamic-slice_fusion.2), channel_id=1, source_target_pairs={{0,2},{1,3},{2,0},{3,1},{4,6},{5,7},{6,4},{7,5},{8,10},{9,11},{10,... | collective-permute-start | bytes 1572872 | tf_op jit(solution)/shard_map/ppermute | solution.py:60
  1228.8 23.6 %collective-permute-start.28 = (bf16[256,512]{1,0:T(8,128)(2,1)S(1)}, bf16[256,512]{1,0:T(8,128)(2,1)S(1)}, u32[]{:S(2)}, u32[]{:S(2)}) collective-permute-start(bf16[256,512]{1,0:T(8,128)(2,1)S(1)} %get-tuple-element.103), channel_id=1, source_target_pairs={{0,1},{1,17},{2,3},{3,19},{4,5},{5,21},{6,7},{7,23},{8,9},{9,25},{... | collective-permute-start | bytes 786440 | tf_op jit(solution)/shard_map/ppermute | solution.py:60
  1228.8 23.5 %collective-permute-start.27 = (bf16[256,512]{1,0:T(8,128)(2,1)S(1)}, bf16[256,512]{1,0:T(8,128)(2,1)S(1)}, u32[]{:S(2)}, u32[]{:S(2)}) collective-permute-start(bf16[256,512]{1,0:T(8,128)(2,1)S(1)} %get-tuple-element.104), channel_id=1, source_target_pairs={{1,16},{3,18},{5,20},{7,22},{9,24},{11,26},{13,28},{15,30},{16,1},... | collective-permute-start | bytes 786440 | tf_op jit(solution)/shard_map/ppermute | solution.py:60
  (72 other events, 387.3 us)
Sparse Core Ops, SparseCore 0:
  64.0 96.1 all-gather.11
  162.4 54.4 all-gather.9
  218.5 65.0 all-gather.13
  429.1 51.1 all-gather.15
  481.8 46.9 all-gather.17
  687.1 45.6 all-gather.21
  734.5 46.9 all-gather.19
  982.5 45.5 all-gather.23
  1029.7 88.4 all-gather.25
